TPU v7x, 256 devices: a whole 4x4x8 slice. The times are simulated.
256 devices in a mesh: dp: 16 (over y_hi, x, core), seq: 16 (over y_lo, z).
Axes of the slice: x: 4, y: 4 (y_hi: 2, y_lo: 2; y = y_hi * 2 + y_lo), z: 8, core: 2. Of those that a mesh axis runs over, the one named last changes fastest.
Arguments:
- inputs: bfloat16 [16, 64, 256, 768], P('dp', 'seq'), may hold values from -6 to 6
- cotangent: bfloat16 [16, 64, 256, 768], P('dp', 'seq'), may hold values from -6 to 6
- value_weight: bfloat16 [768, 768], replicated, may hold values from -0.21875 to 0.21875
- up_weight: bfloat16 [768, 1536], replicated, may hold values from -0.21875 to 0.21875
- down_weight: bfloat16 [1536, 768], replicated, may hold values from -0.15625 to 0.15625
- first_blocks: bfloat16 [64, 256, 256], P('seq'), may hold values from -0.375 to 0.375
- second_blocks: bfloat16 [256, 64, 64], P('seq'), may hold values from -0.75 to 0.75
Outputs:
- value_grad: bfloat16 [768, 768], P('seq')
- up_grad: bfloat16 [768, 1536], P('seq')
- down_grad: bfloat16 [1536, 768], P('seq')
All inputs are finite; a program needn't handle non-finite values.
Results may differ from a plain program's by a relative error of at most 0.02.
Values may be sent and summed in bfloat16 or wider, within the bound.
No kernel may reach another device: no remote copies, remote signals or barrier semaphores. Data moves between devices by JAX's collectives and lax.ppermute only.
A program may use at most 128 MiB of HBM per device.

v0:
```python
import jax
import jax.numpy as jnp
from jax import lax
from jax.sharding import PartitionSpec as P


def gelu_tanh(field):
    return jax.nn.gelu(field, approximate=True)


def silu_slope(field):
    sigmoid_part = jax.nn.sigmoid(field)
    return sigmoid_part * (1.0 + field * (1.0 - sigmoid_part))


def transposed_product(columns, right):
    return lax.dot_general(
        columns, right, (((0,), (0,)), ((), ())), preferred_element_type=jnp.float32
    )


def seq_rows(left, right):
    return lax.psum_scatter(transposed_product(left, right), "seq", scatter_dimension=0, tiled=True)


def local(inputs, cotangent, value_weight, up_weight, down_weight, first_blocks, second_blocks):
    width = inputs.shape[3]
    wide = inputs.astype(jnp.float32)
    normed = (wide * lax.rsqrt(jnp.mean(wide * wide, axis=-1, keepdims=True) + 1e-06)).astype(
        jnp.bfloat16
    )
    flat_normed = normed.reshape(-1, width)
    flat_cot = cotangent.reshape(-1, width)
    values = jnp.dot(flat_normed, value_weight, preferred_element_type=jnp.float32).astype(
        jnp.bfloat16
    )
    values = values.reshape(normed.shape)
    rowmix = jnp.einsum(
        "acb,zabd->zacd", first_blocks, values, preferred_element_type=jnp.float32
    ).astype(jnp.bfloat16)
    mixed = lax.all_to_all(
        jnp.einsum(
            "cxy,zycd->zxcd",
            second_blocks,
            lax.all_to_all(rowmix, "seq", split_axis=2, concat_axis=1, tiled=True),
            preferred_element_type=jnp.float32,
        ).astype(jnp.bfloat16),
        "seq",
        split_axis=1,
        concat_axis=2,
        tiled=True,
    )
    slope = (
        cotangent.astype(jnp.float32)
        * normed.astype(jnp.float32)
        * silu_slope(mixed.astype(jnp.float32))
    ).astype(jnp.bfloat16)
    back_natural = lax.all_to_all(
        jnp.einsum(
            "cxy,zxcd->zycd",
            second_blocks,
            lax.all_to_all(slope, "seq", split_axis=2, concat_axis=1, tiled=True),
            preferred_element_type=jnp.float32,
        ).astype(jnp.bfloat16),
        "seq",
        split_axis=1,
        concat_axis=2,
        tiled=True,
    )
    value_slope = jnp.einsum(
        "acb,zacd->zabd", first_blocks, back_natural, preferred_element_type=jnp.float32
    ).astype(jnp.bfloat16)
    pre_act = jnp.dot(flat_normed, up_weight, preferred_element_type=jnp.float32)
    hidden = gelu_tanh(pre_act).astype(jnp.bfloat16)
    back_hidden = lax.dot_general(
        flat_cot, down_weight, (((1,), (1,)), ((), ())), preferred_element_type=jnp.float32
    )
    up_slope = jax.vjp(gelu_tanh, pre_act)[1](back_hidden)[0].astype(jnp.bfloat16)
    joined = jnp.concatenate([value_slope.reshape(-1, width), up_slope], axis=1)
    total_tokens = (
        inputs.shape[0]
        * inputs.shape[1]
        * inputs.shape[2]
        * lax.axis_size("dp")
        * lax.axis_size("seq")
    )
    factor = float(total_tokens) ** (-0.5)
    part_first = seq_rows(flat_normed, joined)
    part_second = seq_rows(hidden, flat_cot)
    part_first, part_second = lax.psum((part_first, part_second), "dp")
    part_first = (part_first * factor).astype(jnp.bfloat16)
    part_second = (part_second * factor).astype(jnp.bfloat16)
    return (part_first[:, :width], part_first[:, width:], part_second)


def solution(mesh):
    placed = (
        P("dp", "seq", None, None),
        P("dp", "seq", None, None),
        P(),
        P(),
        P(),
        P("seq", None, None),
        P("seq", None, None),
    )
    return jax.shard_map(
        local,
        mesh=mesh,
        in_specs=placed,
        out_specs=(P("seq", None), P("seq", None), P("seq", None)),
        check_vma=False,
    )
```

profile of v0, /device:TPU:1, one launch (start us, length us, event | category | flops | bytes accessed | tf_op | source)
XLA Modules:
  0.0 489.9 jit_solution(7488695772001819373)
XLA Ops:
  7.2 1.9 fusion.11
  9.2 1.7 fusion.12
  12.4 1.9 fusion.23
  14.2 3.8 copy.39
  18.0 10.2 %all-to-all-start = ((bf16[1,4,256,768]{3,1,0,2:T(4,128)(2,1)}), bf16[1,4,256,768]{3,1,0,2:T(4,128)(2,1)}, u32[]{:S(2)}, u32[]{:S(2)}) async-start(bf16[1,4,256,768]{3,1,0,2:T(4,128)(2,1)} %copy.39), calls=%async_computation | async-start | bytes 3145728 | tf_op jit(solution)/shard_map/all_to_all | solution.py:45
  28.2 7.4 %fusion.29 = f32[1024,1536]{1,0:T(8,128)} fusion(bf16[1024,768]{1,0:T(8,128)(2,1)} %bitcast.79, bf16[1536,768]{1,0:T(8,128)(2,1)} %param.11), kind=kOutput, calls=%fused_computation.45 | convolution fusion | flops 2415919104 | bytes 10223616 | tf_op jit(solution)/shard_map/dot_general | solution.py:75
  35.6 28.9 %all-to-all-done = bf16[1,4,256,768]{3,1,0,2:T(4,128)(2,1)} async-done(((bf16[1,4,256,768]{3,1,0,2:T(4,128)(2,1)}), bf16[1,4,256,768]{3,1,0,2:T(4,128)(2,1)}, u32[]{:S(2)}, u32[]{:S(2)}) %all-to-all-start) | async-done | bytes 1572896 | tf_op jit(solution)/shard_map/all_to_all | solution.py:45
  64.5 1.6 copy.40
  66.1 2.5 copy.41
  68.6 3.7 reshape.103
  72.3 2.0 fusion.22
  74.3 2.0 copy.42
  76.3 6.7 %all-to-all-start.1 = ((bf16[1,64,16,768]{3,2,0,1:T(8,128)(2,1)}), bf16[1,64,16,768]{3,2,0,1:T(8,128)(2,1)}, u32[]{:S(2)}, u32[]{:S(2)}) async-start(bf16[1,64,16,768]{3,2,0,1:T(8,128)(2,1)} %copy.42), calls=%async_computation.1 | async-start | bytes 3145728 | tf_op jit(solution)/shard_map/all_to_all | solution.py:41
  83.2 9.6 %fusion.6 = (bf16[1024,1536]{1,0:T(8,128)(2,1)}, f32[1024,1536]{1,0:T(8,128)S(1)}) fusion(f32[1024,1536]{1,0:T(8,128)} %fusion.29, bf16[1024,768]{1,0:T(8,128)(2,1)} %bitcast.84, bf16[768,1536]{1,0:T(8,128)(2,1)S(1)} %copy-done), kind=kOutput, calls=%fused_computation.8 | convolution fusion | flops 2447376384 | bytes 19660800 | tf_op jit(solution)/shard_map/dot_general | solution.py:73
  92.8 5.2 %fusion.20 = f32[1536,768]{1,0:T(8,128)} fusion(bf16[1024,768]{1,0:T(8,128)(2,1)S(1)} %bitcast.80, f32[1024,1536]{1,0:T(8,128)S(1)} %get-tuple-element.6), kind=kOutput, calls=%fused_computation.27 | convolution fusion | flops 2430074880 | bytes 12582912 | tf_op jit(solution)/shard_map/dot_general | solution.py:17
  98.1 22.6 %all-to-all-done.1 = bf16[1,64,16,768]{3,2,0,1:T(8,128)(2,1)} async-done(((bf16[1,64,16,768]{3,2,0,1:T(8,128)(2,1)}), bf16[1,64,16,768]{3,2,0,1:T(8,128)(2,1)}, u32[]{:S(2)}, u32[]{:S(2)}) %all-to-all-start.1) | async-done | bytes 1572896 | tf_op jit(solution)/shard_map/all_to_all | solution.py:41
  120.8 1.9 copy.43
  125.4 61.2 %all_to_all.54 = bf16[1,4,256,768]{3,1,0,2:T(4,128)(2,1)S(1)} all-to-all(bf16[1,4,256,768]{3,1,0,2:T(4,128)(2,1)S(1)} %copy.44), channel_id=1, replica_groups=mesh['dp'=16,'seq'=16] {'seq'}, dimensions={2} | all-to-all | bytes 3145728 | tf_op jit(solution)/shard_map/all_to_all | solution.py:62
  188.7 2.0 fusion.21
  191.6 48.9 %all_to_all.55 = bf16[1,64,16,768]{3,2,0,1:T(8,128)(2,1)S(1)} all-to-all(bf16[1,64,16,768]{3,2,0,1:T(8,128)(2,1)S(1)} %copy.47), channel_id=1, replica_groups=mesh['dp'=16,'seq'=16] {'seq'}, dimensions={1} | all-to-all | bytes 3145728 | tf_op jit(solution)/shard_map/all_to_all | solution.py:58
  242.9 6.1 %fusion.7 = f32[768,2304]{1,0:T(8,128)} fusion(bf16[1024,768]{1,0:T(8,128)(2,1)S(1)} %bitcast.85, bf16[1024,1536]{1,0:T(8,128)(2,1)S(1)} %copy-done.10, bf16[1024,768]{1,0:T(8,128)(2,1)S(1)} %bitcast.81), kind=kOutput, calls=%fused_computation.10 | convolution fusion | flops 3633315840 | bytes 13369344 | tf_op jit(solution)/shard_map/dot_general | solution.py:17
  249.1 84.5 %reduce-scatter.3.cloned.1.call-done = f32[48,2304]{1,0:T(8,128)} async-done(((f32[768,2304]{1,0:T(8,128)}), f32[48,2304]{1,0:T(8,128)}) %reduce-scatter.3.cloned.1.call-update) | async-done | bytes 442384 | tf_op jit(solution)/shard_map/reduce_scatter | solution.py:23
  333.6 145.8 %all-reduce.3.cloned.1.call-done = (f32[48,2304]{1,0:T(8,128)}, f32[96,768]{1,0:T(8,128)}) async-done(((f32[48,2304]{1,0:T(8,128)}, f32[96,768]{1,0:T(8,128)}), (f32[48,2304]{1,0:T(8,128)}, f32[96,768]{1,0:T(8,128)})) %all-reduce.3.cloned.1.call-update) | async-done | bytes 737296 | tf_op jit(solution)/shard_map/psum | solution.py:90
  481.7 1.6 multiply_convert_fusion.3
  (41 shorter events, 12.1 us)
Async XLA Ops:
  7.2 76.1 %copy-start = (bf16[768,1536]{1,0:T(8,128)(2,1)S(1)}, bf16[768,1536]{1,0:T(8,128)(2,1)}, u32[]{:S(2)}) copy-start(bf16[768,1536]{1,0:T(8,128)(2,1)} %param.10) | copy-start | bytes 7077892
  7.2 3.7 copy-start.9
  10.9 1.4 copy-start.6
  10.9 1.4 copy-start.3
  18.0 46.5 %all-to-all-start = ((bf16[1,4,256,768]{3,1,0,2:T(4,128)(2,1)}), bf16[1,4,256,768]{3,1,0,2:T(4,128)(2,1)}, u32[]{:S(2)}, u32[]{:S(2)}) async-start(bf16[1,4,256,768]{3,1,0,2:T(4,128)(2,1)} %copy.39), calls=%async_computation | async-start | bytes 3145728 | tf_op jit(solution)/shard_map/all_to_all | solution.py:45
  66.1 6.2 %copy-start.8 = (bf16[16,64,64]{2,1,0:T(8,128)(2,1)S(1)}, bf16[16,64,64]{2,1,0:T(8,128)(2,1)}, u32[]{:S(2)}) copy-start(bf16[16,64,64]{2,1,0:T(8,128)(2,1)} %param.13) | copy-start | bytes 393220
  76.3 44.5 %all-to-all-start.1 = ((bf16[1,64,16,768]{3,2,0,1:T(8,128)(2,1)}), bf16[1,64,16,768]{3,2,0,1:T(8,128)(2,1)}, u32[]{:S(2)}, u32[]{:S(2)}) async-start(bf16[1,64,16,768]{3,2,0,1:T(8,128)(2,1)} %copy.42), calls=%async_computation.1 | async-start | bytes 3145728 | tf_op jit(solution)/shard_map/all_to_all | solution.py:41
  83.0 166.0 %reduce-scatter.5.cloned.1.call-start = ((), (), s32[]{:S(2)}) async-start(), calls=%async_computation.7 | async-start | bytes 5013504 | tf_op jit(solution)/shard_map/reduce_scatter | solution.py:23
  83.2 9.6 %copy-start.4 = (bf16[1,4,256,768]{3,2,1,0:T(8,128)(2,1)S(1)}, bf16[1,4,256,768]{3,2,1,0:T(8,128)(2,1)}, u32[]{:S(2)}) copy-start(bf16[1,4,256,768]{3,2,1,0:T(8,128)(2,1)} %param.8) | copy-start | bytes 4718596
  98.1 24.6 %copy-start.2 = (bf16[1,4,256,768]{3,2,1,0:T(8,128)(2,1)S(1)}, bf16[1,4,256,768]{3,2,1,0:T(8,128)(2,1)}, u32[]{:S(2)}) copy-start(bf16[1,4,256,768]{3,2,1,0:T(8,128)(2,1)} %param.7) | copy-start | bytes 4718596
  98.1 235.5 %reduce-scatter.3.cloned.1.call-start = ((), (), s32[]{:S(2)}) async-start(), calls=%async_computation.6 | async-start | bytes 7520256 | tf_op jit(solution)/shard_map/reduce_scatter | solution.py:23
  120.8 2.0 copy-start.5
  240.5 1.4 copy-start.7
  240.5 2.4 copy-start.10
  248.9 234.4 %copy-start.1 = (bf16[768,1536]{1,0:T(8,128)(2,1)S(1)}, bf16[768,1536]{1,0:T(8,128)(2,1)}, u32[]{:S(2)}) copy-start(bf16[768,1536]{1,0:T(8,128)(2,1)} %param.10) | copy-start | bytes 7077892
  249.0 230.4 %all-reduce.3.cloned.1.call-start = ((), (), s32[]{:S(2)}) async-start(), calls=%async_computation.8 | async-start | bytes 1474560 | tf_op jit(solution)/shard_map/psum | solution.py:90
Sparse Core Ops, SparseCore 0:
  98.2 119.1 reduce-scatter.4
  249.1 84.3 reduce-scatter.2
  336.5 142.8 all-reduce.2
where the time goes:
time: 494 us; the launch traced here: 490 us
  waiting for transfers between devices  282 us (57%)
  blocking collectives  110 us (22%)
  matrix products  36.1 us (7%)
  local copies, waits for them, and re-layouts  22.8 us (5%)
  starting transfers between devices  17.2 us (3%)
  between operations  14 us (3%)
  other arithmetic  7.78 us (2%)
    psum x1, waiting for transfers between devices, local(): part_first, part_second = lax.psum((part_first, part_second), 'dp')  146 us
    reduce_scatter x2, waiting for transfers between devices, seq_rows(): lax.psum_scatter(transposed_product(left, right), 'seq', scatter_dimensio...  84.5 us
    all_to_all x1, blocking collectives, local(): lax.all_to_all(slope, 'seq', split_axis=2, concat_axis=1, tiled=True)  61.2 us
    all_to_all x1, blocking collectives, local(): lax.all_to_all(jnp.einsum('cxy,zxcd->zycd', second_blocks, lax.all_to_all...  48.9 us
    all_to_all x1, waiting for transfers between devices, local(): lax.all_to_all(rowmix, 'seq', split_axis=2, concat_axis=1, tiled=True)  28.9 us
    all_to_all x1, waiting for transfers between devices, local(): lax.all_to_all(jnp.einsum('cxy,zycd->zxcd', second_blocks, lax.all_to_all...  22.6 us
    dot_general x2, matrix products, transposed_product(): lax.dot_general(columns, right, (((0,), (0,)), ((), ())), preferred_eleme...  11.3 us
    all_to_all x1, starting transfers between devices, local(): lax.all_to_all(rowmix, 'seq', split_axis=2, concat_axis=1, tiled=True)  10.2 us
  transfers between devices with their start and end apart: 5, of which 4 were waited for; matrix products, arithmetic and copies ran while one was open for 8% of the time, Pallas kernels for 0%

commit v1 on v0

v1 whole, which is shorter than its diff:
```python
import jax
import jax.numpy as jnp
from jax import lax
from jax.sharding import PartitionSpec as P

BF16 = jnp.bfloat16
F32 = jnp.float32
PIECE = [
    (i & 1) * 8 + ((((i >> 1) ^ (i >> 2)) & 1) * 4) + ((i >> 2) & 1) * 2 + (i >> 3)
    for i in range(16)
]
OWNER = [PIECE.index(p) for p in range(16)]


def gelu_tanh(field):
    return jax.nn.gelu(field, approximate=True)


def silu_slope(field):
    sigmoid_part = jax.nn.sigmoid(field)
    return sigmoid_part * (1.0 + field * (1.0 - sigmoid_part))


def product(left, right, left_dim, right_dim):
    return lax.dot_general(
        left, right, (((left_dim,), (right_dim,)), ((), ())), preferred_element_type=F32
    )


def swap(block, flip):
    return lax.ppermute(block, "dp", [(i, i ^ flip) for i in range(16)])


def halve(total, axis, bit, flip):
    mine = lax.dynamic_slice_in_dim(total, bit, 1, axis)
    other = lax.dynamic_slice_in_dim(total, 1 - bit, 1, axis).astype(BF16)
    return mine.astype(F32) + swap(other, flip).astype(F32)


def scatter_dp(left, right):
    i = lax.axis_index("dp")
    core, x0, x1, y_hi = i & 1, (i >> 1) & 1, (i >> 2) & 1, i >> 3
    out = []
    for first, block in ((True, left), (False, right)):
        rows, lanes = block.shape
        total = block.reshape(2, 2, 2, 2, rows // 16, lanes)
        total = halve(total, 0, core, 1)
        if first:
            total = halve(total, 1, x0 ^ x1, 2)
            total = halve(total, 2, x1, 6)
        else:
            total = halve(total, 2, x1, 6)
            total = halve(total, 1, x0 ^ x1, 2)
        total = halve(total, 3, y_hi, 8)
        out.append(total.reshape(rows // 16, lanes))
    return out


def exchange(block, axis):
    return lax.all_to_all(block, axis, split_axis=0, concat_axis=0, tiled=True)


def local(inputs, cotangent, value_weight, up_weight, down_weight, first_blocks, second_blocks):
    width = inputs.shape[3]
    rows = inputs.shape[1]
    places = lax.axis_size("seq")
    wide = inputs[0].astype(F32)
    normed = (wide * lax.rsqrt(jnp.mean(wide * wide, axis=-1, keepdims=True) + 1e-06)).astype(BF16)
    weighted = (cotangent[0].astype(F32) * normed.astype(F32)).astype(BF16)
    first_mix = jnp.einsum(
        "acb,abd->acd", first_blocks, normed, preferred_element_type=F32
    ).astype(BF16)

    def by_place(block):
        block = block.reshape(rows, places, -1, width).transpose(1, 0, 2, 3)
        return block.reshape(places, -1, width)

    sent = jnp.concatenate([by_place(first_mix), by_place(weighted)], axis=1)
    came = exchange(sent, "seq")
    half = came.shape[1] // 2
    first_mix = came[:, :half].reshape(-1, width)
    weighted = came[:, half:].reshape(-1, width)

    flat_normed = normed.reshape(-1, width)
    flat_cot = cotangent.reshape(-1, width)
    pre_act = product(flat_normed, up_weight, 1, 0)
    hidden = gelu_tanh(pre_act).astype(BF16)
    back_hidden = product(flat_cot, down_weight, 1, 1)
    up_slope = jax.vjp(gelu_tanh, pre_act)[1](back_hidden)[0].astype(BF16)
    up_t = product(up_slope, flat_normed, 0, 0).astype(BF16)
    down_t = product(flat_cot, hidden, 0, 0).astype(BF16)
    up_t, down_t = scatter_dp(up_t, down_t)

    blocks, size = second_blocks.shape[0], second_blocks.shape[1]
    positions = blocks * size
    stacked = second_blocks.transpose(1, 0, 2).reshape(positions, size)
    row = lax.broadcasted_iota(jnp.int32, (positions, positions), 0)
    col = lax.broadcasted_iota(jnp.int32, (positions, positions), 1)
    spread = (
        lax.broadcasted_iota(jnp.int32, (size, positions), 1) // blocks
        == lax.broadcasted_iota(jnp.int32, (size, positions), 0)
    ).astype(BF16)
    second = jnp.where(
        row % blocks == col % blocks, product(stacked, spread, 1, 0), 0.0
    ).astype(BF16)

    mix = product(second, first_mix, 1, 0).astype(BF16)
    mixed = product(mix, value_weight, 1, 0)
    slope = (weighted.astype(F32) * silu_slope(mixed)).astype(BF16)
    value_t = product(slope, mix, 0, 0).astype(BF16)
    value_left, value_right = scatter_dp(value_t[:, : width // 2], value_t[:, width // 2 :])
    value_t = jnp.concatenate([value_left, value_right], axis=1)

    piece_v, piece_u = value_t.shape[0], up_t.shape[0]
    value_p = value_t.astype(BF16).T.reshape(places, -1, piece_v)
    up_p = up_t.astype(BF16).T.reshape(places, -1, piece_u)
    down_p = down_t.astype(BF16).T.reshape(places, 2, -1, piece_v)
    packed = jnp.concatenate([value_p, up_p, down_p[:, 0], down_p[:, 1]], axis=2)
    total_tokens = (
        inputs.shape[0] * inputs.shape[1] * inputs.shape[2] * lax.axis_size("dp") * places
    )
    factor = float(total_tokens) ** (-0.5)
    packed = jnp.sum(exchange(packed, "seq").astype(F32), axis=0) * factor
    packed = packed.astype(BF16)
    packed = exchange(jnp.broadcast_to(packed[None], (16,) + packed.shape), "dp")
    packed = [packed[k] for k in OWNER]

    def join(start, size):
        return jnp.concatenate([block[:, start : start + size] for block in packed], axis=1)

    a, b = piece_v, piece_v + piece_u
    down = jnp.concatenate([join(b, piece_v), join(b + piece_v, piece_v)], axis=0)
    return join(0, a), join(a, piece_u), down


def solution(mesh):
    placed = (
        P("dp", "seq", None, None),
        P("dp", "seq", None, None),
        P(),
        P(),
        P(),
        P("seq", None, None),
        P("seq", None, None),
    )
    return jax.shard_map(
        local,
        mesh=mesh,
        in_specs=placed,
        out_specs=(P("seq", None), P("seq", None), P("seq", None)),
        check_vma=False,
    )
```

time: 494 us -> 170 us (0.34)
  waiting for transfers between devices: 282 us -> 36.4 us
  blocking collectives: 110 us -> 36 us
  between operations: 14 us -> 1.2 us
  starting transfers between devices: 17.2 us -> 27.7 us
  other arithmetic: 7.78 us -> 14.2 us
    psum x1 -> x0, waiting for transfers between devices: 146 us -> none  [local(): part_first, part_second = lax.psum((part_first, part_second), 'dp')]
    reduce_scatter x2 -> x0, waiting for transfers between devices: 84.5 us -> none  [seq_rows(): lax.psum_scatter(transposed_product(left, right), 'seq', scatter_dimensio...]
    all_to_all x2, blocking collectives: 110 us -> 36 us  [exchange(): return lax.all_to_all(block, axis, split_axis=0, concat_axis=0, tiled=True)]
    all_to_all x2 -> x1, waiting for transfers between devices: 51.6 us -> 2.76 us  [exchange(): return lax.all_to_all(block, axis, split_axis=0, concat_axis=0, tiled=True)]
    ppermute x0 -> x16, waiting for transfers between devices: none -> 33.6 us  [swap(): return lax.ppermute(block, 'dp', [(i, i ^ flip) for i in range(16)])]
    ppermute x0 -> x16, starting transfers between devices: none -> 17.5 us  [swap(): return lax.ppermute(block, 'dp', [(i, i ^ flip) for i in range(16)])]
    convert_element_type x5 -> x12, local copies, waits for them, and re-layouts: 9.82 us -> 1.23 us  [halve(): other = lax.dynamic_slice_in_dim(total, 1 - bit, 1, axis).astype(BF16)]
    all_to_all x2 -> x1, starting transfers between devices: 16.9 us -> 10.2 us  [exchange(): return lax.all_to_all(block, axis, split_axis=0, concat_axis=0, tiled=True)]
  transfers between devices with their start and end apart: 5 -> 17, of which waited for: 4 -> 12; matrix products, arithmetic and copies ran while one was open for 8% -> 31% of each run, Pallas kernels for 0% -> 0%
where the time goes in v1:
time: 170 us; the launch traced here: 169 us
  waiting for transfers between devices  36.4 us (21%)
  blocking collectives  36 us (21%)
  matrix products  35 us (21%)
  starting transfers between devices  27.7 us (16%)
  local copies, waits for them, and re-layouts  19.1 us (11%)
  other arithmetic  14.2 us (8%)
    all_to_all x2, blocking collectives, exchange(): return lax.all_to_all(block, axis, split_axis=0, concat_axis=0, tiled=True)  36 us
    ppermute x16, waiting for transfers between devices, swap(): return lax.ppermute(block, 'dp', [(i, i ^ flip) for i in range(16)])  33.6 us
    dot_general x6, matrix products, product(): lax.dot_general(left, right, (((left_dim,), (right_dim,)), ((), ())), pre...  32.7 us
    ppermute x16, starting transfers between devices, swap(): return lax.ppermute(block, 'dp', [(i, i ^ flip) for i in range(16)])  17.5 us
    all_to_all x1, starting transfers between devices, exchange(): return lax.all_to_all(block, axis, split_axis=0, concat_axis=0, tiled=True)  10.2 us
    add x12, other arithmetic, halve(): return mine.astype(F32) + swap(other, flip).astype(F32)  5.12 us
    slice x1, local copies, waits for them, and re-layouts, local(): weighted = came[:, half:].reshape(-1, width)  3.85 us
    unnamed x29, local copies, waits for them, and re-layouts  3.69 us
  transfers between devices with their start and end apart: 17, of which 12 were waited for; matrix products, arithmetic and copies ran while one was open for 31% of the time, Pallas kernels for 0%

profile of v1, /device:TPU:1, one launch (start us, length us, event | category | flops | bytes accessed | tf_op | source)
XLA Modules:
  0.0 169.5 jit_solution(10666335862140723889)
XLA Ops:
  2.7 2.3 %convolution_convert_fusion.2 = bf16[4,768,256]{1,2,0:T(8,128)(2,1)S(1)} fusion(bf16[4,256,256]{2,1,0:T(8,128)(2,1)} %param.12, bf16[1,4,256,768]{3,2,1,0:T(8,128)(2,1)} %param.7, f32[4,256]{1,0:T(4,128)S(1)} %get-tuple-element.73), kind=kOutput, calls=%fused_computation.33 | convolution fusion | flops 405798912 | bytes 3674112 | tf_op jit(solution)/shard_map/acb,abd->acd/dot_general | solution.py:70
  9.4 10.2 %all-to-all-start = ((bf16[16,128,768]{2,1,0:T(8,128)(2,1)}), bf16[16,128,768]{2,1,0:T(8,128)(2,1)}, u32[]{:S(2)}, u32[]{:S(2)}) async-start(bf16[16,128,768]{2,1,0:T(8,128)(2,1)} %pad_maximum_fusion), calls=%async_computation | async-start | bytes 6291456 | tf_op jit(solution)/shard_map/all_to_all | solution.py:60
  19.6 2.9 %fusion.9 = bf16[1024,768]{1,0:T(8,128)(2,1)} fusion(bf16[1,4,256,768]{3,2,1,0:T(8,128)(2,1)} %param.7, f32[1024]{0:T(1024)S(1)} %bitcast.134), kind=kLoop, calls=%fused_computation.19 | loop fusion | flops 2359296 | bytes 3149824 | tf_op jit(solution)/shard_map/convert_element_type | solution.py:68
  22.4 4.1 %fusion.72 = f32[1024,1536]{1,0:T(8,128)S(1)} fusion(bf16[1024,768]{1,0:T(8,128)(2,1)} %fusion.9, bf16[768,1536]{1,0:T(8,128)(2,1)S(1)} %copy-done), kind=kOutput, calls=%fused_computation.140 | convolution fusion | flops 2415919104 | bytes 10223616 | tf_op jit(solution)/shard_map/dot_general | solution.py:25
  26.6 3.6 %convolution_convert_fusion = bf16[1536,768]{0,1:T(8,128)(2,1)S(1)} fusion(bf16[1024,768]{1,0:T(8,128)(2,1)S(1)} %bitcast.126, f32[1024,1536]{1,0:T(8,128)S(1)} %fusion.72), kind=kOutput, calls=%fused_computation.13 | convolution fusion | flops 2431254528 | bytes 10223616 | tf_op jit(solution)/shard_map/dot_general | solution.py:25
  32.9 13.7 %convolution_convert_fusion.1 = bf16[1536,768]{1,0:T(8,128)(2,1)S(1)} fusion(bf16[1024,768]{1,0:T(8,128)(2,1)} %fusion.9, f32[1024,1536]{1,0:T(8,128)} %copy-done.11, bf16[1024,768]{1,0:T(8,128)(2,1)} %bitcast.124, bf16[1536,768]{1,0:T(8,128)(2,1)} %param.11), kind=kOutput, calls=%fused_computation.14 | convolution fusion | flops 4864475136 | bytes 14155776 | tf_op jit(solution)/shard_map/dot_general | solution.py:25
  48.4 2.0 %convert_add_fusion = f32[1,2,2,2,48,1536]{5,4,3,2,1,0:T(8,128)S(1)} fusion(bf16[1,2,2,2,48,1536]{5,4,3,2,1,0:T(8,128)(2,1)} %collective-permute-done.12, bf16[2,2,2,2,48,1536]{5,4,3,2,1,0:T(8,128)(2,1)} %bitcast.119, s32[]{:T(128)S(6)} %select_n.72), kind=kLoop, calls=%fused_computation.31 | loop fusion | flops 1769472 | bytes 4718596 | tf_op jit(solution)/shard_map/add | solution.py:37
  51.3 2.5 %collective-permute-start.13 = (bf16[1,2,1,2,48,1536]{5,4,3,2,1,0:T(8,128)(2,1)}, bf16[1,2,1,2,48,1536]{5,4,3,2,1,0:T(8,128)(2,1)}, u32[]{:S(2)}, u32[]{:S(2)}) collective-permute-start(bf16[1,2,1,2,48,1536]{5,4,3,2,1,0:T(8,128)(2,1)} %dynamic-slice_convert_fusion), channel_id=1, source_target_pairs={{0,96},{16,112},{32,64},{48,80},{64,32},{80,48},{96,0},{112,16},{1... | collective-permute-start | bytes 1769480 | tf_op jit(solution)/shard_map/ppermute | solution.py:31
  57.8 9.9 %collective-permute-done.13 = bf16[1,2,1,2,48,1536]{5,4,3,2,1,0:T(8,128)(2,1)} collective-permute-done((bf16[1,2,1,2,48,1536]{5,4,3,2,1,0:T(8,128)(2,1)}, bf16[1,2,1,2,48,1536]{5,4,3,2,1,0:T(8,128)(2,1)}, u32[]{:S(2)}, u32[]{:S(2)}) %collective-permute-start.13) | collective-permute-done | bytes 589856 | tf_op jit(solution)/shard_map/ppermute | solution.py:31
  69.1 3.5 %collective-permute-done.9 = bf16[1,1,2,2,96,768]{5,4,3,2,1,0:T(8,128)(2,1)S(1)} collective-permute-done((bf16[1,1,2,2,96,768]{5,4,3,2,1,0:T(8,128)(2,1)S(1)}, bf16[1,1,2,2,96,768]{5,4,3,2,1,0:T(8,128)(2,1)S(1)}, u32[]{:S(2)}, u32[]{:S(2)}) %collective-permute-start.9) | collective-permute-done | bytes 589856 | tf_op jit(solution)/shard_map/ppermute | solution.py:31
  73.0 5.8 %collective-permute-done.14 = bf16[1,1,1,2,48,1536]{5,4,3,2,1,0:T(8,128)(2,1)S(1)} collective-permute-done((bf16[1,1,1,2,48,1536]{5,4,3,2,1,0:T(8,128)(2,1)S(1)}, bf16[1,1,1,2,48,1536]{5,4,3,2,1,0:T(8,128)(2,1)S(1)}, u32[]{:S(2)}, u32[]{:S(2)}) %collective-permute-start.14) | collective-permute-done | bytes 294944 | tf_op jit(solution)/shard_map/ppermute | solution.py:31
  79.0 2.7 %collective-permute-start.15 = (bf16[1,1,1,1,48,1536]{5,4,3,2,1,0:T(8,128)(2,1)S(1)}, bf16[1,1,1,1,48,1536]{5,4,3,2,1,0:T(8,128)(2,1)S(1)}, u32[]{:S(2)}, u32[]{:S(2)}) collective-permute-start(bf16[1,1,1,1,48,1536]{5,4,3,2,1,0:T(8,128)(2,1)S(1)} %dynamic-slice_convert_fusion.4), channel_id=1, source_target_pairs={{0,128},{16,144},{32,160},{48,176},{64,192},{80,208},{96,224},{112... | collective-permute-start | bytes 442376 | tf_op jit(solution)/shard_map/ppermute | solution.py:31
  81.8 2.0 %collective-permute-start.11 = (bf16[1,1,1,1,96,768]{5,4,3,2,1,0:T(8,128)(2,1)S(1)}, bf16[1,1,1,1,96,768]{5,4,3,2,1,0:T(8,128)(2,1)S(1)}, u32[]{:S(2)}, u32[]{:S(2)}) collective-permute-start(bf16[1,1,1,1,96,768]{5,4,3,2,1,0:T(8,128)(2,1)S(1)} %dynamic-slice_convert_fusion.5), channel_id=1, source_target_pairs={{0,128},{16,144},{32,160},{48,176},{64,192},{80,208},{96,224},{112... | collective-permute-start | bytes 442376 | tf_op jit(solution)/shard_map/ppermute | solution.py:31
  87.5 2.8 %all-to-all-done = bf16[16,128,768]{2,1,0:T(8,128)(2,1)} async-done(((bf16[16,128,768]{2,1,0:T(8,128)(2,1)}), bf16[16,128,768]{2,1,0:T(8,128)(2,1)}, u32[]{:S(2)}, u32[]{:S(2)}) %all-to-all-start) | async-done | bytes 3145760 | tf_op jit(solution)/shard_map/all_to_all | solution.py:60
  90.2 3.8 %fusion.51 = (bf16[16,64,768]{2,1,0:T(8,128)(2,1)}, bf16[16,64,768]{2,1,0:T(8,128)(2,1)}) fusion(bf16[16,128,768]{2,1,0:T(8,128)(2,1)} %all-to-all-done), kind=kLoop, calls=%fused_computation.120 | loop fusion | bytes 6291456 | tf_op jit(solution)/shard_map/slice | solution.py:82
  94.1 5.9 %convolution_convert_fusion.3 = bf16[1024,768]{1,0:T(8,128)(2,1)} fusion(bf16[1024,768]{1,0:T(8,128)(2,1)} %bitcast.127, bf16[1024,64]{1,0:T(8,128)(2,1)S(1)} %bitcast.133, s32[1024]{0:T(1024)S(1)} %get-tuple-element.78, s32[1024]{0:T(1024)S(1)} %get-tuple-element.79, pred[1024]{0:T(1024)(128)(4,1)S(1)} %copy-done.9, s32[1024]{0:T(1024)S(1)} %get-tuple-element.77, ...), kind=kOutput, calls=%fused_computation.34 | convolution fusion | flops 1751056384 | bytes 3295232 | tf_op jit(solution)/shard_map/dot_general | solution.py:25
  100.0 3.9 %fusion.8 = bf16[1024,768]{1,0:T(8,128)(2,1)S(1)} fusion(bf16[16,64,768]{2,1,0:T(8,128)(2,1)} %get-tuple-element.3, bf16[1024,768]{1,0:T(8,128)(2,1)} %convolution_convert_fusion.3, bf16[768,768]{1,0:T(8,128)(2,1)S(1)} %copy-done.10), kind=kOutput, calls=%fused_computation.17 | convolution fusion | flops 1215823872 | bytes 5898240 | tf_op jit(solution)/shard_map/dot_general | solution.py:25
  105.6 3.2 %collective-permute-start = (bf16[1,2,2,2,48,384]{5,4,3,2,1,0:T(8,128)(2,1)S(1)}, bf16[1,2,2,2,48,384]{5,4,3,2,1,0:T(8,128)(2,1)S(1)}, u32[]{:S(2)}, u32[]{:S(2)}) collective-permute-start(bf16[1,2,2,2,48,384]{5,4,3,2,1,0:T(8,128)(2,1)S(1)} %constant_dynamic-slice_fusion.3), channel_id=1, source_target_pairs={{0,16},{16,0},{32,48},{48,32},{64,80},{80,64},{96,112},{112,96},{1... | collective-permute-start | bytes 884744 | tf_op jit(solution)/shard_map/ppermute | solution.py:31
  111.9 3.3 %collective-permute-done.1 = bf16[1,1,2,2,48,384]{5,4,3,2,1,0:T(8,128)(2,1)S(1)} collective-permute-done((bf16[1,1,2,2,48,384]{5,4,3,2,1,0:T(8,128)(2,1)S(1)}, bf16[1,1,2,2,48,384]{5,4,3,2,1,0:T(8,128)(2,1)S(1)}, u32[]{:S(2)}, u32[]{:S(2)}) %collective-permute-start.1) | collective-permute-done | bytes 147488 | tf_op jit(solution)/shard_map/ppermute | solution.py:31
  117.6 2.2 %collective-permute-done.2 = bf16[1,1,1,2,48,384]{5,4,3,2,1,0:T(8,128)(2,1)S(1)} collective-permute-done((bf16[1,1,1,2,48,384]{5,4,3,2,1,0:T(8,128)(2,1)S(1)}, bf16[1,1,1,2,48,384]{5,4,3,2,1,0:T(8,128)(2,1)S(1)}, u32[]{:S(2)}, u32[]{:S(2)}) %collective-permute-start.2) | collective-permute-done | bytes 73760 | tf_op jit(solution)/shard_map/ppermute | solution.py:31
  119.8 2.9 %collective-permute-start.3 = (bf16[1,1,1,1,48,384]{5,4,3,2,1,0:T(8,128)(2,1)S(1)}, bf16[1,1,1,1,48,384]{5,4,3,2,1,0:T(8,128)(2,1)S(1)}, u32[]{:S(2)}, u32[]{:S(2)}) collective-permute-start(bf16[1,1,1,1,48,384]{5,4,3,2,1,0:T(8,128)(2,1)S(1)} %dynamic-slice_convert_fusion.11), channel_id=1, source_target_pairs={{0,128},{16,144},{32,160},{48,176},{64,192},{80,208},{96,224},{112... | collective-permute-start | bytes 110600 | tf_op jit(solution)/shard_map/ppermute | solution.py:31
  124.5 3.3 %collective-permute-done.7 = bf16[1,1,1,1,48,384]{5,4,3,2,1,0:T(8,128)(2,1)S(1)} collective-permute-done((bf16[1,1,1,1,48,384]{5,4,3,2,1,0:T(8,128)(2,1)S(1)}, bf16[1,1,1,1,48,384]{5,4,3,2,1,0:T(8,128)(2,1)S(1)}, u32[]{:S(2)}, u32[]{:S(2)}) %collective-permute-start.7) | collective-permute-done | bytes 36896 | tf_op jit(solution)/shard_map/ppermute | solution.py:31
  128.3 15.0 %all_to_all.15 = bf16[16,48,240]{2,1,0:T(8,128)(2,1)S(1)} all-to-all(bf16[16,48,240]{2,1,0:T(8,128)(2,1)S(1)} %pad_maximum_fusion.1), channel_id=1, replica_groups=mesh['dp'=16,'seq'=16] {'seq'}, dimensions={0} | all-to-all | bytes 737280 | tf_op jit(solution)/shard_map/all_to_all | solution.py:60
  143.4 21.0 %all_to_all.16 = bf16[16,48,240]{2,1,0:T(8,128)(2,1)S(1)} all-to-all(bf16[16,48,240]{2,1,0:T(8,128)(2,1)S(1)} %broadcast_in_dim.12), channel_id=1, replica_groups=mesh['dp'=16,'seq'=16] {'dp'}, dimensions={0} | all-to-all | bytes 737280 | tf_op jit(solution)/shard_map/all_to_all | solution.py:60
  (141 shorter events, 35.9 us)
Async XLA Ops:
  0.6 21.8 %copy-start = (bf16[768,1536]{1,0:T(8,128)(2,1)S(1)}, bf16[768,1536]{1,0:T(8,128)(2,1)}, u32[]{:S(2)}) copy-start(bf16[768,1536]{1,0:T(8,128)(2,1)} %param.10) | copy-start | bytes 7077892
  9.4 80.9 %all-to-all-start = ((bf16[16,128,768]{2,1,0:T(8,128)(2,1)}), bf16[16,128,768]{2,1,0:T(8,128)(2,1)}, u32[]{:S(2)}, u32[]{:S(2)}) async-start(bf16[16,128,768]{2,1,0:T(8,128)(2,1)} %pad_maximum_fusion), calls=%async_computation | async-start | bytes 6291456 | tf_op jit(solution)/shard_map/all_to_all | solution.py:60
  22.4 4.1 %copy-start.6 = (bf16[1,4,256,768]{3,2,1,0:T(8,128)(2,1)S(1)}, bf16[1,4,256,768]{3,2,1,0:T(8,128)(2,1)}, u32[]{:S(2)}) copy-start(bf16[1,4,256,768]{3,2,1,0:T(8,128)(2,1)} %param.8) | copy-start | bytes 4718596
  32.0 16.4 %collective-permute-start.12 = (bf16[1,2,2,2,48,1536]{5,4,3,2,1,0:T(8,128)(2,1)}, bf16[1,2,2,2,48,1536]{5,4,3,2,1,0:T(8,128)(2,1)}, u32[]{:S(2)}, u32[]{:S(2)}) collective-permute-start(bf16[1,2,2,2,48,1536]{5,4,3,2,1,0:T(8,128)(2,1)} %constant_dynamic-slice_fusion), channel_id=1, source_target_pairs={{0,16},{16,0},{32,48},{48,32},{64,80},{80,64},{96,112},{112,96},{1... | collective-permute-start | bytes 3538952 | tf_op jit(solution)/shard_map/ppermute | solution.py:31
  47.8 8.3 %collective-permute-start.8 = (bf16[1,2,2,2,96,768]{5,4,3,2,1,0:T(8,128)(2,1)}, bf16[1,2,2,2,96,768]{5,4,3,2,1,0:T(8,128)(2,1)S(1)}, u32[]{:S(2)}, u32[]{:S(2)}) collective-permute-start(bf16[1,2,2,2,96,768]{5,4,3,2,1,0:T(8,128)(2,1)} %constant_dynamic-slice_fusion.1), channel_id=1, source_target_pairs={{0,16},{16,0},{32,48},{48,32},{64,80},{80,64},{96,112},{112,96},{1... | collective-permute-start | bytes 3538952 | tf_op jit(solution)/shard_map/ppermute | solution.py:31
  51.3 16.5 %collective-permute-start.13 = (bf16[1,2,1,2,48,1536]{5,4,3,2,1,0:T(8,128)(2,1)}, bf16[1,2,1,2,48,1536]{5,4,3,2,1,0:T(8,128)(2,1)}, u32[]{:S(2)}, u32[]{:S(2)}) collective-permute-start(bf16[1,2,1,2,48,1536]{5,4,3,2,1,0:T(8,128)(2,1)} %dynamic-slice_convert_fusion), channel_id=1, source_target_pairs={{0,96},{16,112},{32,64},{48,80},{64,32},{80,48},{96,0},{112,16},{1... | collective-permute-start | bytes 1769480 | tf_op jit(solution)/shard_map/ppermute | solution.py:31
  57.7 14.8 %collective-permute-start.9 = (bf16[1,1,2,2,96,768]{5,4,3,2,1,0:T(8,128)(2,1)S(1)}, bf16[1,1,2,2,96,768]{5,4,3,2,1,0:T(8,128)(2,1)S(1)}, u32[]{:S(2)}, u32[]{:S(2)}) collective-permute-start(bf16[1,1,2,2,96,768]{5,4,3,2,1,0:T(8,128)(2,1)S(1)} %dynamic-slice_convert_fusion.1), channel_id=1, source_target_pairs={{0,32},{16,48},{32,0},{48,16},{64,96},{80,112},{96,64},{112,80},{1... | collective-permute-start | bytes 1769480 | tf_op jit(solution)/shard_map/ppermute | solution.py:31
  69.0 9.9 %collective-permute-start.14 = (bf16[1,1,1,2,48,1536]{5,4,3,2,1,0:T(8,128)(2,1)S(1)}, bf16[1,1,1,2,48,1536]{5,4,3,2,1,0:T(8,128)(2,1)S(1)}, u32[]{:S(2)}, u32[]{:S(2)}) collective-permute-start(bf16[1,1,1,2,48,1536]{5,4,3,2,1,0:T(8,128)(2,1)S(1)} %dynamic-slice_convert_fusion.2), channel_id=1, source_target_pairs={{0,32},{16,48},{32,0},{48,16},{64,96},{80,112},{96,64},{112,80},{1... | collective-permute-start | bytes 884744 | tf_op jit(solution)/shard_map/ppermute | solution.py:31
  72.8 9.0 %collective-permute-start.10 = (bf16[1,1,1,2,96,768]{5,4,3,2,1,0:T(8,128)(2,1)S(1)}, bf16[1,1,1,2,96,768]{5,4,3,2,1,0:T(8,128)(2,1)S(1)}, u32[]{:S(2)}, u32[]{:S(2)}) collective-permute-start(bf16[1,1,1,2,96,768]{5,4,3,2,1,0:T(8,128)(2,1)S(1)} %dynamic-slice_convert_fusion.3), channel_id=1, source_target_pairs={{0,96},{16,112},{32,64},{48,80},{64,32},{80,48},{96,0},{112,16},{1... | collective-permute-start | bytes 884744 | tf_op jit(solution)/shard_map/ppermute | solution.py:31
  79.0 6.6 %collective-permute-start.15 = (bf16[1,1,1,1,48,1536]{5,4,3,2,1,0:T(8,128)(2,1)S(1)}, bf16[1,1,1,1,48,1536]{5,4,3,2,1,0:T(8,128)(2,1)S(1)}, u32[]{:S(2)}, u32[]{:S(2)}) collective-permute-start(bf16[1,1,1,1,48,1536]{5,4,3,2,1,0:T(8,128)(2,1)S(1)} %dynamic-slice_convert_fusion.4), channel_id=1, source_target_pairs={{0,128},{16,144},{32,160},{48,176},{64,192},{80,208},{96,224},{112... | collective-permute-start | bytes 442376 | tf_op jit(solution)/shard_map/ppermute | solution.py:31
  81.8 27.0 %collective-permute-start.11 = (bf16[1,1,1,1,96,768]{5,4,3,2,1,0:T(8,128)(2,1)S(1)}, bf16[1,1,1,1,96,768]{5,4,3,2,1,0:T(8,128)(2,1)S(1)}, u32[]{:S(2)}, u32[]{:S(2)}) collective-permute-start(bf16[1,1,1,1,96,768]{5,4,3,2,1,0:T(8,128)(2,1)S(1)} %dynamic-slice_convert_fusion.5), channel_id=1, source_target_pairs={{0,128},{16,144},{32,160},{48,176},{64,192},{80,208},{96,224},{112... | collective-permute-start | bytes 442376 | tf_op jit(solution)/shard_map/ppermute | solution.py:31
  87.4 6.6 %copy-start.7 = (bf16[64,16,64]{2,1,0:T(8,128)(2,1)S(1)}, bf16[64,16,64]{2,1,0:T(8,128)(2,1)}, u32[]{:S(2)}) copy-start(bf16[64,16,64]{2,1,0:T(8,128)(2,1)} %copy.47) | copy-start | bytes 393220
  87.4 6.6 %copy-start.8 = (pred[1024]{0:T(1024)(128)(4,1)S(1)}, pred[1024]{0:T(1024)(128)(4,1)}, u32[]{:S(2)}) copy-start(pred[1024]{0:T(1024)(128)(4,1)} %get-tuple-element.75) | copy-start | bytes 3076
  87.5 6.6 %copy-start.9 = (pred[1024]{0:T(1024)(128)(4,1)S(1)}, pred[1024]{0:T(1024)(128)(4,1)}, u32[]{:S(2)}) copy-start(pred[1024]{0:T(1024)(128)(4,1)} %get-tuple-element.76) | copy-start | bytes 3076
  94.1 5.9 %copy-start.10 = (bf16[768,768]{1,0:T(8,128)(2,1)S(1)}, bf16[768,768]{1,0:T(8,128)(2,1)}, u32[]{:S(2)}) copy-start(bf16[768,768]{1,0:T(8,128)(2,1)} %param.9) | copy-start | bytes 3538948
  105.6 4.4 %collective-permute-start = (bf16[1,2,2,2,48,384]{5,4,3,2,1,0:T(8,128)(2,1)S(1)}, bf16[1,2,2,2,48,384]{5,4,3,2,1,0:T(8,128)(2,1)S(1)}, u32[]{:S(2)}, u32[]{:S(2)}) collective-permute-start(bf16[1,2,2,2,48,384]{5,4,3,2,1,0:T(8,128)(2,1)S(1)} %constant_dynamic-slice_fusion.3), channel_id=1, source_target_pairs={{0,16},{16,0},{32,48},{48,32},{64,80},{80,64},{96,112},{112,96},{1... | collective-permute-start | bytes 884744 | tf_op jit(solution)/shard_map/ppermute | solution.py:31
  109.0 1.7 collective-permute-start.4
  110.1 5.1 %collective-permute-start.1 = (bf16[1,1,2,2,48,384]{5,4,3,2,1,0:T(8,128)(2,1)S(1)}, bf16[1,1,2,2,48,384]{5,4,3,2,1,0:T(8,128)(2,1)S(1)}, u32[]{:S(2)}, u32[]{:S(2)}) collective-permute-start(bf16[1,1,2,2,48,384]{5,4,3,2,1,0:T(8,128)(2,1)S(1)} %dynamic-slice_convert_fusion.7), channel_id=1, source_target_pairs={{0,32},{16,48},{32,0},{48,16},{64,96},{80,112},{96,64},{112,80},{1... | collective-permute-start | bytes 442376 | tf_op jit(solution)/shard_map/ppermute | solution.py:31
  110.8 6.6 %collective-permute-start.5 = (bf16[1,2,1,2,48,384]{5,4,3,2,1,0:T(8,128)(2,1)S(1)}, bf16[1,2,1,2,48,384]{5,4,3,2,1,0:T(8,128)(2,1)S(1)}, u32[]{:S(2)}, u32[]{:S(2)}) collective-permute-start(bf16[1,2,1,2,48,384]{5,4,3,2,1,0:T(8,128)(2,1)S(1)} %dynamic-slice_convert_fusion.6), channel_id=1, source_target_pairs={{0,96},{16,112},{32,64},{48,80},{64,32},{80,48},{96,0},{112,16},{1... | collective-permute-start | bytes 442376 | tf_op jit(solution)/shard_map/ppermute | solution.py:31
  115.3 4.5 %collective-permute-start.2 = (bf16[1,1,1,2,48,384]{5,4,3,2,1,0:T(8,128)(2,1)S(1)}, bf16[1,1,1,2,48,384]{5,4,3,2,1,0:T(8,128)(2,1)S(1)}, u32[]{:S(2)}, u32[]{:S(2)}) collective-permute-start(bf16[1,1,1,2,48,384]{5,4,3,2,1,0:T(8,128)(2,1)S(1)} %dynamic-slice_convert_fusion.9), channel_id=1, source_target_pairs={{0,96},{16,112},{32,64},{48,80},{64,32},{80,48},{96,0},{112,16},{1... | collective-permute-start | bytes 221192 | tf_op jit(solution)/shard_map/ppermute | solution.py:31
  117.5 5.2 %collective-permute-start.6 = (bf16[1,1,1,2,48,384]{5,4,3,2,1,0:T(8,128)(2,1)S(1)}, bf16[1,1,1,2,48,384]{5,4,3,2,1,0:T(8,128)(2,1)S(1)}, u32[]{:S(2)}, u32[]{:S(2)}) collective-permute-start(bf16[1,1,1,2,48,384]{5,4,3,2,1,0:T(8,128)(2,1)S(1)} %dynamic-slice_convert_fusion.8), channel_id=1, source_target_pairs={{0,32},{16,48},{32,0},{48,16},{64,96},{80,112},{96,64},{112,80},{1... | collective-permute-start | bytes 221192 | tf_op jit(solution)/shard_map/ppermute | solution.py:31
  119.8 4.6 %collective-permute-start.3 = (bf16[1,1,1,1,48,384]{5,4,3,2,1,0:T(8,128)(2,1)S(1)}, bf16[1,1,1,1,48,384]{5,4,3,2,1,0:T(8,128)(2,1)S(1)}, u32[]{:S(2)}, u32[]{:S(2)}) collective-permute-start(bf16[1,1,1,1,48,384]{5,4,3,2,1,0:T(8,128)(2,1)S(1)} %dynamic-slice_convert_fusion.11), channel_id=1, source_target_pairs={{0,128},{16,144},{32,160},{48,176},{64,192},{80,208},{96,224},{112... | collective-permute-start | bytes 110600 | tf_op jit(solution)/shard_map/ppermute | solution.py:31
  122.8 5.0 %collective-permute-start.7 = (bf16[1,1,1,1,48,384]{5,4,3,2,1,0:T(8,128)(2,1)S(1)}, bf16[1,1,1,1,48,384]{5,4,3,2,1,0:T(8,128)(2,1)S(1)}, u32[]{:S(2)}, u32[]{:S(2)}) collective-permute-start(bf16[1,1,1,1,48,384]{5,4,3,2,1,0:T(8,128)(2,1)S(1)} %dynamic-slice_convert_fusion.10), channel_id=1, source_target_pairs={{0,128},{16,144},{32,160},{48,176},{64,192},{80,208},{96,224},{112... | collective-permute-start | bytes 110600 | tf_op jit(solution)/shard_map/ppermute | solution.py:31
  143.3 26.1 %copy-start.1 = (bf16[768,1536]{1,0:T(8,128)(2,1)S(1)}, bf16[768,1536]{1,0:T(8,128)(2,1)}, u32[]{:S(2)}) copy-start(bf16[768,1536]{1,0:T(8,128)(2,1)} %param.10) | copy-start | bytes 7077892
  (6 other events, 14.4 us)

commit v2 on v1

v2 whole, which is shorter than its diff:
```python
import functools

import jax
import jax.numpy as jnp
from jax import lax
from jax.experimental import pallas as pl
from jax.experimental.pallas import tpu as pltpu
from jax.sharding import PartitionSpec as P

BF16 = jnp.bfloat16
F32 = jnp.float32
VMEM_LIMIT = 56 * 1024 * 1024
PIECE = [
    (i & 1) * 8 + ((((i >> 1) ^ (i >> 2)) & 1) * 4) + ((i >> 2) & 1) * 2 + (i >> 3)
    for i in range(16)
]


def product(left, right, left_dim, right_dim):
    return lax.dot_general(
        left, right, (((left_dim,), (right_dim,)), ((), ())), preferred_element_type=F32
    )


def normalise(block):
    wide = block.astype(F32)
    return (wide * lax.rsqrt(jnp.mean(wide * wide, axis=-1, keepdims=True) + 1e-06)).astype(BF16)


def send_kernel(inputs_ref, cot_ref, first_ref, sent_ref):
    normed = normalise(inputs_ref[0, 0])
    weighted = (cot_ref[0, 0].astype(F32) * normed.astype(F32)).astype(BF16)
    places, _, _, size, width = sent_ref.shape
    sent_ref[:, 1, 0] = weighted.reshape(places, size, width)
    mix = product(first_ref[0], normed, 1, 0).astype(BF16)
    sent_ref[:, 0, 0] = mix.reshape(places, size, width)


def build_sent(inputs, cotangent, first_blocks, places):
    _, rows, block, width = inputs.shape
    size = block // places
    whole = pl.BlockSpec((1, 1, block, width), lambda a: (0, a, 0, 0))
    return pl.pallas_call(
        send_kernel,
        grid=(rows,),
        in_specs=[whole, whole, pl.BlockSpec((1, block, block), lambda a: (a, 0, 0))],
        out_specs=pl.BlockSpec((places, 2, 1, size, width), lambda a: (0, 0, a, 0, 0)),
        out_shape=jax.ShapeDtypeStruct((places, 2, rows, size, width), BF16),
        compiler_params=pltpu.CompilerParams(vmem_limit_bytes=VMEM_LIMIT),
        name="send",
    )(inputs, cotangent, first_blocks)


def mlp_kernel(inputs_ref, cot_ref, up_ref, down_ref, up_t_ref, down_t_ref, normed_ref, cot_t_ref):
    @pl.when(pl.program_id(0) == 0)
    def _():
        normed_ref[...] = normalise(inputs_ref[...])
        cot_t_ref[...] = cot_ref[...].T

    field = product(normed_ref[...], up_ref[...], 1, 0)
    back = product(cot_ref[...], down_ref[...], 1, 1)
    scale, cubic = 0.7978845608028654, 0.044715
    square = field * field
    bend = jnp.tanh(scale * field * (1.0 + cubic * square))
    upper = 0.5 + 0.5 * bend
    hidden = (field * upper).astype(BF16)
    slope = upper + (0.5 * scale) * field * (1.0 - bend * bend) * (1.0 + 3.0 * cubic * square)
    up_slope = (back * slope).astype(BF16)
    down_t_ref[...] = product(cot_t_ref[...], hidden, 1, 0).astype(BF16)
    up_t_ref[...] = product(up_slope, normed_ref[...], 0, 0).astype(BF16)


def mlp_grads(inputs, cotangent, up_weight, down_weight):
    positions, width = inputs.shape
    units = up_weight.shape[1]
    step = 256
    whole = pl.BlockSpec((positions, width), lambda f: (0, 0))
    by_row = pl.BlockSpec((step, width), lambda f: (f, 0))
    by_col = pl.BlockSpec((width, step), lambda f: (0, f))
    return pl.pallas_call(
        mlp_kernel,
        grid=(units // step,),
        in_specs=[whole, whole, by_col, by_row],
        out_specs=[by_row, by_col],
        out_shape=[
            jax.ShapeDtypeStruct((units, width), BF16),
            jax.ShapeDtypeStruct((width, units), BF16),
        ],
        scratch_shapes=[pltpu.VMEM((positions, width), BF16), pltpu.VMEM((width, positions), BF16)],
        compiler_params=pltpu.CompilerParams(vmem_limit_bytes=VMEM_LIMIT),
        name="mlp",
    )(inputs, cotangent, up_weight, down_weight)


def spread_kernel(blocks, stacked_ref, out_ref):
    positions, size = stacked_ref.shape
    take = lax.broadcasted_iota(jnp.int32, (size, positions), 1) // blocks
    spread = (take == lax.broadcasted_iota(jnp.int32, (size, positions), 0)).astype(BF16)
    wide = product(stacked_ref[...], spread, 1, 0)
    row = lax.broadcasted_iota(jnp.int32, (positions, positions), 0)
    col = lax.broadcasted_iota(jnp.int32, (positions, positions), 1)
    out_ref[...] = jnp.where(row % blocks == col % blocks, wide, 0.0).astype(BF16)


def spread_second(second_blocks):
    blocks, size, _ = second_blocks.shape
    positions = blocks * size
    stacked = second_blocks.transpose(1, 0, 2).reshape(positions, size)
    return pl.pallas_call(
        functools.partial(spread_kernel, blocks),
        out_shape=jax.ShapeDtypeStruct((positions, positions), BF16),
        compiler_params=pltpu.CompilerParams(vmem_limit_bytes=VMEM_LIMIT),
        name="spread",
    )(stacked)


def value_kernel(mix_ref, weighted_ref, second_ref, weight_ref, out_ref, both_ref):
    positions = second_ref.shape[0]

    @pl.when(pl.program_id(0) == 0)
    def _():
        first_mix = mix_ref[:, 0].reshape(positions, -1)
        both_ref[...] = product(second_ref[...], first_mix, 1, 0).astype(BF16)

    mixed = product(both_ref[...], weight_ref[...], 1, 0)
    sigmoid_part = 0.5 + 0.5 * jnp.tanh(0.5 * mixed)
    weighted = weighted_ref[:, 0].reshape(mixed.shape).astype(F32)
    slope = weighted * (sigmoid_part * (1.0 + mixed * (1.0 - sigmoid_part)))
    out_ref[...] = product(slope.astype(BF16), both_ref[...], 0, 0).astype(BF16)


def value_grad(came, second, value_weight):
    places, _, size, width = came.shape
    positions = places * size
    step = 256
    return pl.pallas_call(
        value_kernel,
        grid=(width // step,),
        in_specs=[
            pl.BlockSpec((places, 1, size, width), lambda e: (0, 0, 0, 0)),
            pl.BlockSpec((places, 1, size, step), lambda e: (0, 1, 0, e)),
            pl.BlockSpec((positions, positions), lambda e: (0, 0)),
            pl.BlockSpec((width, step), lambda e: (0, e)),
        ],
        out_specs=pl.BlockSpec((step, width), lambda e: (e, 0)),
        out_shape=jax.ShapeDtypeStruct((width, width), BF16),
        scratch_shapes=[pltpu.VMEM((positions, width), BF16)],
        compiler_params=pltpu.CompilerParams(vmem_limit_bytes=VMEM_LIMIT),
        name="value",
    )(came, came, second, value_weight)


def join_kernel(pieces_ref, value_ref, up_ref, down_ref, rows_ref):
    places, size, lanes = pieces_ref.shape
    for i in range(places):
        rows_ref[PIECE[i] * size : (PIECE[i] + 1) * size, :lanes] = pieces_ref[i]
    turned = rows_ref[...].T
    width = value_ref.shape[1]
    share = value_ref.shape[0]
    value_ref[...] = turned[:share]
    up_ref[:, :width] = turned[share : 2 * share]
    up_ref[:, width:] = turned[2 * share : 3 * share]
    down_ref[...] = turned[3 * share : 5 * share]


def join(pieces):
    places, size, lanes = pieces.shape
    width = places * size
    share = lanes // 5
    padded = -(-lanes // 128) * 128
    return pl.pallas_call(
        join_kernel,
        out_shape=[
            jax.ShapeDtypeStruct((share, width), BF16),
            jax.ShapeDtypeStruct((share, 2 * width), BF16),
            jax.ShapeDtypeStruct((2 * share, width), BF16),
        ],
        scratch_shapes=[pltpu.VMEM((width, padded), BF16)],
        compiler_params=pltpu.CompilerParams(vmem_limit_bytes=VMEM_LIMIT),
        name="join",
    )(pieces)


def swap(block, flip):
    return lax.ppermute(block, "dp", [(i, i ^ flip) for i in range(16)])


def halve(total, axis, bit, flip):
    mine = lax.dynamic_slice_in_dim(total, bit, 1, axis)
    other = lax.dynamic_slice_in_dim(total, 1 - bit, 1, axis).astype(BF16)
    return mine.astype(F32) + swap(other, flip).astype(F32)


def scatter_dp(left, right):
    i = lax.axis_index("dp")
    core, x0, x1, y_hi = i & 1, (i >> 1) & 1, (i >> 2) & 1, i >> 3
    out = []
    for straight, block in ((True, left), (False, right)):
        groups, rows, lanes = block.shape
        total = block.reshape(groups, 2, 2, 2, 2, rows // 16, lanes)
        total = halve(total, 1, core, 1)
        if straight:
            total = halve(total, 2, x0 ^ x1, 2)
            total = halve(total, 3, x1, 6)
        else:
            total = halve(total, 3, x1, 6)
            total = halve(total, 2, x0 ^ x1, 2)
        total = halve(total, 4, y_hi, 8)
        out.append(total.reshape(groups, rows // 16, lanes))
    return out


def exchange(block, axis):
    return lax.all_to_all(block, axis, split_axis=0, concat_axis=0, tiled=True)


def by_place(block, places):
    rows, lanes = block.shape
    return block.astype(BF16).reshape(rows, places, lanes // places).transpose(1, 0, 2)


def local(inputs, cotangent, value_weight, up_weight, down_weight, first_blocks, second_blocks):
    width = inputs.shape[3]
    places = lax.axis_size("seq")
    sent = build_sent(inputs, cotangent, first_blocks, places)
    came = exchange(sent.reshape(places, 2, -1, width), "seq")

    second = spread_second(second_blocks)
    flat, second = lax.optimization_barrier((inputs.reshape(-1, width), second))
    up_t, down_t = mlp_grads(flat, cotangent.reshape(-1, width), up_weight, down_weight)
    up_t, down_t = scatter_dp(up_t.reshape(2, width, width), down_t[None])

    value_t = value_grad(came, second, value_weight)
    value_left, value_right = scatter_dp(
        value_t[None, :, : width // 2], value_t[None, :, width // 2 :]
    )
    value_t = jnp.concatenate([value_left[0], value_right[0]], axis=1)

    packed = jnp.concatenate(
        [by_place(part, places) for part in (value_t, up_t[0], up_t[1], down_t[0])], axis=2
    )
    total_tokens = (
        inputs.shape[0] * inputs.shape[1] * inputs.shape[2] * lax.axis_size("dp") * places
    )
    factor = float(total_tokens) ** (-0.5)
    packed = (jnp.sum(exchange(packed, "seq").astype(F32), axis=0) * factor).astype(BF16)
    return tuple(join(exchange(jnp.broadcast_to(packed[None], (16,) + packed.shape), "dp")))


def solution(mesh):
    placed = (
        P("dp", "seq", None, None),
        P("dp", "seq", None, None),
        P(),
        P(),
        P(),
        P("seq", None, None),
        P("seq", None, None),
    )
    return jax.shard_map(
        local,
        mesh=mesh,
        in_specs=placed,
        out_specs=(P("seq", None), P("seq", None), P("seq", None)),
        check_vma=False,
    )
```

time: 170 us -> 161 us (0.947)
  Pallas kernels: 0 us -> 37.6 us
  matrix products: 35 us -> 0 us
  local copies, waits for them, and re-layouts: 19.1 us -> 11.4 us
  other arithmetic: 14.2 us -> 7.34 us
  starting transfers between devices: 27.7 us -> 32.7 us
  waiting for transfers between devices: 36.4 us -> 32.8 us
  blocking collectives: 36 us -> 37.8 us
    pallas_call x0 -> x5, Pallas kernels: none -> 37.6 us  [the longest x1 17.2 us: mlp_grads(): pl.pallas_call(mlp_kernel, grid=(units // step,), in_specs=[whole, whole,...]
    dot_general x7 -> x0, matrix products: 35 us -> none  [the longest x6 32.7 us: product(): lax.dot_general(left, right, (((left_dim,), (right_dim,)), ((), ())), pre...]
    slice x35 -> x2, local copies, waits for them, and re-layouts: 7 us -> 1.37 us  [the longest x1 1.36 us: local(): value_t[None, :, :width // 2]]
    ppermute x16, starting transfers between devices: 17.5 us -> 22.5 us  [swap(): return lax.ppermute(block, 'dp', [(i, i ^ flip) for i in range(16)])]
    convert_element_type x3 -> x2, other arithmetic: 3.41 us -> 0.04 us  [the longest x1 0.03 us: by_place(): block.astype(BF16).reshape(rows, places, lanes // places).transpose(1, 0, 2)]
    ppermute x16, waiting for transfers between devices: 33.6 us -> 31 us  [swap(): return lax.ppermute(block, 'dp', [(i, i ^ flip) for i in range(16)])]
    concatenate x3 -> x1, other arithmetic: 2.94 us -> 0.39 us  [local(): jnp.concatenate([by_place(part, places) for part in (value_t, up_t[0], up...]
    reduce_sum x2 -> x1, other arithmetic: 2.01 us -> 0.07 us  [local(): jnp.sum(exchange(packed, 'seq').astype(F32), axis=0) * factor]
  transfers between devices with their start and end apart: 17 -> 17, of which waited for: 12 -> 12; matrix products, arithmetic and copies ran while one was open for 31% -> 9% of each run, Pallas kernels for 0% -> 13%
where the time goes in v2:
time: 161 us
  blocking collectives  37.8 us (23%)
  Pallas kernels  37.6 us (23%)
  waiting for transfers between devices  32.8 us (20%)
  starting transfers between devices  32.7 us (20%)
  local copies, waits for them, and re-layouts  11.4 us (7%)
  other arithmetic  7.34 us (5%)
    all_to_all x2, blocking collectives, exchange(): return lax.all_to_all(block, axis, split_axis=0, concat_axis=0, tiled=True)  37.8 us
    ppermute x16, waiting for transfers between devices, swap(): return lax.ppermute(block, 'dp', [(i, i ^ flip) for i in range(16)])  31 us
    ppermute x16, starting transfers between devices, swap(): return lax.ppermute(block, 'dp', [(i, i ^ flip) for i in range(16)])  22.5 us
    pallas_call x1, Pallas kernels, mlp_grads(): pl.pallas_call(mlp_kernel, grid=(units // step,), in_specs=[whole, whole,...  17.2 us
    pallas_call x1, Pallas kernels, value_grad(): pl.pallas_call(value_kernel, grid=(width // step,), in_specs=[pl.BlockSpe...  10.5 us
    all_to_all x1, starting transfers between devices, exchange(): return lax.all_to_all(block, axis, split_axis=0, concat_axis=0, tiled=True)  10.3 us
    add x12, other arithmetic, halve(): return mine.astype(F32) + swap(other, flip).astype(F32)  6.75 us
    pallas_call x1, Pallas kernels, build_sent(): pl.pallas_call(send_kernel, grid=(rows,), in_specs=[whole, whole, pl.Bloc...  5.11 us
  transfers between devices with their start and end apart: 17, of which 12 were waited for; matrix products, arithmetic and copies ran while one was open for 9% of the time, Pallas kernels for 13%

profile of v2, /device:TPU:1, one launch (start us, length us, event | category | flops | bytes accessed | tf_op | source)
XLA Modules:
  0.0 160.8 jit_solution(12894976018173950735)
XLA Ops:
  0.6 5.1 %send.1 = bf16[16,2,4,16,768]{4,3,2,1,0:T(8,128)(2,1)} custom-call(bf16[1,4,256,768]{3,2,1,0:T(8,128)(2,1)} %inputs_ref.1, bf16[1,4,256,768]{3,2,1,0:T(8,128)(2,1)} %cot_ref.1, bf16[4,256,256]{2,1,0:T(8,128)(2,1)} %first_ref.1), custom_call_target="tpu_custom_call" | custom-call | tf_op jit(solution)/shard_map/send/pallas_call | solution.py:43
  5.7 10.3 %all-to-all-start = ((bf16[16,2,64,768]{3,2,1,0:T(8,128)(2,1)}), bf16[16,2,64,768]{3,2,1,0:T(8,128)(2,1)S(1)}, u32[]{:S(2)}, u32[]{:S(2)}) async-start(bf16[16,2,64,768]{3,2,1,0:T(8,128)(2,1)} %bitcast.24), calls=%async_computation | async-start | bytes 6291456 | tf_op jit(solution)/shard_map/all_to_all | solution.py:214
  16.9 3.0 %spread.1.second_ref = bf16[1024,1024]{1,0:T(8,128)(2,1)} custom-call(bf16[1024,64]{1,0:T(8,128)(2,1)} %bitcast.35), custom_call_target="tpu_custom_call" | custom-call | tf_op jit(solution)/shard_map/spread/pallas_call | solution.py:109
  19.9 17.2 %mlp.1 = (bf16[1536,768]{1,0:T(8,128)(2,1)}, bf16[768,1536]{1,0:T(8,128)(2,1)}) custom-call(bf16[1024,768]{1,0:T(8,128)(2,1)} %bitcast.25, bf16[1024,768]{1,0:T(8,128)(2,1)} %bitcast.26, bf16[768,1536]{1,0:T(8,128)(2,1)} %up_ref.1, bf16[1536,768]{1,0:T(8,128)(2,1)} %down_ref.1), custom_call_target="tpu_custom_call" | custom-call | tf_op jit(solution)/shard_map/mlp/pallas_call | solution.py:80
  37.1 2.5 %constant_dynamic-slice_fusion.1 = bf16[2,1,2,2,2,48,768]{6,5,4,3,2,1,0:T(8,128)(2,1)} fusion(bf16[2,2,2,2,2,48,768]{6,5,4,3,2,1,0:T(8,128)(2,1)} %bitcast.29, s32[]{:T(128)S(6)} %select_n.17), kind=kLoop, calls=%fused_computation.33 | loop fusion | bytes 2359300 | tf_op jit(solution)/shard_map/dynamic_slice | solution.py:190
  43.4 2.1 %convert_add_fusion.1 = f32[2,1,2,2,2,48,768]{6,5,4,3,2,1,0:T(8,128)S(1)} fusion(bf16[2,1,2,2,2,48,768]{6,5,4,3,2,1,0:T(8,128)(2,1)} %collective-permute-done.8, bf16[2,2,2,2,2,48,768]{6,5,4,3,2,1,0:T(8,128)(2,1)} %bitcast.30, s32[]{:T(128)S(6)} %select_n.16), kind=kLoop, calls=%fused_computation.1 | loop fusion | flops 1769472 | bytes 4718596 | tf_op jit(solution)/shard_map/add | solution.py:191
  50.9 1.8 %collective-permute-start.13 = (bf16[1,1,2,1,2,48,1536]{6,5,4,3,2,1,0:T(8,128)(2,1)}, bf16[1,1,2,1,2,48,1536]{6,5,4,3,2,1,0:T(8,128)(2,1)}, u32[]{:S(2)}, u32[]{:S(2)}) collective-permute-start(bf16[1,1,2,1,2,48,1536]{6,5,4,3,2,1,0:T(8,128)(2,1)} %dynamic-slice_convert_fusion), channel_id=1, source_target_pairs={{0,96},{16,112},{32,64},{48,80},{64,32},{80,48},{96,0},{112,16},{1... | collective-permute-start | bytes 1769480 | tf_op jit(solution)/shard_map/ppermute | solution.py:185
  52.7 8.6 %collective-permute-done.9 = bf16[2,1,1,2,2,48,768]{6,5,4,3,2,1,0:T(8,128)(2,1)} collective-permute-done((bf16[2,1,1,2,2,48,768]{6,5,4,3,2,1,0:T(8,128)(2,1)}, bf16[2,1,1,2,2,48,768]{6,5,4,3,2,1,0:T(8,128)(2,1)}, u32[]{:S(2)}, u32[]{:S(2)}) %collective-permute-start.9) | collective-permute-done | bytes 589856 | tf_op jit(solution)/shard_map/ppermute | solution.py:185
  63.0 2.6 %collective-permute-start.10 = (bf16[2,1,1,1,2,48,768]{6,5,4,3,2,1,0:T(8,128)(2,1)S(1)}, bf16[2,1,1,1,2,48,768]{6,5,4,3,2,1,0:T(8,128)(2,1)S(1)}, u32[]{:S(2)}, u32[]{:S(2)}) collective-permute-start(bf16[2,1,1,1,2,48,768]{6,5,4,3,2,1,0:T(8,128)(2,1)S(1)} %dynamic-slice_convert_fusion.3), channel_id=1, source_target_pairs={{0,96},{16,112},{32,64},{48,80},{64,32},{80,48},{96,0},{112,16},{1... | collective-permute-start | bytes 884744 | tf_op jit(solution)/shard_map/ppermute | solution.py:185
  68.0 5.0 %collective-permute-done.10 = bf16[2,1,1,1,2,48,768]{6,5,4,3,2,1,0:T(8,128)(2,1)S(1)} collective-permute-done((bf16[2,1,1,1,2,48,768]{6,5,4,3,2,1,0:T(8,128)(2,1)S(1)}, bf16[2,1,1,1,2,48,768]{6,5,4,3,2,1,0:T(8,128)(2,1)S(1)}, u32[]{:S(2)}, u32[]{:S(2)}) %collective-permute-start.10) | collective-permute-done | bytes 294944 | tf_op jit(solution)/shard_map/ppermute | solution.py:185
  73.1 2.7 %collective-permute-start.11 = (bf16[2,1,1,1,1,48,768]{6,5,4,3,2,1,0:T(8,128)(2,1)S(1)}, bf16[2,1,1,1,1,48,768]{6,5,4,3,2,1,0:T(8,128)(2,1)S(1)}, u32[]{:S(2)}, u32[]{:S(2)}) collective-permute-start(bf16[2,1,1,1,1,48,768]{6,5,4,3,2,1,0:T(8,128)(2,1)S(1)} %dynamic-slice_convert_fusion.5), channel_id=1, source_target_pairs={{0,128},{16,144},{32,160},{48,176},{64,192},{80,208},{96,224},{112... | collective-permute-start | bytes 442376 | tf_op jit(solution)/shard_map/ppermute | solution.py:185
  77.3 1.9 %collective-permute-done.11 = bf16[2,1,1,1,1,48,768]{6,5,4,3,2,1,0:T(8,128)(2,1)S(1)} collective-permute-done((bf16[2,1,1,1,1,48,768]{6,5,4,3,2,1,0:T(8,128)(2,1)S(1)}, bf16[2,1,1,1,1,48,768]{6,5,4,3,2,1,0:T(8,128)(2,1)S(1)}, u32[]{:S(2)}, u32[]{:S(2)}) %collective-permute-start.11) | collective-permute-done | bytes 147488 | tf_op jit(solution)/shard_map/ppermute | solution.py:185
  79.3 5.5 %collective-permute-done.15 = bf16[1,1,1,1,1,48,1536]{6,5,4,3,2,1,0:T(8,128)(2,1)S(1)} collective-permute-done((bf16[1,1,1,1,1,48,1536]{6,5,4,3,2,1,0:T(8,128)(2,1)S(1)}, bf16[1,1,1,1,1,48,1536]{6,5,4,3,2,1,0:T(8,128)(2,1)S(1)}, u32[]{:S(2)}, u32[]{:S(2)}) %collective-permute-start.15) | collective-permute-done | bytes 147488 | tf_op jit(solution)/shard_map/ppermute | solution.py:185
  84.9 1.7 %all-to-all-done.mix_ref.weighted_ref = bf16[16,2,64,768]{3,2,1,0:T(8,128)(2,1)S(1)} async-done(((bf16[16,2,64,768]{3,2,1,0:T(8,128)(2,1)}), bf16[16,2,64,768]{3,2,1,0:T(8,128)(2,1)S(1)}, u32[]{:S(2)}, u32[]{:S(2)}) %all-to-all-start) | async-done | bytes 3145760 | tf_op jit(solution)/shard_map/all_to_all | solution.py:214
  88.2 10.5 %value.1 = bf16[768,768]{1,0:T(8,128)(2,1)} custom-call(bf16[16,2,64,768]{3,2,1,0:T(8,128)(2,1)} %copy-done, bf16[16,2,64,768]{3,2,1,0:T(8,128)(2,1)} %copy-done, bf16[1024,1024]{1,0:T(8,128)(2,1)} %spread.1.second_ref, bf16[768,768]{1,0:T(8,128)(2,1)} %weight_ref.1), custom_call_target="tpu_custom_call" | custom-call | tf_op jit(solution)/shard_map/value/pallas_call | solution.py:136
  100.1 1.8 %collective-permute-start = (bf16[1,1,2,2,2,48,384]{6,5,4,3,2,1,0:T(8,128)(2,1)S(1)}, bf16[1,1,2,2,2,48,384]{6,5,4,3,2,1,0:T(8,128)(2,1)S(1)}, u32[]{:S(2)}, u32[]{:S(2)}) collective-permute-start(bf16[1,1,2,2,2,48,384]{6,5,4,3,2,1,0:T(8,128)(2,1)S(1)} %constant_dynamic-slice_fusion.3), channel_id=1, source_target_pairs={{0,16},{16,0},{32,48},{48,32},{64,80},{80,64},{96,112},{112,96},{1... | collective-permute-start | bytes 884744 | tf_op jit(solution)/shard_map/ppermute | solution.py:185
  104.4 2.3 %collective-permute-start.5 = (bf16[1,1,2,1,2,48,384]{6,5,4,3,2,1,0:T(8,128)(2,1)S(1)}, bf16[1,1,2,1,2,48,384]{6,5,4,3,2,1,0:T(8,128)(2,1)S(1)}, u32[]{:S(2)}, u32[]{:S(2)}) collective-permute-start(bf16[1,1,2,1,2,48,384]{6,5,4,3,2,1,0:T(8,128)(2,1)S(1)} %dynamic-slice_convert_fusion.6), channel_id=1, source_target_pairs={{0,96},{16,112},{32,64},{48,80},{64,32},{80,48},{96,0},{112,16},{1... | collective-permute-start | bytes 442376 | tf_op jit(solution)/shard_map/ppermute | solution.py:185
  108.5 2.3 %collective-permute-start.2 = (bf16[1,1,1,1,2,48,384]{6,5,4,3,2,1,0:T(8,128)(2,1)S(1)}, bf16[1,1,1,1,2,48,384]{6,5,4,3,2,1,0:T(8,128)(2,1)S(1)}, u32[]{:S(2)}, u32[]{:S(2)}) collective-permute-start(bf16[1,1,1,1,2,48,384]{6,5,4,3,2,1,0:T(8,128)(2,1)S(1)} %dynamic-slice_convert_fusion.9), channel_id=1, source_target_pairs={{0,96},{16,112},{32,64},{48,80},{64,32},{80,48},{96,0},{112,16},{1... | collective-permute-start | bytes 221192 | tf_op jit(solution)/shard_map/ppermute | solution.py:185
  110.9 2.1 %collective-permute-done.2 = bf16[1,1,1,1,2,48,384]{6,5,4,3,2,1,0:T(8,128)(2,1)S(1)} collective-permute-done((bf16[1,1,1,1,2,48,384]{6,5,4,3,2,1,0:T(8,128)(2,1)S(1)}, bf16[1,1,1,1,2,48,384]{6,5,4,3,2,1,0:T(8,128)(2,1)S(1)}, u32[]{:S(2)}, u32[]{:S(2)}) %collective-permute-start.2) | collective-permute-done | bytes 73760 | tf_op jit(solution)/shard_map/ppermute | solution.py:185
  113.0 2.4 %collective-permute-start.3 = (bf16[1,1,1,1,1,48,384]{6,5,4,3,2,1,0:T(8,128)(2,1)S(1)}, bf16[1,1,1,1,1,48,384]{6,5,4,3,2,1,0:T(8,128)(2,1)S(1)}, u32[]{:S(2)}, u32[]{:S(2)}) collective-permute-start(bf16[1,1,1,1,1,48,384]{6,5,4,3,2,1,0:T(8,128)(2,1)S(1)} %dynamic-slice_convert_fusion.11), channel_id=1, source_target_pairs={{0,128},{16,144},{32,160},{48,176},{64,192},{80,208},{96,224},{112... | collective-permute-start | bytes 110600 | tf_op jit(solution)/shard_map/ppermute | solution.py:185
  117.6 2.7 %collective-permute-done.7 = bf16[1,1,1,1,1,48,384]{6,5,4,3,2,1,0:T(8,128)(2,1)S(1)} collective-permute-done((bf16[1,1,1,1,1,48,384]{6,5,4,3,2,1,0:T(8,128)(2,1)S(1)}, bf16[1,1,1,1,1,48,384]{6,5,4,3,2,1,0:T(8,128)(2,1)S(1)}, u32[]{:S(2)}, u32[]{:S(2)}) %collective-permute-start.7) | collective-permute-done | bytes 36896 | tf_op jit(solution)/shard_map/ppermute | solution.py:185
  120.9 17.8 %all_to_all.15 = bf16[16,48,240]{2,1,0:T(8,128)(2,1)S(1)} all-to-all(bf16[16,48,240]{2,1,0:T(8,128)(2,1)S(1)} %copy.13), channel_id=1, replica_groups=mesh['dp'=16,'seq'=16] {'seq'}, dimensions={0} | all-to-all | bytes 737280 | tf_op jit(solution)/shard_map/all_to_all | solution.py:214
  138.9 20.0 %all_to_all.16.pieces_ref = bf16[16,48,240]{2,1,0:T(8,128)(2,1)} all-to-all(bf16[16,48,240]{2,1,0:T(8,128)(2,1)S(1)} %broadcast_in_dim.2), channel_id=1, replica_groups=mesh['dp'=16,'seq'=16] {'dp'}, dimensions={0} | all-to-all | bytes 737280 | tf_op jit(solution)/shard_map/all_to_all | solution.py:214
  158.9 1.9 %join.1 = (bf16[48,768]{1,0:T(8,128)(2,1)}, bf16[48,1536]{1,0:T(8,128)(2,1)}, bf16[96,768]{1,0:T(8,128)(2,1)}) custom-call(bf16[16,48,240]{2,1,0:T(8,128)(2,1)} %all_to_all.16.pieces_ref), custom_call_target="tpu_custom_call" | custom-call | tf_op jit(solution)/shard_map/join/pallas_call | solution.py:171
  (77 shorter events, 26.0 us)
Async XLA Ops:
  5.7 10.3 %copy-start.6 = (bf16[16,64,64]{2,1,0:T(8,128)(2,1)S(1)}, bf16[16,64,64]{2,1,0:T(8,128)(2,1)}, u32[]{:S(2)}) copy-start(bf16[16,64,64]{2,1,0:T(8,128)(2,1)} %param.13) | copy-start | bytes 393220
  5.7 80.9 %all-to-all-start = ((bf16[16,2,64,768]{3,2,1,0:T(8,128)(2,1)}), bf16[16,2,64,768]{3,2,1,0:T(8,128)(2,1)S(1)}, u32[]{:S(2)}, u32[]{:S(2)}) async-start(bf16[16,2,64,768]{3,2,1,0:T(8,128)(2,1)} %bitcast.24), calls=%async_computation | async-start | bytes 6291456 | tf_op jit(solution)/shard_map/all_to_all | solution.py:214
  37.1 3.5 %copy-start.4 = (bf16[768,1536]{1,0:T(8,128)(2,1)S(1)}, bf16[768,1536]{1,0:T(8,128)(2,1)}, u32[]{:S(2)}) copy-start(bf16[768,1536]{1,0:T(8,128)(2,1)} %get-tuple-element.10) | copy-start | bytes 7077892
  39.6 3.8 %collective-permute-start.8 = (bf16[2,1,2,2,2,48,768]{6,5,4,3,2,1,0:T(8,128)(2,1)}, bf16[2,1,2,2,2,48,768]{6,5,4,3,2,1,0:T(8,128)(2,1)}, u32[]{:S(2)}, u32[]{:S(2)}) collective-permute-start(bf16[2,1,2,2,2,48,768]{6,5,4,3,2,1,0:T(8,128)(2,1)} %constant_dynamic-slice_fusion.1), channel_id=1, source_target_pairs={{0,16},{16,0},{32,48},{48,32},{64,80},{80,64},{96,112},{112,96},{1... | collective-permute-start | bytes 3538952 | tf_op jit(solution)/shard_map/ppermute | solution.py:185
  41.7 6.0 %collective-permute-start.12 = (bf16[1,1,2,2,2,48,1536]{6,5,4,3,2,1,0:T(8,128)(2,1)}, bf16[1,1,2,2,2,48,1536]{6,5,4,3,2,1,0:T(8,128)(2,1)}, u32[]{:S(2)}, u32[]{:S(2)}) collective-permute-start(bf16[1,1,2,2,2,48,1536]{6,5,4,3,2,1,0:T(8,128)(2,1)} %constant_dynamic-slice_fusion), channel_id=1, source_target_pairs={{0,16},{16,0},{32,48},{48,32},{64,80},{80,64},{96,112},{112,96},{1... | collective-permute-start | bytes 3538952 | tf_op jit(solution)/shard_map/ppermute | solution.py:185
  43.4 4.3 %copy-start.5 = (bf16[768,1536]{1,0:T(8,128)(2,1)S(1)}, bf16[768,1536]{1,0:T(8,128)(2,1)}, u32[]{:S(2)}) copy-start(bf16[768,1536]{1,0:T(8,128)(2,1)} %get-tuple-element.10) | copy-start | bytes 7077892
  45.5 3.8 %copy-start.1 = (f32[2,1,2,2,2,48,768]{6,5,4,3,2,1,0:T(8,128)}, f32[2,1,2,2,2,48,768]{6,5,4,3,2,1,0:T(8,128)S(1)}, u32[]{:S(2)}) copy-start(f32[2,1,2,2,2,48,768]{6,5,4,3,2,1,0:T(8,128)S(1)} %convert_add_fusion.1) | copy-start | bytes 7077892
  46.5 14.9 %collective-permute-start.9 = (bf16[2,1,1,2,2,48,768]{6,5,4,3,2,1,0:T(8,128)(2,1)}, bf16[2,1,1,2,2,48,768]{6,5,4,3,2,1,0:T(8,128)(2,1)}, u32[]{:S(2)}, u32[]{:S(2)}) collective-permute-start(bf16[2,1,1,2,2,48,768]{6,5,4,3,2,1,0:T(8,128)(2,1)} %dynamic-slice_convert_fusion.1), channel_id=1, source_target_pairs={{0,32},{16,48},{32,0},{48,16},{64,96},{80,112},{96,64},{112,80},{1... | collective-permute-start | bytes 1769480 | tf_op jit(solution)/shard_map/ppermute | solution.py:185
  49.3 1.6 %copy-start.2 = (f32[1,1,2,2,2,48,1536]{6,5,4,3,2,1,0:T(8,128)}, f32[1,1,2,2,2,48,1536]{6,5,4,3,2,1,0:T(8,128)S(1)}, u32[]{:S(2)}) copy-start(f32[1,1,2,2,2,48,1536]{6,5,4,3,2,1,0:T(8,128)S(1)} %convert_add_fusion) | copy-start | bytes 7077892
  50.9 15.7 %collective-permute-start.13 = (bf16[1,1,2,1,2,48,1536]{6,5,4,3,2,1,0:T(8,128)(2,1)}, bf16[1,1,2,1,2,48,1536]{6,5,4,3,2,1,0:T(8,128)(2,1)}, u32[]{:S(2)}, u32[]{:S(2)}) collective-permute-start(bf16[1,1,2,1,2,48,1536]{6,5,4,3,2,1,0:T(8,128)(2,1)} %dynamic-slice_convert_fusion), channel_id=1, source_target_pairs={{0,96},{16,112},{32,64},{48,80},{64,32},{80,48},{96,0},{112,16},{1... | collective-permute-start | bytes 1769480 | tf_op jit(solution)/shard_map/ppermute | solution.py:185
  52.7 13.9 %copy-start.3 = (f32[1,1,2,2,2,48,1536]{6,5,4,3,2,1,0:T(8,128)S(1)}, f32[1,1,2,2,2,48,1536]{6,5,4,3,2,1,0:T(8,128)}, u32[]{:S(2)}) copy-start(f32[1,1,2,2,2,48,1536]{6,5,4,3,2,1,0:T(8,128)} %copy-done.2) | copy-start | bytes 7077892
  63.0 10.0 %collective-permute-start.10 = (bf16[2,1,1,1,2,48,768]{6,5,4,3,2,1,0:T(8,128)(2,1)S(1)}, bf16[2,1,1,1,2,48,768]{6,5,4,3,2,1,0:T(8,128)(2,1)S(1)}, u32[]{:S(2)}, u32[]{:S(2)}) collective-permute-start(bf16[2,1,1,1,2,48,768]{6,5,4,3,2,1,0:T(8,128)(2,1)S(1)} %dynamic-slice_convert_fusion.3), channel_id=1, source_target_pairs={{0,96},{16,112},{32,64},{48,80},{64,32},{80,48},{96,0},{112,16},{1... | collective-permute-start | bytes 884744 | tf_op jit(solution)/shard_map/ppermute | solution.py:185
  67.9 7.9 %collective-permute-start.14 = (bf16[1,1,1,1,2,48,1536]{6,5,4,3,2,1,0:T(8,128)(2,1)S(1)}, bf16[1,1,1,1,2,48,1536]{6,5,4,3,2,1,0:T(8,128)(2,1)S(1)}, u32[]{:S(2)}, u32[]{:S(2)}) collective-permute-start(bf16[1,1,1,1,2,48,1536]{6,5,4,3,2,1,0:T(8,128)(2,1)S(1)} %dynamic-slice_convert_fusion.2), channel_id=1, source_target_pairs={{0,32},{16,48},{32,0},{48,16},{64,96},{80,112},{96,64},{112,80},{1... | collective-permute-start | bytes 884744 | tf_op jit(solution)/shard_map/ppermute | solution.py:185
  73.1 6.2 %collective-permute-start.11 = (bf16[2,1,1,1,1,48,768]{6,5,4,3,2,1,0:T(8,128)(2,1)S(1)}, bf16[2,1,1,1,1,48,768]{6,5,4,3,2,1,0:T(8,128)(2,1)S(1)}, u32[]{:S(2)}, u32[]{:S(2)}) collective-permute-start(bf16[2,1,1,1,1,48,768]{6,5,4,3,2,1,0:T(8,128)(2,1)S(1)} %dynamic-slice_convert_fusion.5), channel_id=1, source_target_pairs={{0,128},{16,144},{32,160},{48,176},{64,192},{80,208},{96,224},{112... | collective-permute-start | bytes 442376 | tf_op jit(solution)/shard_map/ppermute | solution.py:185
  75.9 8.9 %collective-permute-start.15 = (bf16[1,1,1,1,1,48,1536]{6,5,4,3,2,1,0:T(8,128)(2,1)S(1)}, bf16[1,1,1,1,1,48,1536]{6,5,4,3,2,1,0:T(8,128)(2,1)S(1)}, u32[]{:S(2)}, u32[]{:S(2)}) collective-permute-start(bf16[1,1,1,1,1,48,1536]{6,5,4,3,2,1,0:T(8,128)(2,1)S(1)} %dynamic-slice_convert_fusion.4), channel_id=1, source_target_pairs={{0,128},{16,144},{32,160},{48,176},{64,192},{80,208},{96,224},{112... | collective-permute-start | bytes 442376 | tf_op jit(solution)/shard_map/ppermute | solution.py:185
  86.6 1.6 %copy-start = (bf16[16,2,64,768]{3,2,1,0:T(8,128)(2,1)}, bf16[16,2,64,768]{3,2,1,0:T(8,128)(2,1)S(1)}, u32[]{:S(2)}) copy-start(bf16[16,2,64,768]{3,2,1,0:T(8,128)(2,1)S(1)} %all-to-all-done.mix_ref.weighted_ref) | copy-start | bytes 9437188
  100.1 3.0 %collective-permute-start = (bf16[1,1,2,2,2,48,384]{6,5,4,3,2,1,0:T(8,128)(2,1)S(1)}, bf16[1,1,2,2,2,48,384]{6,5,4,3,2,1,0:T(8,128)(2,1)S(1)}, u32[]{:S(2)}, u32[]{:S(2)}) collective-permute-start(bf16[1,1,2,2,2,48,384]{6,5,4,3,2,1,0:T(8,128)(2,1)S(1)} %constant_dynamic-slice_fusion.3), channel_id=1, source_target_pairs={{0,16},{16,0},{32,48},{48,32},{64,80},{80,64},{96,112},{112,96},{1... | collective-permute-start | bytes 884744 | tf_op jit(solution)/shard_map/ppermute | solution.py:185
  102.6 1.7 %collective-permute-start.4 = (bf16[1,1,2,2,2,48,384]{6,5,4,3,2,1,0:T(8,128)(2,1)S(1)}, bf16[1,1,2,2,2,48,384]{6,5,4,3,2,1,0:T(8,128)(2,1)S(1)}, u32[]{:S(2)}, u32[]{:S(2)}) collective-permute-start(bf16[1,1,2,2,2,48,384]{6,5,4,3,2,1,0:T(8,128)(2,1)S(1)} %constant_dynamic-slice_fusion.2), channel_id=1, source_target_pairs={{0,16},{16,0},{32,48},{48,32},{64,80},{80,64},{96,112},{112,96},{1... | collective-permute-start | bytes 884744 | tf_op jit(solution)/shard_map/ppermute | solution.py:185
  103.3 5.1 %collective-permute-start.1 = (bf16[1,1,1,2,2,48,384]{6,5,4,3,2,1,0:T(8,128)(2,1)S(1)}, bf16[1,1,1,2,2,48,384]{6,5,4,3,2,1,0:T(8,128)(2,1)S(1)}, u32[]{:S(2)}, u32[]{:S(2)}) collective-permute-start(bf16[1,1,1,2,2,48,384]{6,5,4,3,2,1,0:T(8,128)(2,1)S(1)} %dynamic-slice_convert_fusion.7), channel_id=1, source_target_pairs={{0,32},{16,48},{32,0},{48,16},{64,96},{80,112},{96,64},{112,80},{1... | collective-permute-start | bytes 442376 | tf_op jit(solution)/shard_map/ppermute | solution.py:185
  104.4 6.3 %collective-permute-start.5 = (bf16[1,1,2,1,2,48,384]{6,5,4,3,2,1,0:T(8,128)(2,1)S(1)}, bf16[1,1,2,1,2,48,384]{6,5,4,3,2,1,0:T(8,128)(2,1)S(1)}, u32[]{:S(2)}, u32[]{:S(2)}) collective-permute-start(bf16[1,1,2,1,2,48,384]{6,5,4,3,2,1,0:T(8,128)(2,1)S(1)} %dynamic-slice_convert_fusion.6), channel_id=1, source_target_pairs={{0,96},{16,112},{32,64},{48,80},{64,32},{80,48},{96,0},{112,16},{1... | collective-permute-start | bytes 442376 | tf_op jit(solution)/shard_map/ppermute | solution.py:185
  108.5 4.5 %collective-permute-start.2 = (bf16[1,1,1,1,2,48,384]{6,5,4,3,2,1,0:T(8,128)(2,1)S(1)}, bf16[1,1,1,1,2,48,384]{6,5,4,3,2,1,0:T(8,128)(2,1)S(1)}, u32[]{:S(2)}, u32[]{:S(2)}) collective-permute-start(bf16[1,1,1,1,2,48,384]{6,5,4,3,2,1,0:T(8,128)(2,1)S(1)} %dynamic-slice_convert_fusion.9), channel_id=1, source_target_pairs={{0,96},{16,112},{32,64},{48,80},{64,32},{80,48},{96,0},{112,16},{1... | collective-permute-start | bytes 221192 | tf_op jit(solution)/shard_map/ppermute | solution.py:185
  110.8 4.6 %collective-permute-start.6 = (bf16[1,1,1,1,2,48,384]{6,5,4,3,2,1,0:T(8,128)(2,1)S(1)}, bf16[1,1,1,1,2,48,384]{6,5,4,3,2,1,0:T(8,128)(2,1)S(1)}, u32[]{:S(2)}, u32[]{:S(2)}) collective-permute-start(bf16[1,1,1,1,2,48,384]{6,5,4,3,2,1,0:T(8,128)(2,1)S(1)} %dynamic-slice_convert_fusion.8), channel_id=1, source_target_pairs={{0,32},{16,48},{32,0},{48,16},{64,96},{80,112},{96,64},{112,80},{1... | collective-permute-start | bytes 221192 | tf_op jit(solution)/shard_map/ppermute | solution.py:185
  113.0 4.4 %collective-permute-start.3 = (bf16[1,1,1,1,1,48,384]{6,5,4,3,2,1,0:T(8,128)(2,1)S(1)}, bf16[1,1,1,1,1,48,384]{6,5,4,3,2,1,0:T(8,128)(2,1)S(1)}, u32[]{:S(2)}, u32[]{:S(2)}) collective-permute-start(bf16[1,1,1,1,1,48,384]{6,5,4,3,2,1,0:T(8,128)(2,1)S(1)} %dynamic-slice_convert_fusion.11), channel_id=1, source_target_pairs={{0,128},{16,144},{32,160},{48,176},{64,192},{80,208},{96,224},{112... | collective-permute-start | bytes 110600 | tf_op jit(solution)/shard_map/ppermute | solution.py:185
  115.5 4.7 %collective-permute-start.7 = (bf16[1,1,1,1,1,48,384]{6,5,4,3,2,1,0:T(8,128)(2,1)S(1)}, bf16[1,1,1,1,1,48,384]{6,5,4,3,2,1,0:T(8,128)(2,1)S(1)}, u32[]{:S(2)}, u32[]{:S(2)}) collective-permute-start(bf16[1,1,1,1,1,48,384]{6,5,4,3,2,1,0:T(8,128)(2,1)S(1)} %dynamic-slice_convert_fusion.10), channel_id=1, source_target_pairs={{0,128},{16,144},{32,160},{48,176},{64,192},{80,208},{96,224},{112... | collective-permute-start | bytes 110600 | tf_op jit(solution)/shard_map/ppermute | solution.py:185

commit v3 on v2

v3 whole, which is shorter than its diff:
```python
import jax
import jax.numpy as jnp
from jax import lax
from jax.experimental import pallas as pl
from jax.experimental.pallas import tpu as pltpu
from jax.sharding import PartitionSpec as P

BF16 = jnp.bfloat16
F32 = jnp.float32
VMEM_LIMIT = 56 * 1024 * 1024


def product(left, right, left_dim, right_dim):
    return lax.dot_general(
        left, right, (((left_dim,), (right_dim,)), ((), ())), preferred_element_type=F32
    )


def normalise(block):
    wide = block.astype(F32)
    return (wide * lax.rsqrt(jnp.mean(wide * wide, axis=-1, keepdims=True) + 1e-06)).astype(BF16)


def send_kernel(inputs_ref, cot_ref, first_ref, sent_ref):
    places, _, groups, tile, width = sent_ref.shape

    def part(block):
        return block.reshape(places, groups, -1, width)

    mixes, weights = [], []
    for a in range(inputs_ref.shape[1]):
        normed = normalise(inputs_ref[0, a])
        weights.append(part(cot_ref[0, a].astype(F32) * normed.astype(F32)))
        mixes.append(part(product(first_ref[a], normed, 1, 0)))
    for k, parts in enumerate((mixes, weights)):
        sent_ref[:, k] = jnp.concatenate(parts, axis=2).astype(BF16)


def build_sent(inputs, cotangent, first_blocks, places):
    _, rows, block, width = inputs.shape
    groups, step = 2, 2
    tile = step * block // places // groups
    whole = pl.BlockSpec((1, step, block, width), lambda a: (0, a, 0, 0))
    return pl.pallas_call(
        send_kernel,
        grid=(rows // step,),
        in_specs=[whole, whole, pl.BlockSpec((step, block, block), lambda a: (a, 0, 0))],
        out_specs=pl.BlockSpec((places, 2, groups, tile, width), lambda a: (0, 0, 0, a, 0)),
        out_shape=jax.ShapeDtypeStruct((places, 2, groups, tile * rows // step, width), BF16),
        compiler_params=pltpu.CompilerParams(vmem_limit_bytes=VMEM_LIMIT),
        name="send",
    )(inputs, cotangent, first_blocks)


def mlp_kernel(
    core_ref, inputs_ref, cot_ref, up_ref, down_ref,
    up_keep_ref, up_give_ref, down_keep_ref, down_give_ref, normed_ref, normed_t_ref,
):
    core, step, steps = core_ref[0], pl.program_id(0), pl.num_programs(0)

    @pl.when(step == 0)
    def _():
        normed = normalise(inputs_ref[...])
        normed_ref[...] = normed
        normed_t_ref[...] = normed.T

    field = product(normed_ref[...], up_ref[...], 1, 0)
    back = product(cot_ref[...], down_ref[...], 1, 1)
    scale, cubic = 0.7978845608028654, 0.044715
    square = field * field
    bend = jnp.tanh(scale * field * (1.0 + cubic * square))
    upper = 0.5 + 0.5 * bend
    hidden = (field * upper).astype(BF16)
    slope = upper + (0.5 * scale) * field * (1.0 - bend * bend) * (1.0 + 3.0 * cubic * square)
    up_slope = (back * slope).astype(BF16)
    up_grad = product(normed_t_ref[...], up_slope, 1, 0).astype(BF16)

    @pl.when(step < steps // 2)
    def _():
        up_give_ref[...] = up_grad

    @pl.when(step >= steps // 2)
    def _():
        up_keep_ref[...] = up_grad

    half = down_keep_ref.shape[1]
    hidden_t = hidden.T
    keep = pl.ds(pl.multiple_of(core * half, half), half)
    give = pl.ds(pl.multiple_of((1 - core) * half, half), half)
    down_keep_ref[...] = product(hidden_t, cot_ref[:, keep], 1, 0).astype(BF16)
    down_give_ref[...] = product(hidden_t, cot_ref[:, give], 1, 0).astype(BF16)


def mlp_grads(core, inputs, cotangent, up_weight, down_weight):
    positions, width = inputs.shape
    units = up_weight.shape[1]
    block = 256
    steps = units // block
    half = steps // 2

    def unit(f, c):
        return jnp.where(f < half, (1 - c[0]) * half + f, c[0] * half + f - half)

    whole = pl.BlockSpec((positions, width), lambda f, c: (0, 0))
    down_half = pl.BlockSpec((block, width // 2), lambda f, c: (unit(f, c), 0))
    return pl.pallas_call(
        mlp_kernel,
        grid_spec=pltpu.PrefetchScalarGridSpec(
            num_scalar_prefetch=1,
            grid=(steps,),
            in_specs=[
                whole,
                whole,
                pl.BlockSpec((width, block), lambda f, c: (0, unit(f, c))),
                pl.BlockSpec((block, width), lambda f, c: (unit(f, c), 0)),
            ],
            out_specs=[
                pl.BlockSpec((width, block), lambda f, c: (0, jnp.maximum(f - half, 0))),
                pl.BlockSpec((width, block), lambda f, c: (0, jnp.minimum(f, half - 1))),
                down_half,
                down_half,
            ],
            scratch_shapes=[
                pltpu.VMEM((positions, width), BF16),
                pltpu.VMEM((width, positions), BF16),
            ],
        ),
        out_shape=[jax.ShapeDtypeStruct((width, units // 2), BF16)] * 2
        + [jax.ShapeDtypeStruct((units, width // 2), BF16)] * 2,
        compiler_params=pltpu.CompilerParams(vmem_limit_bytes=VMEM_LIMIT),
        name="mlp",
    )(core, inputs, cotangent, up_weight, down_weight)


def spread_kernel(stacked_ref, out_ref):
    groups, positions, size = stacked_ref.shape
    blocks = positions // size
    take = lax.broadcasted_iota(jnp.int32, (size, positions), 1) // blocks
    spread = (take == lax.broadcasted_iota(jnp.int32, (size, positions), 0)).astype(BF16)
    row = lax.broadcasted_iota(jnp.int32, (positions, positions), 0)
    col = lax.broadcasted_iota(jnp.int32, (positions, positions), 1)
    same = row % blocks == col % blocks
    for k in range(groups):
        wide = product(stacked_ref[k], spread, 1, 0)
        out_ref[k] = jnp.where(same, wide, 0.0).astype(BF16)


def spread_second(second_blocks, groups):
    blocks, size, _ = second_blocks.shape
    positions = blocks // groups * size
    stacked = second_blocks.reshape(groups, -1, size, size).transpose(0, 2, 1, 3)
    return pl.pallas_call(
        spread_kernel,
        out_shape=jax.ShapeDtypeStruct((groups, positions, positions), BF16),
        compiler_params=pltpu.CompilerParams(vmem_limit_bytes=VMEM_LIMIT),
        name="spread",
    )(stacked.reshape(groups, positions, size))


def value_kernel(
    core_ref, mix_ref, weighted_ref, second_ref, weight_ref, keep_ref, give_ref, both_ref, both_t_ref
):
    groups, positions, _ = second_ref.shape
    step = pl.program_id(0)

    @pl.when(step == 0)
    def _():
        for k in range(groups):
            first_mix = mix_ref[:, 0, k].reshape(positions, -1)
            both = product(second_ref[k], first_mix, 1, 0).astype(BF16)
            rows = pl.ds(k * positions, positions)
            both_ref[rows] = both
            both_t_ref[:, rows] = both.T

    slopes = []
    for k in range(groups):
        mixed = product(both_ref[pl.ds(k * positions, positions)], weight_ref[...], 1, 0)
        sigmoid_part = 0.5 + 0.5 * jnp.tanh(0.5 * mixed)
        weighted = weighted_ref[:, 0, k].reshape(mixed.shape).astype(F32)
        slope = weighted * (sigmoid_part * (1.0 + mixed * (1.0 - sigmoid_part)))
        slopes.append(slope.astype(BF16))
    grad = product(both_t_ref[...], jnp.concatenate(slopes, axis=0), 1, 0).astype(BF16)

    @pl.when(step == 0)
    def _():
        give_ref[...] = grad

    @pl.when(step == 1)
    def _():
        keep_ref[...] = grad


def value_grad(core, came, second, value_weight):
    places, _, groups, tile, width = came.shape
    positions = places * groups * tile
    half = width // 2

    def part(e, c):
        return jnp.where(e == 0, 1 - c[0], c[0])

    whole = pl.BlockSpec((width, half), lambda e, c: (0, 0))
    return pl.pallas_call(
        value_kernel,
        grid_spec=pltpu.PrefetchScalarGridSpec(
            num_scalar_prefetch=1,
            grid=(2,),
            in_specs=[
                pl.BlockSpec((places, 1, groups, tile, width), lambda e, c: (0, 0, 0, 0, 0)),
                pl.BlockSpec((places, 1, groups, tile, half), lambda e, c: (0, 1, 0, 0, part(e, c))),
                pl.BlockSpec(second.shape, lambda e, c: (0, 0, 0)),
                pl.BlockSpec((width, half), lambda e, c: (0, part(e, c))),
            ],
            out_specs=[whole, whole],
            scratch_shapes=[
                pltpu.VMEM((positions, width), BF16),
                pltpu.VMEM((width, positions), BF16),
            ],
        ),
        out_shape=[jax.ShapeDtypeStruct((width, half), BF16)] * 2,
        compiler_params=pltpu.CompilerParams(vmem_limit_bytes=VMEM_LIMIT),
        name="value",
    )(core, came, came, second, value_weight)


def join_kernel(blocks_ref, value_ref, up_ref, down_ref):
    count, _, half = blocks_ref.shape
    share = value_ref.shape[0]
    cut = share // 2
    for core in range(2):
        lanes = slice(core * half, (core + 1) * half)
        total = blocks_ref[core, cut:].astype(F32)
        for i in range(2 + core, count, 2):
            total = total + blocks_ref[i, cut:].astype(F32)
        value_ref[:, lanes] = total.astype(BF16)
        for x1 in range(2):
            for x0 in range(2):
                i = x1 * 4 + x0 * 2 + core
                f, g = x0 ^ x1, x1
                column = (core * 2 + f) * half
                up_ref[g * cut : (g + 1) * cut, column : column + half] = blocks_ref[i, :cut]
                row = f * share + g * cut
                down_ref[row : row + cut, lanes] = blocks_ref[8 + i, :cut]


def join(blocks):
    _, rows, half = blocks.shape
    share = rows * 2 // 3
    return pl.pallas_call(
        join_kernel,
        out_shape=[
            jax.ShapeDtypeStruct((share, 2 * half), BF16),
            jax.ShapeDtypeStruct((share, 4 * half), BF16),
            jax.ShapeDtypeStruct((2 * share, 2 * half), BF16),
        ],
        compiler_params=pltpu.CompilerParams(vmem_limit_bytes=VMEM_LIMIT),
        name="join",
    )(blocks)


def swap(block, flip):
    return lax.ppermute(block, "dp", [(i, i ^ flip) for i in range(16)])


def add_swapped(keep, give, flip):
    return keep.astype(F32) + swap(give, flip).astype(F32)


def halve(total, axis, bit, flip):
    keep = lax.dynamic_slice_in_dim(total, bit, 1, axis)
    give = lax.dynamic_slice_in_dim(total, 1 - bit, 1, axis).astype(BF16)
    return add_swapped(keep, give, flip)


def exchange(block, axis):
    return lax.all_to_all(block, axis, split_axis=0, concat_axis=0, tiled=True)


def local(inputs, cotangent, value_weight, up_weight, down_weight, first_blocks, second_blocks):
    width = inputs.shape[3]
    places = lax.axis_size("seq")
    share, half = width // places, width // 2
    i = lax.axis_index("dp")
    core, x0, x1, y_hi = i & 1, (i >> 1) & 1, (i >> 2) & 1, i >> 3
    core_arg = jnp.full((1,), core, jnp.int32)

    came = exchange(build_sent(inputs, cotangent, first_blocks, places), "seq")

    flat = inputs.reshape(-1, width)
    grads = mlp_grads(core_arg, flat, cotangent.reshape(-1, width), up_weight, down_weight)
    up_keep, up_give, down_keep, down_give = grads
    second = spread_second(second_blocks, 2)

    up = add_swapped(up_keep, up_give, 1).reshape(places, 2, share // 2, 2, half)
    down = add_swapped(down_keep, down_give, 1).reshape(places, 2, 2, share // 2, half)
    up = halve(halve(up, 3, x0 ^ x1, 2), 1, x1, 6)
    down = halve(halve(down, 2, x1, 6), 1, x0 ^ x1, 2)
    up = up.reshape(places, share // 2, half)
    down = down.reshape(places, share // 2, half)
    keep = jnp.where(y_hi == 0, up, down)
    give = jnp.where(y_hi == 0, down, up).astype(BF16)
    mlp_part = add_swapped(keep, give, 8).astype(BF16)

    value_keep, value_give = value_grad(core_arg, came, second, value_weight)
    value_part = add_swapped(value_keep, value_give, 1).astype(BF16).reshape(places, share, half)

    part = exchange(jnp.concatenate([mlp_part, value_part], axis=1), "seq")
    total_tokens = (
        inputs.shape[0] * inputs.shape[1] * inputs.shape[2] * lax.axis_size("dp") * places
    )
    factor = float(total_tokens) ** (-0.5)
    part = (jnp.sum(part.astype(F32), axis=0) * factor).astype(BF16)
    return tuple(join(exchange(jnp.broadcast_to(part[None], (16,) + part.shape), "dp")))


def solution(mesh):
    placed = (
        P("dp", "seq", None, None),
        P("dp", "seq", None, None),
        P(),
        P(),
        P(),
        P("seq", None, None),
        P("seq", None, None),
    )
    return jax.shard_map(
        local,
        mesh=mesh,
        in_specs=placed,
        out_specs=(P("seq", None), P("seq", None), P("seq", None)),
        check_vma=False,
    )
```

time: 161 us -> 167 us (1.037)
  blocking collectives: 37.8 us -> 54.4 us
  starting transfers between devices: 32.7 us -> 20.1 us
  waiting for transfers between devices: 32.8 us -> 22.2 us
  local copies, waits for them, and re-layouts: 11.4 us -> 17.9 us
  Pallas kernels: 37.6 us -> 40.8 us
  other arithmetic: 7.34 us -> 9.81 us
    all_to_all x2, blocking collectives: 37.8 us -> 54.4 us  [exchange(): return lax.all_to_all(block, axis, split_axis=0, concat_axis=0, tiled=True)]
    ppermute x16 -> x8, waiting for transfers between devices: 31 us -> 18.2 us  [swap(): return lax.ppermute(block, 'dp', [(i, i ^ flip) for i in range(16)])]
    ppermute x16 -> x8, starting transfers between devices: 22.5 us -> 10 us  [swap(): return lax.ppermute(block, 'dp', [(i, i ^ flip) for i in range(16)])]
    reshape x0 -> x2, local copies, waits for them, and re-layouts: none -> 5.73 us  [the longest x1 3.88 us: local(): add_swapped(up_keep, up_give, 1).reshape(places, 2, share // 2, 2, half)]
    pallas_call x5, Pallas kernels: 37.6 us -> 40.8 us  [the longest x1 24.2 us: mlp_grads(): pl.pallas_call(mlp_kernel, grid_spec=pltpu.PrefetchScalarGridSpec(num_sca...]
    convert_element_type x2 -> x4, other arithmetic: 0.04 us -> 2.35 us  [the longest x1 1.11 us: local(): mlp_part = add_swapped(keep, give, 8).astype(BF16)]
    unnamed x14 -> x20, local copies, waits for them, and re-layouts: 2.28 us -> 4.55 us
    all_to_all x1, waiting for transfers between devices: 1.75 us -> 3.99 us  [exchange(): return lax.all_to_all(block, axis, split_axis=0, concat_axis=0, tiled=True)]
  transfers between devices with their start and end apart: 17 -> 9, of which waited for: 12 -> 4; matrix products, arithmetic and copies ran while one was open for 9% -> 15% of each run, Pallas kernels for 13% -> 21%
where the time goes in v3:
time: 167 us; the launch traced here: 166 us
  blocking collectives  54.4 us (33%)
  Pallas kernels  40.8 us (24%)
  waiting for transfers between devices  22.2 us (13%)
  starting transfers between devices  20.1 us (12%)
  local copies, waits for them, and re-layouts  17.9 us (11%)
  other arithmetic  9.81 us (6%)
    all_to_all x2, blocking collectives, exchange(): return lax.all_to_all(block, axis, split_axis=0, concat_axis=0, tiled=True)  54.4 us
    pallas_call x1, Pallas kernels, mlp_grads(): pl.pallas_call(mlp_kernel, grid_spec=pltpu.PrefetchScalarGridSpec(num_sca...  24.2 us
    ppermute x8, waiting for transfers between devices, swap(): return lax.ppermute(block, 'dp', [(i, i ^ flip) for i in range(16)])  18.2 us
    all_to_all x1, starting transfers between devices, exchange(): return lax.all_to_all(block, axis, split_axis=0, concat_axis=0, tiled=True)  10.1 us
    ppermute x8, starting transfers between devices, swap(): return lax.ppermute(block, 'dp', [(i, i ^ flip) for i in range(16)])  10 us
    pallas_call x1, Pallas kernels, value_grad(): pl.pallas_call(value_kernel, grid_spec=pltpu.PrefetchScalarGridSpec(num_s...  8.35 us
    add x4, other arithmetic, add_swapped(): return keep.astype(F32) + swap(give, flip).astype(F32)  7.24 us
    unnamed x20, local copies, waits for them, and re-layouts  4.55 us
  transfers between devices with their start and end apart: 9, of which 4 were waited for; matrix products, arithmetic and copies ran while one was open for 15% of the time, Pallas kernels for 21%

profile of v3, /device:TPU:1, one launch (start us, length us, event | category | flops | bytes accessed | tf_op | source)
XLA Modules:
  0.0 166.0 jit_solution(12895482608637354732)
XLA Ops:
  0.6 4.0 %send.1 = bf16[16,2,2,32,768]{4,3,2,1,0:T(8,128)(2,1)} custom-call(bf16[1,4,256,768]{3,2,1,0:T(8,128)(2,1)} %inputs_ref.1, bf16[1,4,256,768]{3,2,1,0:T(8,128)(2,1)} %cot_ref.1, bf16[4,256,256]{2,1,0:T(8,128)(2,1)} %first_ref.1), custom_call_target="tpu_custom_call" | custom-call | tf_op jit(solution)/shard_map/send/pallas_call | solution.py:44
  4.6 10.1 %all-to-all-start = ((bf16[16,2,2,32,768]{4,3,2,1,0:T(8,128)(2,1)}), bf16[16,2,2,32,768]{4,3,2,1,0:T(8,128)(2,1)S(1)}, u32[]{:S(2)}, u32[]{:S(2)}) async-start(bf16[16,2,2,32,768]{4,3,2,1,0:T(8,128)(2,1)} %send.1), calls=%async_computation | async-start | bytes 6291456 | tf_op jit(solution)/shard_map/all_to_all | solution.py:275
  14.8 24.2 %mlp.1 = (bf16[768,768]{1,0:T(8,128)(2,1)}, bf16[768,768]{1,0:T(8,128)(2,1)}, bf16[1536,384]{1,0:T(8,128)(2,1)}, bf16[1536,384]{1,0:T(8,128)(2,1)}) custom-call(s32[1]{0:T(128)} %bitcast.core_ref, bf16[1024,768]{1,0:T(8,128)(2,1)} %bitcast.25, bf16[1024,768]{1,0:T(8,128)(2,1)} %bitcast.26, bf16[768,1536]{1,0:T(8,128)(2,1)} %up_ref.1, bf16[1536,768]{1,0:T(8,128)(2,1)} %down_ref.1), custom_call_target="tpu_custom_call" | custom-call | tf_op jit(solution)/shard_map/mlp/pallas_call | solution.py:106
  40.1 2.7 %collective-permute-done.3 = bf16[1536,384]{1,0:T(8,128)(2,1)} collective-permute-done((bf16[1536,384]{1,0:T(8,128)(2,1)}, bf16[1536,384]{1,0:T(8,128)(2,1)}, u32[]{:S(2)}, u32[]{:S(2)}) %collective-permute-start.3) | collective-permute-done | bytes 1179680 | tf_op jit(solution)/shard_map/ppermute | solution.py:261
  42.8 1.9 %convert_add_fusion = f32[1536,384]{1,0:T(8,128)S(1)} fusion(bf16[1536,384]{1,0:T(8,128)(2,1)} %collective-permute-done.3, bf16[1536,384]{1,0:T(8,128)(2,1)} %get-tuple-element.11), kind=kLoop, calls=%fused_computation | loop fusion | flops 1769472 | bytes 4718592 | tf_op jit(solution)/shard_map/add | solution.py:265
  46.3 2.5 %collective-permute-start.4 = (bf16[16,2,1,24,384]{4,3,0,2,1:T(8,128)(2,1)}, bf16[16,2,1,24,384]{4,3,0,2,1:T(8,128)(2,1)}, u32[]{:S(2)}, u32[]{:S(2)}) collective-permute-start(bf16[16,2,1,24,384]{4,3,0,2,1:T(8,128)(2,1)} %copy.24), channel_id=1, source_target_pairs={{0,96},{16,112},{32,64},{48,80},{64,32},{80,48},{96,0},{112,16},{1... | collective-permute-start | bytes 1769480 | tf_op jit(solution)/shard_map/ppermute | solution.py:261
  48.8 3.0 %convert_add_fusion.1 = f32[768,768]{1,0:T(8,128)} fusion(bf16[768,768]{1,0:T(8,128)(2,1)} %collective-permute-done, bf16[768,768]{1,0:T(8,128)(2,1)S(1)} %copy-done.7), kind=kLoop, calls=%fused_computation.1 | loop fusion | flops 1769472 | bytes 4718592 | tf_op jit(solution)/shard_map/add | solution.py:265
  51.8 3.9 %reshape.39 = f32[16,2,24,2,384]{4,3,2,1,0:T(2,128)} reshape(f32[768,768]{1,0:T(8,128)} %convert_add_fusion.1) | data formatting | bytes 4718592 | tf_op jit(solution)/shard_map/reshape | solution.py:293
  55.7 2.7 %constant_dynamic-slice_fusion.2 = bf16[16,2,24,1,384]{4,3,2,1,0:T(2,128)(2,1)S(1)} fusion(f32[16,2,24,2,384]{4,3,2,1,0:T(2,128)} %reshape.39, s32[]{:T(128)S(6)} %select_n.30), kind=kLoop, calls=%fused_computation.22 | loop fusion | bytes 1179652 | tf_op jit(solution)/shard_map/dynamic_slice | solution.py:270
  59.4 3.0 %constant_dynamic-slice_fusion.3 = f32[16,2,24,1,384]{4,3,2,1,0:T(1,128)S(1)} fusion(f32[16,2,24,2,384]{4,3,2,1,0:T(2,128)} %reshape.39, s32[]{:T(128)S(6)} %select_n.29), kind=kLoop, calls=%fused_computation.23 | loop fusion | bytes 2359300 | tf_op jit(solution)/shard_map/dynamic_slice | solution.py:269
  62.5 1.2 copy_add_fusion
  64.5 1.5 collective-permute-start.5
  66.0 8.0 %collective-permute-done.1 = bf16[16,2,24,1,384]{4,2,0,3,1:T(8,128)(2,1)} collective-permute-done((bf16[16,2,24,1,384]{4,2,0,3,1:T(8,128)(2,1)}, bf16[16,2,24,1,384]{4,2,0,3,1:T(8,128)(2,1)}, u32[]{:S(2)}, u32[]{:S(2)}) %collective-permute-start.1) | collective-permute-done | bytes 589856 | tf_op jit(solution)/shard_map/ppermute | solution.py:261
  77.2 1.8 %copy.26 = bf16[2,8,64,64]{3,1,2,0:T(8,128)(2,1)} copy(bf16[2,8,64,64]{3,2,1,0:T(8,128)(2,1)} %bitcast.29) | data formatting | bytes 262144 | tf_op jit(solution)/shard_map/reshape | solution.py:151
  79.0 2.4 %spread.1.second_ref = bf16[2,512,512]{2,1,0:T(8,128)(2,1)} custom-call(bf16[2,512,64]{2,1,0:T(8,128)(2,1)} %bitcast.28), custom_call_target="tpu_custom_call" | custom-call | tf_op jit(solution)/shard_map/spread/pallas_call | solution.py:152
  81.4 4.0 %all-to-all-done.mix_ref.weighted_ref = bf16[16,2,2,32,768]{4,3,2,1,0:T(8,128)(2,1)S(1)} async-done(((bf16[16,2,2,32,768]{4,3,2,1,0:T(8,128)(2,1)}), bf16[16,2,2,32,768]{4,3,2,1,0:T(8,128)(2,1)S(1)}, u32[]{:S(2)}, u32[]{:S(2)}) %all-to-all-start) | async-done | bytes 3145760 | tf_op jit(solution)/shard_map/all_to_all | solution.py:275
  85.4 1.6 copy-done
  87.0 8.3 %value.1 = (bf16[768,384]{1,0:T(8,128)(2,1)}, bf16[768,384]{1,0:T(8,128)(2,1)}) custom-call(s32[1]{0:T(128)} %bitcast.core_ref, bf16[16,2,2,32,768]{4,3,2,1,0:T(8,128)(2,1)} %copy-done, bf16[16,2,2,32,768]{4,3,2,1,0:T(8,128)(2,1)} %copy-done, bf16[2,512,512]{2,1,0:T(8,128)(2,1)} %spread.1.second_ref, bf16[768,768]{1,0:T(8,128)(2,1)} %weight_ref.1), custom_call_target="tpu_custom_call" | custom-call | tf_op jit(solution)/shard_map/value/pallas_call | solution.py:202
  95.4 1.5 collective-permute-start.7
  97.9 2.7 %collective-permute-start.6 = (bf16[16,24,384]{2,1,0:T(8,128)(2,1)S(1)}, bf16[16,24,384]{2,1,0:T(8,128)(2,1)S(1)}, u32[]{:S(2)}, u32[]{:S(2)}) collective-permute-start(bf16[16,24,384]{2,1,0:T(8,128)(2,1)S(1)} %fusion.2), channel_id=1, source_target_pairs={{0,128},{16,144},{32,160},{48,176},{64,192},{80,208},{96,224},{112... | collective-permute-start | bytes 884744 | tf_op jit(solution)/shard_map/ppermute | solution.py:261
  100.6 7.5 %collective-permute-done.6 = bf16[16,24,384]{2,1,0:T(8,128)(2,1)S(1)} collective-permute-done((bf16[16,24,384]{2,1,0:T(8,128)(2,1)S(1)}, bf16[16,24,384]{2,1,0:T(8,128)(2,1)S(1)}, u32[]{:S(2)}, u32[]{:S(2)}) %collective-permute-start.6) | collective-permute-done | bytes 294944 | tf_op jit(solution)/shard_map/ppermute | solution.py:261
  109.5 30.2 %all_to_all.15 = bf16[16,72,384]{2,1,0:T(8,128)(2,1)S(1)} all-to-all(bf16[16,72,384]{2,1,0:T(8,128)(2,1)S(1)} %pad_maximum_fusion), channel_id=1, replica_groups=mesh['dp'=16,'seq'=16] {'seq'}, dimensions={0} | all-to-all | bytes 1769472 | tf_op jit(solution)/shard_map/all_to_all | solution.py:275
  139.9 24.2 %all_to_all.16.blocks_ref = bf16[16,72,384]{2,1,0:T(8,128)(2,1)} all-to-all(bf16[16,72,384]{2,1,0:T(8,128)(2,1)S(1)} %broadcast_in_dim.10), channel_id=1, replica_groups=mesh['dp'=16,'seq'=16] {'dp'}, dimensions={0} | all-to-all | bytes 1769472 | tf_op jit(solution)/shard_map/all_to_all | solution.py:275
  164.1 1.9 %join.1 = (bf16[48,768]{1,0:T(8,128)(2,1)}, bf16[48,1536]{1,0:T(8,128)(2,1)}, bf16[96,768]{1,0:T(8,128)(2,1)}) custom-call(bf16[16,72,384]{2,1,0:T(8,128)(2,1)} %all_to_all.16.blocks_ref), custom_call_target="tpu_custom_call" | custom-call | tf_op jit(solution)/shard_map/join/pallas_call | solution.py:248
  (39 shorter events, 10.4 us)
Async XLA Ops:
  4.6 80.7 %all-to-all-start = ((bf16[16,2,2,32,768]{4,3,2,1,0:T(8,128)(2,1)}), bf16[16,2,2,32,768]{4,3,2,1,0:T(8,128)(2,1)S(1)}, u32[]{:S(2)}, u32[]{:S(2)}) async-start(bf16[16,2,2,32,768]{4,3,2,1,0:T(8,128)(2,1)} %send.1), calls=%async_computation | async-start | bytes 6291456 | tf_op jit(solution)/shard_map/all_to_all | solution.py:275
  39.0 3.8 %collective-permute-start.3 = (bf16[1536,384]{1,0:T(8,128)(2,1)}, bf16[1536,384]{1,0:T(8,128)(2,1)}, u32[]{:S(2)}, u32[]{:S(2)}) collective-permute-start(bf16[1536,384]{1,0:T(8,128)(2,1)} %get-tuple-element.12), channel_id=1, source_target_pairs={{0,16},{16,0},{32,48},{48,32},{64,80},{80,64},{96,112},{112,96},{1... | collective-permute-start | bytes 3538952 | tf_op jit(solution)/shard_map/ppermute | solution.py:261
  40.0 8.8 %collective-permute-start = (bf16[768,768]{1,0:T(8,128)(2,1)}, bf16[768,768]{1,0:T(8,128)(2,1)}, u32[]{:S(2)}, u32[]{:S(2)}) collective-permute-start(bf16[768,768]{1,0:T(8,128)(2,1)} %get-tuple-element.10), channel_id=1, source_target_pairs={{0,16},{16,0},{32,48},{48,32},{64,80},{80,64},{96,112},{112,96},{1... | collective-permute-start | bytes 3538952 | tf_op jit(solution)/shard_map/ppermute | solution.py:261
  44.6 1.6 copy-start.1
  44.7 4.1 %copy-start.7 = (bf16[768,768]{1,0:T(8,128)(2,1)S(1)}, bf16[768,768]{1,0:T(8,128)(2,1)}, u32[]{:S(2)}) copy-start(bf16[768,768]{1,0:T(8,128)(2,1)} %get-tuple-element.9) | copy-start | bytes 3538948
  46.3 16.2 %collective-permute-start.4 = (bf16[16,2,1,24,384]{4,3,0,2,1:T(8,128)(2,1)}, bf16[16,2,1,24,384]{4,3,0,2,1:T(8,128)(2,1)}, u32[]{:S(2)}, u32[]{:S(2)}) collective-permute-start(bf16[16,2,1,24,384]{4,3,0,2,1:T(8,128)(2,1)} %copy.24), channel_id=1, source_target_pairs={{0,96},{16,112},{32,64},{48,80},{64,32},{80,48},{96,0},{112,16},{1... | collective-permute-start | bytes 1769480 | tf_op jit(solution)/shard_map/ppermute | solution.py:261
  59.4 14.5 %collective-permute-start.1 = (bf16[16,2,24,1,384]{4,2,0,3,1:T(8,128)(2,1)}, bf16[16,2,24,1,384]{4,2,0,3,1:T(8,128)(2,1)}, u32[]{:S(2)}, u32[]{:S(2)}) collective-permute-start(bf16[16,2,24,1,384]{4,2,0,3,1:T(8,128)(2,1)} %copy.25), channel_id=1, source_target_pairs={{0,32},{16,48},{32,0},{48,16},{64,96},{80,112},{96,64},{112,80},{1... | collective-permute-start | bytes 1769480 | tf_op jit(solution)/shard_map/ppermute | solution.py:261
  59.4 3.0 %copy-start.2 = (f32[1536,384]{1,0:T(8,128)S(1)}, f32[1536,384]{1,0:T(8,128)}, u32[]{:S(2)}) copy-start(f32[1536,384]{1,0:T(8,128)} %copy-done.1) | copy-start | bytes 7077892
  63.6 11.5 %copy-start.3 = (f32[16,2,1,24,384]{4,3,0,2,1:T(8,128)}, f32[16,2,1,24,384]{4,3,0,2,1:T(8,128)S(1)}, u32[]{:S(2)}) copy-start(f32[16,2,1,24,384]{4,3,0,2,1:T(8,128)S(1)} %copy_add_fusion) | copy-start | bytes 3538948
  64.5 32.3 %collective-permute-start.5 = (bf16[16,1,1,24,384]{4,3,0,2,1:T(8,128)(2,1)}, bf16[16,1,1,24,384]{4,3,0,2,1:T(8,128)(2,1)S(1)}, u32[]{:S(2)}, u32[]{:S(2)}) collective-permute-start(bf16[16,1,1,24,384]{4,3,0,2,1:T(8,128)(2,1)} %dynamic-slice_convert_fusion), channel_id=1, source_target_pairs={{0,32},{16,48},{32,0},{48,16},{64,96},{80,112},{96,64},{112,80},{1... | collective-permute-start | bytes 884744 | tf_op jit(solution)/shard_map/ppermute | solution.py:261
  75.1 1.2 copy-start.5
  76.3 20.5 %collective-permute-start.2 = (bf16[16,1,24,1,384]{4,2,0,3,1:T(8,128)(2,1)}, bf16[16,1,24,1,384]{4,2,0,3,1:T(8,128)(2,1)}, u32[]{:S(2)}, u32[]{:S(2)}) collective-permute-start(bf16[16,1,24,1,384]{4,2,0,3,1:T(8,128)(2,1)} %dynamic-slice_convert_fusion.1), channel_id=1, source_target_pairs={{0,96},{16,112},{32,64},{48,80},{64,32},{80,48},{96,0},{112,16},{1... | collective-permute-start | bytes 884744 | tf_op jit(solution)/shard_map/ppermute | solution.py:261
  85.4 1.6 copy-start
  87.0 9.8 %copy-start.4 = (f32[16,2,1,24,384]{4,3,0,2,1:T(8,128)S(1)}, f32[16,2,1,24,384]{4,3,0,2,1:T(8,128)}, u32[]{:S(2)}) copy-start(f32[16,2,1,24,384]{4,3,0,2,1:T(8,128)} %copy-done.3) | copy-start | bytes 3538948
  87.0 9.8 %copy-start.6 = (f32[16,2,24,1,384]{4,2,0,3,1:T(8,128)S(1)}, f32[16,2,24,1,384]{4,2,0,3,1:T(8,128)}, u32[]{:S(2)}) copy-start(f32[16,2,24,1,384]{4,2,0,3,1:T(8,128)} %copy-done.5) | copy-start | bytes 3538948
  95.4 13.9 %collective-permute-start.7 = (bf16[768,384]{1,0:T(8,128)(2,1)}, bf16[768,384]{1,0:T(8,128)(2,1)S(1)}, u32[]{:S(2)}, u32[]{:S(2)}) collective-permute-start(bf16[768,384]{1,0:T(8,128)(2,1)} %get-tuple-element.14), channel_id=1, source_target_pairs={{0,16},{16,0},{32,48},{48,32},{64,80},{80,64},{96,112},{112,96},{1... | collective-permute-start | bytes 1769480 | tf_op jit(solution)/shard_map/ppermute | solution.py:261
  97.9 11.4 %copy-start.8 = (bf16[768,384]{1,0:T(8,128)(2,1)S(1)}, bf16[768,384]{1,0:T(8,128)(2,1)}, u32[]{:S(2)}) copy-start(bf16[768,384]{1,0:T(8,128)(2,1)} %get-tuple-element.13) | copy-start | bytes 1769476
  97.9 10.2 %collective-permute-start.6 = (bf16[16,24,384]{2,1,0:T(8,128)(2,1)S(1)}, bf16[16,24,384]{2,1,0:T(8,128)(2,1)S(1)}, u32[]{:S(2)}, u32[]{:S(2)}) collective-permute-start(bf16[16,24,384]{2,1,0:T(8,128)(2,1)S(1)} %fusion.2), channel_id=1, source_target_pairs={{0,128},{16,144},{32,160},{48,176},{64,192},{80,208},{96,224},{112... | collective-permute-start | bytes 884744 | tf_op jit(solution)/shard_map/ppermute | solution.py:261

commit v4 on v2

v4 whole, which is shorter than its diff:
```python
import jax
import jax.numpy as jnp
from jax import lax
from jax.experimental import pallas as pl
from jax.experimental.pallas import tpu as pltpu
from jax.sharding import PartitionSpec as P

BF16 = jnp.bfloat16
F32 = jnp.float32
VMEM_LIMIT = 56 * 1024 * 1024
PIECE = [
    (i & 1) * 8 + ((((i >> 1) ^ (i >> 2)) & 1) * 4) + ((i >> 2) & 1) * 2 + (i >> 3)
    for i in range(16)
]


def product(left, right, left_dim, right_dim):
    return lax.dot_general(
        left, right, (((left_dim,), (right_dim,)), ((), ())), preferred_element_type=F32
    )


def normalise(block):
    wide = block.astype(F32)
    return (wide * lax.rsqrt(jnp.mean(wide * wide, axis=-1, keepdims=True) + 1e-06)).astype(BF16)


def send_kernel(inputs_ref, cot_ref, first_ref, sent_ref):
    places, _, groups, tile, width = sent_ref.shape

    def part(block):
        return block.reshape(places, groups, -1, width)

    mixes, weights = [], []
    for a in range(inputs_ref.shape[1]):
        normed = normalise(inputs_ref[0, a])
        weights.append(part(cot_ref[0, a].astype(F32) * normed.astype(F32)))
        mixes.append(part(product(first_ref[a], normed, 1, 0)))
    for k, parts in enumerate((mixes, weights)):
        sent_ref[:, k] = jnp.concatenate(parts, axis=2).astype(BF16)


def build_sent(inputs, cotangent, first_blocks, places):
    _, rows, block, width = inputs.shape
    groups, step = 2, 2
    tile = step * block // places // groups
    whole = pl.BlockSpec((1, step, block, width), lambda a: (0, a, 0, 0))
    return pl.pallas_call(
        send_kernel,
        grid=(rows // step,),
        in_specs=[whole, whole, pl.BlockSpec((step, block, block), lambda a: (a, 0, 0))],
        out_specs=pl.BlockSpec((places, 2, groups, tile, width), lambda a: (0, 0, 0, a, 0)),
        out_shape=jax.ShapeDtypeStruct((places, 2, groups, tile * rows // step, width), BF16),
        compiler_params=pltpu.CompilerParams(vmem_limit_bytes=VMEM_LIMIT),
        name="send",
    )(inputs, cotangent, first_blocks)


def mlp_kernel(inputs_ref, cot_ref, up_ref, down_ref, up_t_ref, down_t_ref, normed_ref, cot_t_ref):
    @pl.when(pl.program_id(0) == 0)
    def _():
        normed_ref[...] = normalise(inputs_ref[...])
        cot_t_ref[...] = cot_ref[...].T

    field = product(normed_ref[...], up_ref[...], 1, 0)
    back = product(cot_ref[...], down_ref[...], 1, 1)
    scale, cubic = 0.7978845608028654, 0.044715
    square = field * field
    bend = jnp.tanh(scale * field * (1.0 + cubic * square))
    upper = 0.5 + 0.5 * bend
    hidden = (field * upper).astype(BF16)
    slope = upper + (0.5 * scale) * field * (1.0 - bend * bend) * (1.0 + 3.0 * cubic * square)
    up_slope = (back * slope).astype(BF16)
    down_t_ref[...] = product(cot_t_ref[...], hidden, 1, 0).astype(BF16)
    up_t_ref[...] = product(up_slope, normed_ref[...], 0, 0).astype(BF16)


def mlp_grads(inputs, cotangent, up_weight, down_weight):
    positions, width = inputs.shape
    units = up_weight.shape[1]
    step = 256
    whole = pl.BlockSpec((positions, width), lambda f: (0, 0))
    by_row = pl.BlockSpec((step, width), lambda f: (f, 0))
    by_col = pl.BlockSpec((width, step), lambda f: (0, f))
    return pl.pallas_call(
        mlp_kernel,
        grid=(units // step,),
        in_specs=[whole, whole, by_col, by_row],
        out_specs=[by_row, by_col],
        out_shape=[
            jax.ShapeDtypeStruct((units, width), BF16),
            jax.ShapeDtypeStruct((width, units), BF16),
        ],
        scratch_shapes=[pltpu.VMEM((positions, width), BF16), pltpu.VMEM((width, positions), BF16)],
        compiler_params=pltpu.CompilerParams(vmem_limit_bytes=VMEM_LIMIT),
        name="mlp",
    )(inputs, cotangent, up_weight, down_weight)


def spread_kernel(stacked_ref, out_ref):
    groups, positions, size = stacked_ref.shape
    blocks = positions // size
    take = lax.broadcasted_iota(jnp.int32, (size, positions), 1) // blocks
    spread = (take == lax.broadcasted_iota(jnp.int32, (size, positions), 0)).astype(BF16)
    row = lax.broadcasted_iota(jnp.int32, (positions, positions), 0)
    col = lax.broadcasted_iota(jnp.int32, (positions, positions), 1)
    same = row % blocks == col % blocks
    for k in range(groups):
        wide = product(stacked_ref[k], spread, 1, 0)
        out_ref[k] = jnp.where(same, wide, 0.0).astype(BF16)


def spread_second(second_blocks, groups):
    blocks, size, _ = second_blocks.shape
    positions = blocks // groups * size
    stacked = second_blocks.reshape(groups, -1, size, size).transpose(0, 2, 1, 3)
    return pl.pallas_call(
        spread_kernel,
        out_shape=jax.ShapeDtypeStruct((groups, positions, positions), BF16),
        compiler_params=pltpu.CompilerParams(vmem_limit_bytes=VMEM_LIMIT),
        name="spread",
    )(stacked.reshape(groups, positions, size))


def value_kernel(
    core_ref, mix_ref, weighted_ref, second_ref, weight_ref, keep_ref, give_ref, both_ref
):
    groups, positions, _ = second_ref.shape
    step = pl.program_id(0)

    @pl.when(step == 0)
    def _():
        for k in range(groups):
            first_mix = mix_ref[:, 0, k].reshape(positions, -1)
            both = product(second_ref[k], first_mix, 1, 0)
            both_ref[pl.ds(k * positions, positions)] = both.astype(BF16)

    slopes = []
    for k in range(groups):
        mixed = product(both_ref[pl.ds(k * positions, positions)], weight_ref[...], 1, 0)
        sigmoid_part = 0.5 + 0.5 * jnp.tanh(0.5 * mixed)
        weighted = weighted_ref[:, 0, k].reshape(mixed.shape).astype(F32)
        slope = weighted * (sigmoid_part * (1.0 + mixed * (1.0 - sigmoid_part)))
        slopes.append(slope.astype(BF16))
    grad = product(jnp.concatenate(slopes, axis=0), both_ref[...], 0, 0).astype(BF16)

    @pl.when(step == 0)
    def _():
        give_ref[...] = grad

    @pl.when(step == 1)
    def _():
        keep_ref[...] = grad


def value_grad(core, came, second, value_weight):
    places, _, groups, tile, width = came.shape
    positions = places * groups * tile
    half = width // 2

    def part(e, c):
        return jnp.where(e == 0, 1 - c[0], c[0])

    whole = pl.BlockSpec((half, width), lambda e, c: (0, 0))
    return pl.pallas_call(
        value_kernel,
        grid_spec=pltpu.PrefetchScalarGridSpec(
            num_scalar_prefetch=1,
            grid=(2,),
            in_specs=[
                pl.BlockSpec((places, 1, groups, tile, width), lambda e, c: (0, 0, 0, 0, 0)),
                pl.BlockSpec((places, 1, groups, tile, half), lambda e, c: (0, 1, 0, 0, part(e, c))),
                pl.BlockSpec(second.shape, lambda e, c: (0, 0, 0)),
                pl.BlockSpec((width, half), lambda e, c: (0, part(e, c))),
            ],
            out_specs=[whole, whole],
            scratch_shapes=[pltpu.VMEM((positions, width), BF16)],
        ),
        out_shape=[jax.ShapeDtypeStruct((half, width), BF16)] * 2,
        compiler_params=pltpu.CompilerParams(vmem_limit_bytes=24 * 1024 * 1024),
        name="value",
    )(core, came, came, second, value_weight)


def join_kernel(pieces_ref, value_ref, up_ref, down_ref, rows_ref):
    places, size, lanes = pieces_ref.shape
    for i in range(places):
        rows_ref[PIECE[i] * size : (PIECE[i] + 1) * size, :lanes] = pieces_ref[i]
    turned = rows_ref[...].T
    width = value_ref.shape[1]
    share = value_ref.shape[0]
    value_ref[...] = turned[:share]
    up_ref[:, :width] = turned[share : 2 * share]
    up_ref[:, width:] = turned[2 * share : 3 * share]
    down_ref[...] = turned[3 * share : 5 * share]


def join(pieces):
    places, size, lanes = pieces.shape
    width = places * size
    share = lanes // 5
    padded = -(-lanes // 128) * 128
    return pl.pallas_call(
        join_kernel,
        out_shape=[
            jax.ShapeDtypeStruct((share, width), BF16),
            jax.ShapeDtypeStruct((share, 2 * width), BF16),
            jax.ShapeDtypeStruct((2 * share, width), BF16),
        ],
        scratch_shapes=[pltpu.VMEM((width, padded), BF16)],
        compiler_params=pltpu.CompilerParams(vmem_limit_bytes=VMEM_LIMIT),
        name="join",
    )(pieces)


def swap(block, flip):
    return lax.ppermute(block, "dp", [(i, i ^ flip) for i in range(16)])


def add_swapped(keep, give, flip):
    return keep.astype(F32) + swap(give.astype(BF16), flip).astype(F32)


def halve(total, axis, bit, flip):
    keep = lax.dynamic_slice_in_dim(total, bit, 1, axis)
    give = lax.dynamic_slice_in_dim(total, 1 - bit, 1, axis)
    return add_swapped(keep, give, flip)


def scatter_chips(left, right):
    i = lax.axis_index("dp")
    x0, x1, y_hi = (i >> 1) & 1, (i >> 2) & 1, i >> 3
    out = []
    for straight, block in ((True, left), (False, right)):
        groups, rows, lanes = block.shape
        total = block.reshape(groups, 2, 2, 2, rows // 8, lanes)
        if straight:
            total = halve(total, 1, x0 ^ x1, 2)
            total = halve(total, 2, x1, 6)
        else:
            total = halve(total, 2, x1, 6)
            total = halve(total, 1, x0 ^ x1, 2)
        total = halve(total, 3, y_hi, 8)
        out.append(total.reshape(groups, rows // 8, lanes).astype(BF16))
    return out


def exchange(block, axis):
    return lax.all_to_all(block, axis, split_axis=0, concat_axis=0, tiled=True)


def by_place(block, places):
    rows, lanes = block.shape
    return block.reshape(rows, places, lanes // places).transpose(1, 0, 2)


def local(inputs, cotangent, value_weight, up_weight, down_weight, first_blocks, second_blocks):
    width = inputs.shape[3]
    half = width // 2
    places = lax.axis_size("seq")
    core = lax.axis_index("dp") & 1
    core_arg = jnp.full((1,), core, jnp.int32)
    total_tokens = (
        inputs.shape[0] * inputs.shape[1] * inputs.shape[2] * lax.axis_size("dp") * places
    )
    factor = float(total_tokens) ** (-0.5)

    def pack(parts):
        return jnp.concatenate([by_place(part, places) for part in parts], axis=2)

    came = exchange(build_sent(inputs, cotangent, first_blocks, places), "seq")

    flat = inputs.reshape(-1, width)
    up_t, down_t = mlp_grads(flat, cotangent.reshape(-1, width), up_weight, down_weight)
    up_t = halve(up_t.reshape(2, 2, half, width), 1, core, 1).reshape(2, half, width)
    down_t = halve(down_t.reshape(1, 2, half, 2 * width), 1, core, 1).reshape(1, half, 2 * width)
    up_t, down_t = scatter_chips(up_t, down_t)

    mlp_part = pack((up_t[0], up_t[1], down_t[0]))

    second = spread_second(second_blocks, 2)
    came, mlp_part, second = lax.optimization_barrier((came, mlp_part, second))
    value_keep, value_give = value_grad(core_arg, came, second, value_weight)
    value_t = add_swapped(value_keep, value_give, 1)
    value_left, value_right = scatter_chips(value_t[None, :, :half], value_t[None, :, half:])
    value_t = jnp.concatenate([value_left[0], value_right[0]], axis=1)

    part = exchange(jnp.concatenate([pack((value_t,)), mlp_part], axis=2), "seq")
    part = (jnp.sum(part.astype(F32), axis=0) * factor).astype(BF16)
    return tuple(join(exchange(jnp.broadcast_to(part[None], (16,) + part.shape), "dp")))


def solution(mesh):
    placed = (
        P("dp", "seq", None, None),
        P("dp", "seq", None, None),
        P(),
        P(),
        P(),
        P("seq", None, None),
        P("seq", None, None),
    )
    return jax.shard_map(
        local,
        mesh=mesh,
        in_specs=placed,
        out_specs=(P("seq", None), P("seq", None), P("seq", None)),
        check_vma=False,
    )
```

time: 161 us -> 156 us (0.969)
  Pallas kernels: 37.6 us -> 30.8 us
  waiting for transfers between devices: 32.8 us -> 28.6 us
  local copies, waits for them, and re-layouts: 11.4 us -> 14.4 us
  other arithmetic: 7.34 us -> 9.59 us
    pallas_call x3, Pallas kernels: 18.6 us -> 11.7 us  [the longest x1 5.28 us: value_grad(): pl.pallas_call(value_kernel, grid_spec=pltpu.PrefetchScalarGridSpec(num_s...]
    ppermute x16 -> x15, waiting for transfers between devices: 31 us -> 25.1 us  [swap(): return lax.ppermute(block, 'dp', [(i, i ^ flip) for i in range(16)])]
    unnamed x14 -> x18, local copies, waits for them, and re-layouts: 2.28 us -> 4.74 us
    another operation x0 -> x2, local copies, waits for them, and re-layouts: none -> 1.77 us  [by_place(): return block.reshape(rows, places, lanes // places).transpose(1, 0, 2)]
    all_to_all x1, waiting for transfers between devices: 1.75 us -> 3.46 us  [exchange(): return lax.all_to_all(block, axis, split_axis=0, concat_axis=0, tiled=True)]
    ppermute x16 -> x15, starting transfers between devices: 22.5 us -> 22.2 us  [swap(): return lax.ppermute(block, 'dp', [(i, i ^ flip) for i in range(16)])]
    dynamic_slice x4 -> x2, local copies, waits for them, and re-layouts: 3.73 us -> 3.62 us  [halve(): give = lax.dynamic_slice_in_dim(total, 1 - bit, 1, axis)]
    add x12 -> x11, other arithmetic: 6.75 us -> 6.7 us  [add_swapped(): return keep.astype(F32) + swap(give.astype(BF16), flip).astype(F32)]
  transfers between devices with their start and end apart: 17 -> 16, of which waited for: 12 -> 11; matrix products, arithmetic and copies ran while one was open for 9% -> 12% of each run, Pallas kernels for 13% -> 13%
where the time goes in v4:
time: 156 us
  blocking collectives  39.2 us (25%)
  starting transfers between devices  32.3 us (21%)
  Pallas kernels  30.8 us (20%)
  waiting for transfers between devices  28.6 us (18%)
  local copies, waits for them, and re-layouts  14.4 us (9%)
  other arithmetic  9.59 us (6%)
    all_to_all x2, blocking collectives, exchange(): return lax.all_to_all(block, axis, split_axis=0, concat_axis=0, tiled=True)  39.2 us
    ppermute x15, waiting for transfers between devices, swap(): return lax.ppermute(block, 'dp', [(i, i ^ flip) for i in range(16)])  25.1 us
    ppermute x15, starting transfers between devices, swap(): return lax.ppermute(block, 'dp', [(i, i ^ flip) for i in range(16)])  22.2 us
    pallas_call x1, Pallas kernels, mlp_grads(): pl.pallas_call(mlp_kernel, grid=(units // step,), in_specs=[whole, whole,...  17.2 us
    all_to_all x1, starting transfers between devices, exchange(): return lax.all_to_all(block, axis, split_axis=0, concat_axis=0, tiled=True)  10.1 us
    add x11, other arithmetic, add_swapped(): return keep.astype(F32) + swap(give.astype(BF16), flip).astype(F32)  6.7 us
    pallas_call x1, Pallas kernels, value_grad(): pl.pallas_call(value_kernel, grid_spec=pltpu.PrefetchScalarGridSpec(num_s...  5.28 us
    unnamed x18, local copies, waits for them, and re-layouts  4.74 us
  transfers between devices with their start and end apart: 16, of which 11 were waited for; matrix products, arithmetic and copies ran while one was open for 12% of the time, Pallas kernels for 13%

profile of v4, /device:TPU:1, one launch (start us, length us, event | category | flops | bytes accessed | tf_op | source)
XLA Modules:
  0.0 155.8 jit_solution(12546672771759125988)
XLA Ops:
  0.6 4.0 %send.1 = bf16[16,2,2,32,768]{4,3,2,1,0:T(8,128)(2,1)} custom-call(bf16[1,4,256,768]{3,2,1,0:T(8,128)(2,1)} %inputs_ref.1, bf16[1,4,256,768]{3,2,1,0:T(8,128)(2,1)} %cot_ref.1, bf16[4,256,256]{2,1,0:T(8,128)(2,1)} %first_ref.1), custom_call_target="tpu_custom_call" | custom-call | tf_op jit(solution)/shard_map/send/pallas_call | solution.py:48
  4.6 10.1 %all-to-all-start = ((bf16[16,2,2,32,768]{4,3,2,1,0:T(8,128)(2,1)}), bf16[16,2,2,32,768]{4,3,2,1,0:T(8,128)(2,1)S(1)}, u32[]{:S(2)}, u32[]{:S(2)}) async-start(bf16[16,2,2,32,768]{4,3,2,1,0:T(8,128)(2,1)} %send.1), calls=%async_computation | async-start | bytes 6291456 | tf_op jit(solution)/shard_map/all_to_all | solution.py:249
  14.8 17.2 %mlp.1 = (bf16[1536,768]{1,0:T(8,128)(2,1)}, bf16[768,1536]{1,0:T(8,128)(2,1)}) custom-call(bf16[1024,768]{1,0:T(8,128)(2,1)} %bitcast.34, bf16[1024,768]{1,0:T(8,128)(2,1)} %bitcast.35, bf16[768,1536]{1,0:T(8,128)(2,1)} %up_ref.1, bf16[1536,768]{1,0:T(8,128)(2,1)} %down_ref.1), custom_call_target="tpu_custom_call" | custom-call | tf_op jit(solution)/shard_map/mlp/pallas_call | solution.py:85
  32.0 2.5 %constant_dynamic-slice_fusion.1 = bf16[2,1,384,768]{3,2,1,0:T(8,128)(2,1)} fusion(bf16[2,2,384,768]{3,2,1,0:T(8,128)(2,1)} %bitcast.38, s32[]{:T(128)S(6)} %select_n.17), kind=kLoop, calls=%fused_computation.34 | loop fusion | bytes 2359300 | tf_op jit(solution)/shard_map/dynamic_slice | solution.py:226
  38.3 2.0 %convert_add_fusion.1 = f32[2,1,384,768]{3,2,1,0:T(8,128)S(1)} fusion(bf16[2,1,384,768]{3,2,1,0:T(8,128)(2,1)} %collective-permute-done, bf16[2,2,384,768]{3,2,1,0:T(8,128)(2,1)} %bitcast.39, s32[]{:T(128)S(6)} %select_n.16), kind=kLoop, calls=%fused_computation.1 | loop fusion | flops 1769472 | bytes 4718596 | tf_op jit(solution)/shard_map/add | solution.py:221
  46.4 1.8 %collective-permute-start.5 = (bf16[1,2,1,2,48,1536]{5,4,3,2,1,0:T(8,128)(2,1)}, bf16[1,2,1,2,48,1536]{5,4,3,2,1,0:T(8,128)(2,1)}, u32[]{:S(2)}, u32[]{:S(2)}) collective-permute-start(bf16[1,2,1,2,48,1536]{5,4,3,2,1,0:T(8,128)(2,1)} %dynamic-slice_convert_fusion), channel_id=1, source_target_pairs={{0,96},{16,112},{32,64},{48,80},{64,32},{80,48},{96,0},{112,16},{1... | collective-permute-start | bytes 1769480 | tf_op jit(solution)/shard_map/ppermute | solution.py:217
  49.1 2.4 %spread.1.second_ref = bf16[2,512,512]{2,1,0:T(8,128)(2,1)} custom-call(bf16[2,512,64]{2,1,0:T(8,128)(2,1)} %bitcast.44), custom_call_target="tpu_custom_call" | custom-call | tf_op jit(solution)/shard_map/spread/pallas_call | solution.py:117
  51.5 4.6 %collective-permute-done.1 = bf16[2,1,2,2,48,768]{5,4,3,2,1,0:T(8,128)(2,1)} collective-permute-done((bf16[2,1,2,2,48,768]{5,4,3,2,1,0:T(8,128)(2,1)}, bf16[2,1,2,2,48,768]{5,4,3,2,1,0:T(8,128)(2,1)}, u32[]{:S(2)}, u32[]{:S(2)}) %collective-permute-start.1) | collective-permute-done | bytes 589856 | tf_op jit(solution)/shard_map/ppermute | solution.py:217
  57.8 2.6 %collective-permute-start.2 = (bf16[2,1,1,2,48,768]{5,4,3,2,1,0:T(8,128)(2,1)S(1)}, bf16[2,1,1,2,48,768]{5,4,3,2,1,0:T(8,128)(2,1)S(1)}, u32[]{:S(2)}, u32[]{:S(2)}) collective-permute-start(bf16[2,1,1,2,48,768]{5,4,3,2,1,0:T(8,128)(2,1)S(1)} %dynamic-slice_convert_fusion.3), channel_id=1, source_target_pairs={{0,96},{16,112},{32,64},{48,80},{64,32},{80,48},{96,0},{112,16},{1... | collective-permute-start | bytes 884744 | tf_op jit(solution)/shard_map/ppermute | solution.py:217
  60.3 1.8 %collective-permute-done.5 = bf16[1,2,1,2,48,1536]{5,4,3,2,1,0:T(8,128)(2,1)} collective-permute-done((bf16[1,2,1,2,48,1536]{5,4,3,2,1,0:T(8,128)(2,1)}, bf16[1,2,1,2,48,1536]{5,4,3,2,1,0:T(8,128)(2,1)}, u32[]{:S(2)}, u32[]{:S(2)}) %collective-permute-start.5) | collective-permute-done | bytes 589856 | tf_op jit(solution)/shard_map/ppermute | solution.py:217
  63.5 4.9 %collective-permute-done.2 = bf16[2,1,1,2,48,768]{5,4,3,2,1,0:T(8,128)(2,1)S(1)} collective-permute-done((bf16[2,1,1,2,48,768]{5,4,3,2,1,0:T(8,128)(2,1)S(1)}, bf16[2,1,1,2,48,768]{5,4,3,2,1,0:T(8,128)(2,1)S(1)}, u32[]{:S(2)}, u32[]{:S(2)}) %collective-permute-start.2) | collective-permute-done | bytes 294944 | tf_op jit(solution)/shard_map/ppermute | solution.py:217
  68.5 2.7 %collective-permute-start.3 = (bf16[2,1,1,1,48,768]{5,4,3,2,1,0:T(8,128)(2,1)S(1)}, bf16[2,1,1,1,48,768]{5,4,3,2,1,0:T(8,128)(2,1)S(1)}, u32[]{:S(2)}, u32[]{:S(2)}) collective-permute-start(bf16[2,1,1,1,48,768]{5,4,3,2,1,0:T(8,128)(2,1)S(1)} %dynamic-slice_convert_fusion.7), channel_id=1, source_target_pairs={{0,128},{16,144},{32,160},{48,176},{64,192},{80,208},{96,224},{112... | collective-permute-start | bytes 442376 | tf_op jit(solution)/shard_map/ppermute | solution.py:217
  76.2 2.4 %collective-permute-done.7 = bf16[1,1,1,1,48,1536]{5,4,3,2,1,0:T(8,128)(2,1)} collective-permute-done((bf16[1,1,1,1,48,1536]{5,4,3,2,1,0:T(8,128)(2,1)S(1)}, bf16[1,1,1,1,48,1536]{5,4,3,2,1,0:T(8,128)(2,1)}, u32[]{:S(2)}, u32[]{:S(2)}) %collective-permute-start.7) | collective-permute-done | bytes 147488 | tf_op jit(solution)/shard_map/ppermute | solution.py:217
  81.9 3.5 %all-to-all-done.mix_ref.weighted_ref = bf16[16,2,2,32,768]{4,3,2,1,0:T(8,128)(2,1)S(1)} async-done(((bf16[16,2,2,32,768]{4,3,2,1,0:T(8,128)(2,1)}), bf16[16,2,2,32,768]{4,3,2,1,0:T(8,128)(2,1)S(1)}, u32[]{:S(2)}, u32[]{:S(2)}) %all-to-all-start) | async-done | bytes 3145760 | tf_op jit(solution)/shard_map/all_to_all | solution.py:249
  87.8 5.3 %value.1 = (bf16[384,768]{1,0:T(8,128)(2,1)S(1)}, bf16[384,768]{1,0:T(8,128)(2,1)S(1)}) custom-call(s32[1]{0:T(128)} %bitcast.core_ref, bf16[16,2,2,32,768]{4,3,2,1,0:T(8,128)(2,1)S(1)} %all-to-all-done.mix_ref.weighted_ref, bf16[16,2,2,32,768]{4,3,2,1,0:T(8,128)(2,1)S(1)} %all-to-all-done.mix_ref.weighted_ref, bf16[2,512,512]{2,1,0:T(8,128)(2,1)S(1)} %copy-done, ...), custom_call_target="tpu_custom_call" | custom-call | tf_op jit(solution)/shard_map/value/pallas_call | solution.py:165
  97.9 1.9 %collective-permute-start.12 = (bf16[1,2,1,2,48,384]{5,4,3,2,1,0:T(8,128)(2,1)S(1)}, bf16[1,2,1,2,48,384]{5,4,3,2,1,0:T(8,128)(2,1)S(1)}, u32[]{:S(2)}, u32[]{:S(2)}) collective-permute-start(bf16[1,2,1,2,48,384]{5,4,3,2,1,0:T(8,128)(2,1)S(1)} %dynamic-slice_convert_fusion.4), channel_id=1, source_target_pairs={{0,96},{16,112},{32,64},{48,80},{64,32},{80,48},{96,0},{112,16},{1... | collective-permute-start | bytes 442376 | tf_op jit(solution)/shard_map/ppermute | solution.py:217
  99.8 1.9 %collective-permute-done.9 = bf16[1,1,2,2,48,384]{5,4,3,2,1,0:T(8,128)(2,1)S(1)} collective-permute-done((bf16[1,1,2,2,48,384]{5,4,3,2,1,0:T(8,128)(2,1)S(1)}, bf16[1,1,2,2,48,384]{5,4,3,2,1,0:T(8,128)(2,1)S(1)}, u32[]{:S(2)}, u32[]{:S(2)}) %collective-permute-start.9) | collective-permute-done | bytes 147488 | tf_op jit(solution)/shard_map/ppermute | solution.py:217
  101.8 2.6 %collective-permute-start.10 = (bf16[1,1,1,2,48,384]{5,4,3,2,1,0:T(8,128)(2,1)S(1)}, bf16[1,1,1,2,48,384]{5,4,3,2,1,0:T(8,128)(2,1)S(1)}, u32[]{:S(2)}, u32[]{:S(2)}) collective-permute-start(bf16[1,1,1,2,48,384]{5,4,3,2,1,0:T(8,128)(2,1)S(1)} %dynamic-slice_convert_fusion.9), channel_id=1, source_target_pairs={{0,96},{16,112},{32,64},{48,80},{64,32},{80,48},{96,0},{112,16},{1... | collective-permute-start | bytes 221192 | tf_op jit(solution)/shard_map/ppermute | solution.py:217
  104.5 1.8 %collective-permute-done.10 = bf16[1,1,1,2,48,384]{5,4,3,2,1,0:T(8,128)(2,1)S(1)} collective-permute-done((bf16[1,1,1,2,48,384]{5,4,3,2,1,0:T(8,128)(2,1)S(1)}, bf16[1,1,1,2,48,384]{5,4,3,2,1,0:T(8,128)(2,1)S(1)}, u32[]{:S(2)}, u32[]{:S(2)}) %collective-permute-start.10) | collective-permute-done | bytes 73760 | tf_op jit(solution)/shard_map/ppermute | solution.py:217
  106.3 2.7 %collective-permute-start.11 = (bf16[1,1,1,1,48,384]{5,4,3,2,1,0:T(8,128)(2,1)S(1)}, bf16[1,1,1,1,48,384]{5,4,3,2,1,0:T(8,128)(2,1)S(1)}, u32[]{:S(2)}, u32[]{:S(2)}) collective-permute-start(bf16[1,1,1,1,48,384]{5,4,3,2,1,0:T(8,128)(2,1)S(1)} %dynamic-slice_convert_fusion.11), channel_id=1, source_target_pairs={{0,128},{16,144},{32,160},{48,176},{64,192},{80,208},{96,224},{112... | collective-permute-start | bytes 110600 | tf_op jit(solution)/shard_map/ppermute | solution.py:217
  110.9 3.2 %collective-permute-done.14 = bf16[1,1,1,1,48,384]{5,4,3,2,1,0:T(8,128)(2,1)S(1)} collective-permute-done((bf16[1,1,1,1,48,384]{5,4,3,2,1,0:T(8,128)(2,1)S(1)}, bf16[1,1,1,1,48,384]{5,4,3,2,1,0:T(8,128)(2,1)S(1)}, u32[]{:S(2)}, u32[]{:S(2)}) %collective-permute-start.14) | collective-permute-done | bytes 36896 | tf_op jit(solution)/shard_map/ppermute | solution.py:217
  114.6 18.8 %all_to_all.15 = bf16[16,48,240]{2,1,0:T(8,128)(2,1)S(1)} all-to-all(bf16[16,48,240]{2,1,0:T(8,128)(2,1)S(1)} %copy.13), channel_id=1, replica_groups=mesh['dp'=16,'seq'=16] {'seq'}, dimensions={0} | all-to-all | bytes 737280 | tf_op jit(solution)/shard_map/all_to_all | solution.py:249
  133.6 20.4 %all_to_all.16.pieces_ref = bf16[16,48,240]{2,1,0:T(8,128)(2,1)} all-to-all(bf16[16,48,240]{2,1,0:T(8,128)(2,1)S(1)} %broadcast_in_dim.10), channel_id=1, replica_groups=mesh['dp'=16,'seq'=16] {'dp'}, dimensions={0} | all-to-all | bytes 737280 | tf_op jit(solution)/shard_map/all_to_all | solution.py:249
  154.0 1.9 %join.1 = (bf16[48,768]{1,0:T(8,128)(2,1)}, bf16[48,1536]{1,0:T(8,128)(2,1)}, bf16[96,768]{1,0:T(8,128)(2,1)}) custom-call(bf16[16,48,240]{2,1,0:T(8,128)(2,1)} %all_to_all.16.pieces_ref), custom_call_target="tpu_custom_call" | custom-call | tf_op jit(solution)/shard_map/join/pallas_call | solution.py:203
  (77 shorter events, 31.9 us)
Async XLA Ops:
  4.6 80.7 %all-to-all-start = ((bf16[16,2,2,32,768]{4,3,2,1,0:T(8,128)(2,1)}), bf16[16,2,2,32,768]{4,3,2,1,0:T(8,128)(2,1)S(1)}, u32[]{:S(2)}, u32[]{:S(2)}) async-start(bf16[16,2,2,32,768]{4,3,2,1,0:T(8,128)(2,1)} %send.1), calls=%async_computation | async-start | bytes 6291456 | tf_op jit(solution)/shard_map/all_to_all | solution.py:249
  32.0 3.5 %copy-start.5 = (bf16[768,1536]{1,0:T(8,128)(2,1)S(1)}, bf16[768,1536]{1,0:T(8,128)(2,1)}, u32[]{:S(2)}) copy-start(bf16[768,1536]{1,0:T(8,128)(2,1)} %get-tuple-element.11) | copy-start | bytes 7077892
  34.5 3.8 %collective-permute-start = (bf16[2,1,384,768]{3,2,1,0:T(8,128)(2,1)}, bf16[2,1,384,768]{3,2,1,0:T(8,128)(2,1)}, u32[]{:S(2)}, u32[]{:S(2)}) collective-permute-start(bf16[2,1,384,768]{3,2,1,0:T(8,128)(2,1)} %constant_dynamic-slice_fusion.1), channel_id=1, source_target_pairs={{0,16},{16,0},{32,48},{48,32},{64,80},{80,64},{96,112},{112,96},{1... | collective-permute-start | bytes 3538952 | tf_op jit(solution)/shard_map/ppermute | solution.py:217
  36.6 6.0 %collective-permute-start.4 = (bf16[1,1,384,1536]{3,2,1,0:T(8,128)(2,1)}, bf16[1,1,384,1536]{3,2,1,0:T(8,128)(2,1)}, u32[]{:S(2)}, u32[]{:S(2)}) collective-permute-start(bf16[1,1,384,1536]{3,2,1,0:T(8,128)(2,1)} %constant_dynamic-slice_fusion), channel_id=1, source_target_pairs={{0,16},{16,0},{32,48},{48,32},{64,80},{80,64},{96,112},{112,96},{1... | collective-permute-start | bytes 3538952 | tf_op jit(solution)/shard_map/ppermute | solution.py:217
  38.3 4.2 %copy-start.6 = (bf16[768,1536]{1,0:T(8,128)(2,1)S(1)}, bf16[768,1536]{1,0:T(8,128)(2,1)}, u32[]{:S(2)}) copy-start(bf16[768,1536]{1,0:T(8,128)(2,1)} %get-tuple-element.11) | copy-start | bytes 7077892
  40.3 3.8 %copy-start.2 = (f32[2,1,384,768]{3,2,1,0:T(8,128)}, f32[2,1,384,768]{3,2,1,0:T(8,128)S(1)}, u32[]{:S(2)}) copy-start(f32[2,1,384,768]{3,2,1,0:T(8,128)S(1)} %convert_add_fusion.1) | copy-start | bytes 7077892
  41.3 14.9 %collective-permute-start.1 = (bf16[2,1,2,2,48,768]{5,4,3,2,1,0:T(8,128)(2,1)}, bf16[2,1,2,2,48,768]{5,4,3,2,1,0:T(8,128)(2,1)}, u32[]{:S(2)}, u32[]{:S(2)}) collective-permute-start(bf16[2,1,2,2,48,768]{5,4,3,2,1,0:T(8,128)(2,1)} %dynamic-slice_convert_fusion.1), channel_id=1, source_target_pairs={{0,32},{16,48},{32,0},{48,16},{64,96},{80,112},{96,64},{112,80},{1... | collective-permute-start | bytes 1769480 | tf_op jit(solution)/shard_map/ppermute | solution.py:217
  44.1 1.4 copy-start.3
  44.1 4.1 %copy-start.8 = (bf16[16,64,64]{2,1,0:T(8,128)(2,1)S(1)}, bf16[16,64,64]{2,1,0:T(8,128)(2,1)}, u32[]{:S(2)}) copy-start(bf16[16,64,64]{2,1,0:T(8,128)(2,1)} %param.13) | copy-start | bytes 393220
  46.4 15.7 %collective-permute-start.5 = (bf16[1,2,1,2,48,1536]{5,4,3,2,1,0:T(8,128)(2,1)}, bf16[1,2,1,2,48,1536]{5,4,3,2,1,0:T(8,128)(2,1)}, u32[]{:S(2)}, u32[]{:S(2)}) collective-permute-start(bf16[1,2,1,2,48,1536]{5,4,3,2,1,0:T(8,128)(2,1)} %dynamic-slice_convert_fusion), channel_id=1, source_target_pairs={{0,96},{16,112},{32,64},{48,80},{64,32},{80,48},{96,0},{112,16},{1... | collective-permute-start | bytes 1769480 | tf_op jit(solution)/shard_map/ppermute | solution.py:217
  51.5 10.6 %copy-start.4 = (f32[1,1,384,1536]{3,2,1,0:T(8,128)S(1)}, f32[1,1,384,1536]{3,2,1,0:T(8,128)}, u32[]{:S(2)}) copy-start(f32[1,1,384,1536]{3,2,1,0:T(8,128)} %copy-done.3) | copy-start | bytes 7077892
  57.8 10.6 %collective-permute-start.2 = (bf16[2,1,1,2,48,768]{5,4,3,2,1,0:T(8,128)(2,1)S(1)}, bf16[2,1,1,2,48,768]{5,4,3,2,1,0:T(8,128)(2,1)S(1)}, u32[]{:S(2)}, u32[]{:S(2)}) collective-permute-start(bf16[2,1,1,2,48,768]{5,4,3,2,1,0:T(8,128)(2,1)S(1)} %dynamic-slice_convert_fusion.3), channel_id=1, source_target_pairs={{0,96},{16,112},{32,64},{48,80},{64,32},{80,48},{96,0},{112,16},{1... | collective-permute-start | bytes 884744 | tf_op jit(solution)/shard_map/ppermute | solution.py:217
  63.4 7.8 %collective-permute-start.6 = (bf16[1,1,1,2,48,1536]{5,4,3,2,1,0:T(8,128)(2,1)S(1)}, bf16[1,1,1,2,48,1536]{5,4,3,2,1,0:T(8,128)(2,1)S(1)}, u32[]{:S(2)}, u32[]{:S(2)}) collective-permute-start(bf16[1,1,1,2,48,1536]{5,4,3,2,1,0:T(8,128)(2,1)S(1)} %dynamic-slice_convert_fusion.2), channel_id=1, source_target_pairs={{0,32},{16,48},{32,0},{48,16},{64,96},{80,112},{96,64},{112,80},{1... | collective-permute-start | bytes 884744 | tf_op jit(solution)/shard_map/ppermute | solution.py:217
  68.5 5.9 %collective-permute-start.3 = (bf16[2,1,1,1,48,768]{5,4,3,2,1,0:T(8,128)(2,1)S(1)}, bf16[2,1,1,1,48,768]{5,4,3,2,1,0:T(8,128)(2,1)S(1)}, u32[]{:S(2)}, u32[]{:S(2)}) collective-permute-start(bf16[2,1,1,1,48,768]{5,4,3,2,1,0:T(8,128)(2,1)S(1)} %dynamic-slice_convert_fusion.7), channel_id=1, source_target_pairs={{0,128},{16,144},{32,160},{48,176},{64,192},{80,208},{96,224},{112... | collective-permute-start | bytes 442376 | tf_op jit(solution)/shard_map/ppermute | solution.py:217
  72.1 6.5 %collective-permute-start.7 = (bf16[1,1,1,1,48,1536]{5,4,3,2,1,0:T(8,128)(2,1)S(1)}, bf16[1,1,1,1,48,1536]{5,4,3,2,1,0:T(8,128)(2,1)}, u32[]{:S(2)}, u32[]{:S(2)}) collective-permute-start(bf16[1,1,1,1,48,1536]{5,4,3,2,1,0:T(8,128)(2,1)S(1)} %dynamic-slice_convert_fusion.6), channel_id=1, source_target_pairs={{0,128},{16,144},{32,160},{48,176},{64,192},{80,208},{96,224},{112... | collective-permute-start | bytes 442376 | tf_op jit(solution)/shard_map/ppermute | solution.py:217
  85.4 1.2 copy-start
  86.6 1.3 copy-start.1
  93.1 3.2 %collective-permute-start.8 = (bf16[384,768]{1,0:T(8,128)(2,1)S(1)}, bf16[384,768]{1,0:T(8,128)(2,1)S(1)}, u32[]{:S(2)}, u32[]{:S(2)}) collective-permute-start(bf16[384,768]{1,0:T(8,128)(2,1)S(1)} %get-tuple-element.15), channel_id=1, source_target_pairs={{0,16},{16,0},{32,48},{48,32},{64,80},{80,64},{96,112},{112,96},{1... | collective-permute-start | bytes 1769480 | tf_op jit(solution)/shard_map/ppermute | solution.py:217
  96.6 5.1 %collective-permute-start.9 = (bf16[1,1,2,2,48,384]{5,4,3,2,1,0:T(8,128)(2,1)S(1)}, bf16[1,1,2,2,48,384]{5,4,3,2,1,0:T(8,128)(2,1)S(1)}, u32[]{:S(2)}, u32[]{:S(2)}) collective-permute-start(bf16[1,1,2,2,48,384]{5,4,3,2,1,0:T(8,128)(2,1)S(1)} %dynamic-slice_convert_fusion.5), channel_id=1, source_target_pairs={{0,32},{16,48},{32,0},{48,16},{64,96},{80,112},{96,64},{112,80},{1... | collective-permute-start | bytes 442376 | tf_op jit(solution)/shard_map/ppermute | solution.py:217
  97.9 6.5 %collective-permute-start.12 = (bf16[1,2,1,2,48,384]{5,4,3,2,1,0:T(8,128)(2,1)S(1)}, bf16[1,2,1,2,48,384]{5,4,3,2,1,0:T(8,128)(2,1)S(1)}, u32[]{:S(2)}, u32[]{:S(2)}) collective-permute-start(bf16[1,2,1,2,48,384]{5,4,3,2,1,0:T(8,128)(2,1)S(1)} %dynamic-slice_convert_fusion.4), channel_id=1, source_target_pairs={{0,96},{16,112},{32,64},{48,80},{64,32},{80,48},{96,0},{112,16},{1... | collective-permute-start | bytes 442376 | tf_op jit(solution)/shard_map/ppermute | solution.py:217
  101.8 4.5 %collective-permute-start.10 = (bf16[1,1,1,2,48,384]{5,4,3,2,1,0:T(8,128)(2,1)S(1)}, bf16[1,1,1,2,48,384]{5,4,3,2,1,0:T(8,128)(2,1)S(1)}, u32[]{:S(2)}, u32[]{:S(2)}) collective-permute-start(bf16[1,1,1,2,48,384]{5,4,3,2,1,0:T(8,128)(2,1)S(1)} %dynamic-slice_convert_fusion.9), channel_id=1, source_target_pairs={{0,96},{16,112},{32,64},{48,80},{64,32},{80,48},{96,0},{112,16},{1... | collective-permute-start | bytes 221192 | tf_op jit(solution)/shard_map/ppermute | solution.py:217
  104.4 4.6 %collective-permute-start.13 = (bf16[1,1,1,2,48,384]{5,4,3,2,1,0:T(8,128)(2,1)S(1)}, bf16[1,1,1,2,48,384]{5,4,3,2,1,0:T(8,128)(2,1)S(1)}, u32[]{:S(2)}, u32[]{:S(2)}) collective-permute-start(bf16[1,1,1,2,48,384]{5,4,3,2,1,0:T(8,128)(2,1)S(1)} %dynamic-slice_convert_fusion.8), channel_id=1, source_target_pairs={{0,32},{16,48},{32,0},{48,16},{64,96},{80,112},{96,64},{112,80},{1... | collective-permute-start | bytes 221192 | tf_op jit(solution)/shard_map/ppermute | solution.py:217
  106.3 4.4 %collective-permute-start.11 = (bf16[1,1,1,1,48,384]{5,4,3,2,1,0:T(8,128)(2,1)S(1)}, bf16[1,1,1,1,48,384]{5,4,3,2,1,0:T(8,128)(2,1)S(1)}, u32[]{:S(2)}, u32[]{:S(2)}) collective-permute-start(bf16[1,1,1,1,48,384]{5,4,3,2,1,0:T(8,128)(2,1)S(1)} %dynamic-slice_convert_fusion.11), channel_id=1, source_target_pairs={{0,128},{16,144},{32,160},{48,176},{64,192},{80,208},{96,224},{112... | collective-permute-start | bytes 110600 | tf_op jit(solution)/shard_map/ppermute | solution.py:217
  109.1 5.0 %collective-permute-start.14 = (bf16[1,1,1,1,48,384]{5,4,3,2,1,0:T(8,128)(2,1)S(1)}, bf16[1,1,1,1,48,384]{5,4,3,2,1,0:T(8,128)(2,1)S(1)}, u32[]{:S(2)}, u32[]{:S(2)}) collective-permute-start(bf16[1,1,1,1,48,384]{5,4,3,2,1,0:T(8,128)(2,1)S(1)} %dynamic-slice_convert_fusion.10), channel_id=1, source_target_pairs={{0,128},{16,144},{32,160},{48,176},{64,192},{80,208},{96,224},{112... | collective-permute-start | bytes 110600 | tf_op jit(solution)/shard_map/ppermute | solution.py:217
  (1 other events, 0.8 us)

commit v5 on v4

--- a/solution.py
+++ b/solution.py
@@ -8,6 +8,8 @@
 BF16 = jnp.bfloat16
 F32 = jnp.float32
 VMEM_LIMIT = 56 * 1024 * 1024
+SMALL_LIMIT = 24 * 1024 * 1024
+CHIPS = 8
 PIECE = [
     (i & 1) * 8 + ((((i >> 1) ^ (i >> 2)) & 1) * 4) + ((i >> 2) & 1) * 2 + (i >> 3)
     for i in range(16)
@@ -97,52 +99,52 @@
     )(inputs, cotangent, up_weight, down_weight)
 
 
-def spread_kernel(stacked_ref, out_ref):
+def value_kernel(
+    core_ref, mix_ref, weighted_ref, stacked_ref, weight_ref, keep_ref, give_ref,
+    both_ref, held_ref, copied,
+):
     groups, positions, size = stacked_ref.shape
-    blocks = positions // size
-    take = lax.broadcasted_iota(jnp.int32, (size, positions), 1) // blocks
-    spread = (take == lax.broadcasted_iota(jnp.int32, (size, positions), 0)).astype(BF16)
-    row = lax.broadcasted_iota(jnp.int32, (positions, positions), 0)
-    col = lax.broadcasted_iota(jnp.int32, (positions, positions), 1)
-    same = row % blocks == col % blocks
-    for k in range(groups):
-        wide = product(stacked_ref[k], spread, 1, 0)
-        out_ref[k] = jnp.where(same, wide, 0.0).astype(BF16)
-
-
-def spread_second(second_blocks, groups):
-    blocks, size, _ = second_blocks.shape
-    positions = blocks // groups * size
-    stacked = second_blocks.reshape(groups, -1, size, size).transpose(0, 2, 1, 3)
-    return pl.pallas_call(
-        spread_kernel,
-        out_shape=jax.ShapeDtypeStruct((groups, positions, positions), BF16),
-        compiler_params=pltpu.CompilerParams(vmem_limit_bytes=VMEM_LIMIT),
-        name="spread",
-    )(stacked.reshape(groups, positions, size))
-
-
-def value_kernel(
-    core_ref, mix_ref, weighted_ref, second_ref, weight_ref, keep_ref, give_ref, both_ref
-):
-    groups, positions, _ = second_ref.shape
     step = pl.program_id(0)
+    half = held_ref.shape[2]
+
+    def copy(k):
+        part = jnp.where(k == 0, 1 - core_ref[0], core_ref[0])
+        lanes = pl.ds(pl.multiple_of(part * half, half), half)
+        return pltpu.make_async_copy(weight_ref.at[:, lanes], held_ref.at[k], copied.at[k])
 
     @pl.when(step == 0)
     def _():
+        copy(0).start()
+        copy(1).start()
+        blocks = positions // size
+        take = lax.broadcasted_iota(jnp.int32, (size, positions), 1) // blocks
+        spread = (take == lax.broadcasted_iota(jnp.int32, (size, positions), 0)).astype(BF16)
+        row = lax.broadcasted_iota(jnp.int32, (positions, positions), 0)
+        col = lax.broadcasted_iota(jnp.int32, (positions, positions), 1)
+        same = row % blocks == col % blocks
         for k in range(groups):
+            wide = product(stacked_ref[k], spread, 1, 0)
+            second = jnp.where(same, wide, 0.0).astype(BF16)
             first_mix = mix_ref[:, 0, k].reshape(positions, -1)
-            both = product(second_ref[k], first_mix, 1, 0)
+            both = product(second, first_mix, 1, 0)
             both_ref[pl.ds(k * positions, positions)] = both.astype(BF16)
+        copy(0).wait()
+
+    @pl.when(step == 1)
+    def _():
+        copy(1).wait()
 
     slopes = []
     for k in range(groups):
-        mixed = product(both_ref[pl.ds(k * positions, positions)], weight_ref[...], 1, 0)
+        mixed = product(both_ref[pl.ds(k * positions, positions)], held_ref[step], 1, 0)
         sigmoid_part = 0.5 + 0.5 * jnp.tanh(0.5 * mixed)
         weighted = weighted_ref[:, 0, k].reshape(mixed.shape).astype(F32)
         slope = weighted * (sigmoid_part * (1.0 + mixed * (1.0 - sigmoid_part)))
         slopes.append(slope.astype(BF16))
     grad = product(jnp.concatenate(slopes, axis=0), both_ref[...], 0, 0).astype(BF16)
+    size = grad.shape[0] // CHIPS
+    pieces = [PIECE[2 * chip] % CHIPS for chip in range(CHIPS)]
+    grad = jnp.concatenate([grad[p * size : (p + 1) * size] for p in pieces], axis=0)
 
     @pl.when(step == 0)
     def _():
@@ -153,10 +155,13 @@
         keep_ref[...] = grad
 
 
-def value_grad(core, came, second, value_weight):
+def value_grad(core, came, second_blocks, value_weight):
     places, _, groups, tile, width = came.shape
     positions = places * groups * tile
     half = width // 2
+    size = second_blocks.shape[1]
+    stacked = second_blocks.reshape(groups, -1, size, size).transpose(0, 2, 1, 3)
+    stacked = stacked.reshape(groups, positions // groups, size)
 
     def part(e, c):
         return jnp.where(e == 0, 1 - c[0], c[0])
@@ -170,16 +175,20 @@
             in_specs=[
                 pl.BlockSpec((places, 1, groups, tile, width), lambda e, c: (0, 0, 0, 0, 0)),
                 pl.BlockSpec((places, 1, groups, tile, half), lambda e, c: (0, 1, 0, 0, part(e, c))),
-                pl.BlockSpec(second.shape, lambda e, c: (0, 0, 0)),
-                pl.BlockSpec((width, half), lambda e, c: (0, part(e, c))),
+                pl.BlockSpec(stacked.shape, lambda e, c: (0, 0, 0)),
+                pl.BlockSpec(memory_space=pltpu.HBM),
             ],
             out_specs=[whole, whole],
-            scratch_shapes=[pltpu.VMEM((positions, width), BF16)],
+            scratch_shapes=[
+                pltpu.VMEM((positions, width), BF16),
+                pltpu.VMEM((2, width, half), BF16),
+                pltpu.SemaphoreType.DMA((2,)),
+            ],
         ),
         out_shape=[jax.ShapeDtypeStruct((half, width), BF16)] * 2,
-        compiler_params=pltpu.CompilerParams(vmem_limit_bytes=24 * 1024 * 1024),
+        compiler_params=pltpu.CompilerParams(vmem_limit_bytes=SMALL_LIMIT),
         name="value",
-    )(core, came, came, second, value_weight)
+    )(core, came, came, stacked, value_weight)
 
 
 def join_kernel(pieces_ref, value_ref, up_ref, down_ref, rows_ref):
@@ -208,7 +217,7 @@
             jax.ShapeDtypeStruct((2 * share, width), BF16),
         ],
         scratch_shapes=[pltpu.VMEM((width, padded), BF16)],
-        compiler_params=pltpu.CompilerParams(vmem_limit_bytes=VMEM_LIMIT),
+        compiler_params=pltpu.CompilerParams(vmem_limit_bytes=SMALL_LIMIT),
         name="join",
     )(pieces)
 
@@ -245,8 +254,14 @@
     return out
 
 
-def exchange(block, axis):
-    return lax.all_to_all(block, axis, split_axis=0, concat_axis=0, tiled=True)
+def exchange(block, axis, groups=None):
+    return lax.all_to_all(
+        block, axis, split_axis=0, concat_axis=0, tiled=True, axis_index_groups=groups
+    )
+
+
+def same_core():
+    return [[2 * chip + core for chip in range(CHIPS)] for core in range(2)]
 
 
 def by_place(block, places):
@@ -278,12 +293,11 @@
 
     mlp_part = pack((up_t[0], up_t[1], down_t[0]))
 
-    second = spread_second(second_blocks, 2)
-    came, mlp_part, second = lax.optimization_barrier((came, mlp_part, second))
-    value_keep, value_give = value_grad(core_arg, came, second, value_weight)
+    came, mlp_part = lax.optimization_barrier((came, mlp_part))
+    value_keep, value_give = value_grad(core_arg, came, second_blocks, value_weight)
     value_t = add_swapped(value_keep, value_give, 1)
-    value_left, value_right = scatter_chips(value_t[None, :, :half], value_t[None, :, half:])
-    value_t = jnp.concatenate([value_left[0], value_right[0]], axis=1)
+    value_t = exchange(value_t.astype(BF16).reshape(CHIPS, -1, width), "dp", same_core())
+    value_t = jnp.sum(value_t.astype(F32), axis=0).astype(BF16)
 
     part = exchange(jnp.concatenate([pack((value_t,)), mlp_part], axis=2), "seq")
     part = (jnp.sum(part.astype(F32), axis=0) * factor).astype(BF16)

time: 156 us -> 153 us (0.981)
  blocking collectives: 39.2 us -> 54.1 us
  starting transfers between devices: 32.3 us -> 23 us
  waiting for transfers between devices: 28.6 us -> 22.5 us
  Pallas kernels: 30.8 us -> 27.8 us
    all_to_all x2 -> x3, blocking collectives: 39.2 us -> 54.1 us  [exchange(): lax.all_to_all(block, axis, split_axis=0, concat_axis=0, tiled=True, axis...]
    ppermute x15 -> x9, starting transfers between devices: 22.2 us -> 12.8 us  [swap(): return lax.ppermute(block, 'dp', [(i, i ^ flip) for i in range(16)])]
    ppermute x15 -> x9, waiting for transfers between devices: 25.1 us -> 20.6 us  [swap(): return lax.ppermute(block, 'dp', [(i, i ^ flip) for i in range(16)])]
    pallas_call x1 -> x0, Pallas kernels: 2.41 us -> none  [spread_second(): pl.pallas_call(spread_kernel, out_shape=jax.ShapeDtypeStruct((groups, pos...]
    all_to_all x1, waiting for transfers between devices: 3.46 us -> 1.84 us  [exchange(): lax.all_to_all(block, axis, split_axis=0, concat_axis=0, tiled=True, axis...]
    unnamed x18 -> x16, local copies, waits for them, and re-layouts: 4.74 us -> 3.56 us
    add x11 -> x6, other arithmetic: 6.7 us -> 6.5 us  [add_swapped(): return keep.astype(F32) + swap(give.astype(BF16), flip).astype(F32)]
  transfers between devices with their start and end apart: 16 -> 10, of which waited for: 11 -> 8; matrix products, arithmetic and copies ran while one was open for 12% -> 13% of each run, Pallas kernels for 13% -> 11%
where the time goes in v5:
time: 153 us; the launch traced here: 152 us
  blocking collectives  54.1 us (35%)
  Pallas kernels  27.8 us (18%)
  starting transfers between devices  23 us (15%)
  waiting for transfers between devices  22.5 us (15%)
  local copies, waits for them, and re-layouts  14 us (9%)
  other arithmetic  10.3 us (7%)
    all_to_all x3, blocking collectives, exchange(): lax.all_to_all(block, axis, split_axis=0, concat_axis=0, tiled=True, axis...  54.1 us
    ppermute x9, waiting for transfers between devices, swap(): return lax.ppermute(block, 'dp', [(i, i ^ flip) for i in range(16)])  20.6 us
    pallas_call x1, Pallas kernels, mlp_grads(): pl.pallas_call(mlp_kernel, grid=(units // step,), in_specs=[whole, whole,...  17.2 us
    ppermute x9, starting transfers between devices, swap(): return lax.ppermute(block, 'dp', [(i, i ^ flip) for i in range(16)])  12.8 us
    all_to_all x1, starting transfers between devices, exchange(): lax.all_to_all(block, axis, split_axis=0, concat_axis=0, tiled=True, axis...  10.1 us
    add x6, other arithmetic, add_swapped(): return keep.astype(F32) + swap(give.astype(BF16), flip).astype(F32)  6.5 us
    pallas_call x1, Pallas kernels, value_grad(): pl.pallas_call(value_kernel, grid_spec=pltpu.PrefetchScalarGridSpec(num_s...  5.66 us
    pallas_call x1, Pallas kernels, build_sent(): pl.pallas_call(send_kernel, grid=(rows // step,), in_specs=[whole, whole,...  4.02 us
  transfers between devices with their start and end apart: 10, of which 8 were waited for; matrix products, arithmetic and copies ran while one was open for 13% of the time, Pallas kernels for 11%

profile of v5, /device:TPU:1, one launch (start us, length us, event | category | flops | bytes accessed | tf_op | source)
XLA Modules:
  0.0 152.5 jit_solution(14483605282097012651)
XLA Ops:
  0.6 4.0 %send.1 = bf16[16,2,2,32,768]{4,3,2,1,0:T(8,128)(2,1)} custom-call(bf16[1,4,256,768]{3,2,1,0:T(8,128)(2,1)} %inputs_ref.1, bf16[1,4,256,768]{3,2,1,0:T(8,128)(2,1)} %cot_ref.1, bf16[4,256,256]{2,1,0:T(8,128)(2,1)} %first_ref.1), custom_call_target="tpu_custom_call" | custom-call | tf_op jit(solution)/shard_map/send/pallas_call | solution.py:50
  4.6 10.1 %all-to-all-start = ((bf16[16,2,2,32,768]{4,3,2,1,0:T(8,128)(2,1)}), bf16[16,2,2,32,768]{4,3,2,1,0:T(8,128)(2,1)S(1)}, u32[]{:S(2)}, u32[]{:S(2)}) async-start(bf16[16,2,2,32,768]{4,3,2,1,0:T(8,128)(2,1)} %send.1), calls=%async_computation | async-start | bytes 6291456 | tf_op jit(solution)/shard_map/all_to_all | solution.py:258
  14.8 17.2 %mlp.1 = (bf16[1536,768]{1,0:T(8,128)(2,1)}, bf16[768,1536]{1,0:T(8,128)(2,1)}) custom-call(bf16[1024,768]{1,0:T(8,128)(2,1)} %bitcast.29, bf16[1024,768]{1,0:T(8,128)(2,1)} %bitcast.30, bf16[768,1536]{1,0:T(8,128)(2,1)} %up_ref.1, bf16[1536,768]{1,0:T(8,128)(2,1)} %down_ref.1), custom_call_target="tpu_custom_call" | custom-call | tf_op jit(solution)/shard_map/mlp/pallas_call | solution.py:87
  32.0 2.6 %constant_dynamic-slice_fusion.1 = bf16[2,1,384,768]{3,2,1,0:T(8,128)(2,1)} fusion(bf16[2,2,384,768]{3,2,1,0:T(8,128)(2,1)} %bitcast.33, s32[]{:T(128)S(6)} %select_n.33), kind=kLoop, calls=%fused_computation.21 | loop fusion | bytes 2359300 | tf_op jit(solution)/shard_map/dynamic_slice | solution.py:235
  36.6 1.7 %collective-permute-done = bf16[2,1,384,768]{3,2,1,0:T(8,128)(2,1)} collective-permute-done((bf16[2,1,384,768]{3,2,1,0:T(8,128)(2,1)}, bf16[2,1,384,768]{3,2,1,0:T(8,128)(2,1)}, u32[]{:S(2)}, u32[]{:S(2)}) %collective-permute-start) | collective-permute-done | bytes 1179680 | tf_op jit(solution)/shard_map/ppermute | solution.py:226
  38.3 2.0 %convert_add_fusion.1 = f32[2,1,384,768]{3,2,1,0:T(8,128)S(1)} fusion(bf16[2,1,384,768]{3,2,1,0:T(8,128)(2,1)} %collective-permute-done, bf16[2,2,384,768]{3,2,1,0:T(8,128)(2,1)} %bitcast.34, s32[]{:T(128)S(6)} %select_n.32), kind=kLoop, calls=%fused_computation.1 | loop fusion | flops 1769472 | bytes 4718596 | tf_op jit(solution)/shard_map/add | solution.py:230
  42.6 1.6 %convert_add_fusion = f32[1,1,384,1536]{3,2,1,0:T(8,128)S(1)} fusion(bf16[1,1,384,1536]{3,2,1,0:T(8,128)(2,1)} %collective-permute-done.4, bf16[1,2,384,1536]{3,2,1,0:T(8,128)(2,1)S(1)} %bitcast.32, s32[]{:T(128)S(6)} %select_n.32), kind=kLoop, calls=%fused_computation | loop fusion | flops 1769472 | bytes 4718596 | tf_op jit(solution)/shard_map/add | solution.py:230
  44.2 1.5 copy-done.1
  46.6 1.9 %collective-permute-start.5 = (bf16[1,2,1,2,48,1536]{5,4,3,2,1,0:T(8,128)(2,1)}, bf16[1,2,1,2,48,1536]{5,4,3,2,1,0:T(8,128)(2,1)}, u32[]{:S(2)}, u32[]{:S(2)}) collective-permute-start(bf16[1,2,1,2,48,1536]{5,4,3,2,1,0:T(8,128)(2,1)} %dynamic-slice_convert_fusion), channel_id=1, source_target_pairs={{0,96},{16,112},{32,64},{48,80},{64,32},{80,48},{96,0},{112,16},{1... | collective-permute-start | bytes 1769480 | tf_op jit(solution)/shard_map/ppermute | solution.py:226
  49.6 6.6 %collective-permute-done.1 = bf16[2,1,2,2,48,768]{5,4,3,2,1,0:T(8,128)(2,1)} collective-permute-done((bf16[2,1,2,2,48,768]{5,4,3,2,1,0:T(8,128)(2,1)}, bf16[2,1,2,2,48,768]{5,4,3,2,1,0:T(8,128)(2,1)}, u32[]{:S(2)}, u32[]{:S(2)}) %collective-permute-start.1) | collective-permute-done | bytes 589856 | tf_op jit(solution)/shard_map/ppermute | solution.py:226
  56.2 1.6 %convert_add_fusion.3 = f32[2,1,2,2,48,768]{5,4,3,2,1,0:T(8,128)S(1)} fusion(bf16[2,1,2,2,48,768]{5,4,3,2,1,0:T(8,128)(2,1)} %collective-permute-done.1, f32[2,2,2,2,48,768]{5,4,3,2,1,0:T(8,128)} %bitcast.28, s32[]{:T(128)S(6)} %select_n.34), kind=kLoop, calls=%fused_computation.5 | loop fusion | flops 589824 | bytes 2949124 | tf_op jit(solution)/shard_map/add | solution.py:230
  57.8 2.6 %collective-permute-start.2 = (bf16[2,1,1,2,48,768]{5,4,3,2,1,0:T(8,128)(2,1)S(1)}, bf16[2,1,1,2,48,768]{5,4,3,2,1,0:T(8,128)(2,1)S(1)}, u32[]{:S(2)}, u32[]{:S(2)}) collective-permute-start(bf16[2,1,1,2,48,768]{5,4,3,2,1,0:T(8,128)(2,1)S(1)} %dynamic-slice_convert_fusion.3), channel_id=1, source_target_pairs={{0,96},{16,112},{32,64},{48,80},{64,32},{80,48},{96,0},{112,16},{1... | collective-permute-start | bytes 884744 | tf_op jit(solution)/shard_map/ppermute | solution.py:226
  60.4 2.0 %collective-permute-done.5 = bf16[1,2,1,2,48,1536]{5,4,3,2,1,0:T(8,128)(2,1)} collective-permute-done((bf16[1,2,1,2,48,1536]{5,4,3,2,1,0:T(8,128)(2,1)}, bf16[1,2,1,2,48,1536]{5,4,3,2,1,0:T(8,128)(2,1)}, u32[]{:S(2)}, u32[]{:S(2)}) %collective-permute-start.5) | collective-permute-done | bytes 589856 | tf_op jit(solution)/shard_map/ppermute | solution.py:226
  63.7 4.9 %collective-permute-done.2 = bf16[2,1,1,2,48,768]{5,4,3,2,1,0:T(8,128)(2,1)S(1)} collective-permute-done((bf16[2,1,1,2,48,768]{5,4,3,2,1,0:T(8,128)(2,1)S(1)}, bf16[2,1,1,2,48,768]{5,4,3,2,1,0:T(8,128)(2,1)S(1)}, u32[]{:S(2)}, u32[]{:S(2)}) %collective-permute-start.2) | collective-permute-done | bytes 294944 | tf_op jit(solution)/shard_map/ppermute | solution.py:226
  68.7 2.7 %collective-permute-start.3 = (bf16[2,1,1,1,48,768]{5,4,3,2,1,0:T(8,128)(2,1)S(1)}, bf16[2,1,1,1,48,768]{5,4,3,2,1,0:T(8,128)(2,1)S(1)}, u32[]{:S(2)}, u32[]{:S(2)}) collective-permute-start(bf16[2,1,1,1,48,768]{5,4,3,2,1,0:T(8,128)(2,1)S(1)} %dynamic-slice_convert_fusion.5), channel_id=1, source_target_pairs={{0,128},{16,144},{32,160},{48,176},{64,192},{80,208},{96,224},{112... | collective-permute-start | bytes 442376 | tf_op jit(solution)/shard_map/ppermute | solution.py:226
  76.4 3.0 %collective-permute-done.7 = bf16[1,1,1,1,48,1536]{5,4,3,2,1,0:T(8,128)(2,1)} collective-permute-done((bf16[1,1,1,1,48,1536]{5,4,3,2,1,0:T(8,128)(2,1)}, bf16[1,1,1,1,48,1536]{5,4,3,2,1,0:T(8,128)(2,1)}, u32[]{:S(2)}, u32[]{:S(2)}) %collective-permute-start.7) | collective-permute-done | bytes 147488 | tf_op jit(solution)/shard_map/ppermute | solution.py:226
  81.4 2.2 %pad_maximum_fusion = bf16[16,48,192]{2,0,1:T(8,128)(2,1)} fusion(bf16[16,48,96]{2,0,1:T(8,128)(2,1)} %bitcast.38, bf16[16,48,48]{2,0,1:T(8,128)(2,1)} %bitcast.37, bf16[16,48,48]{2,0,1:T(8,128)(2,1)} %bitcast.36), kind=kLoop, calls=%fused_computation.12 | loop fusion | flops 884736 | bytes 589824 | tf_op jit(solution)/shard_map/concatenate | solution.py:284
  83.5 1.8 %all-to-all-done.mix_ref.weighted_ref = bf16[16,2,2,32,768]{4,3,2,1,0:T(8,128)(2,1)S(1)} async-done(((bf16[16,2,2,32,768]{4,3,2,1,0:T(8,128)(2,1)}), bf16[16,2,2,32,768]{4,3,2,1,0:T(8,128)(2,1)S(1)}, u32[]{:S(2)}, u32[]{:S(2)}) %all-to-all-start) | async-done | bytes 3145760 | tf_op jit(solution)/shard_map/all_to_all | solution.py:258
  86.7 5.7 %value.1 = (bf16[384,768]{1,0:T(8,128)(2,1)S(1)}, bf16[384,768]{1,0:T(8,128)(2,1)S(1)}) custom-call(s32[1]{0:T(128)} %bitcast.core_ref, bf16[16,2,2,32,768]{4,3,2,1,0:T(8,128)(2,1)S(1)} %all-to-all-done.mix_ref.weighted_ref, bf16[16,2,2,32,768]{4,3,2,1,0:T(8,128)(2,1)S(1)} %all-to-all-done.mix_ref.weighted_ref, bf16[2,512,64]{2,1,0:T(8,128)(2,1)S(1)} %bitcast.24, ...), custom_call_target="tpu_custom_call" | custom-call | tf_op jit(solution)/shard_map/value/pallas_call | solution.py:170
  92.3 2.6 %collective-permute-start.8 = (bf16[384,768]{1,0:T(8,128)(2,1)S(1)}, bf16[384,768]{1,0:T(8,128)(2,1)S(1)}, u32[]{:S(2)}, u32[]{:S(2)}) collective-permute-start(bf16[384,768]{1,0:T(8,128)(2,1)S(1)} %get-tuple-element.13), channel_id=1, source_target_pairs={{0,16},{16,0},{32,48},{48,32},{64,80},{80,64},{96,112},{112,96},{1... | collective-permute-start | bytes 1769480 | tf_op jit(solution)/shard_map/ppermute | solution.py:226
  94.9 1.6 %collective-permute-done.8 = bf16[384,768]{1,0:T(8,128)(2,1)S(1)} collective-permute-done((bf16[384,768]{1,0:T(8,128)(2,1)S(1)}, bf16[384,768]{1,0:T(8,128)(2,1)S(1)}, u32[]{:S(2)}, u32[]{:S(2)}) %collective-permute-start.8) | collective-permute-done | bytes 589856 | tf_op jit(solution)/shard_map/ppermute | solution.py:226
  96.7 18.9 %all_to_all.20 = bf16[8,48,768]{2,1,0:T(8,128)(2,1)S(1)} all-to-all(bf16[8,48,768]{2,1,0:T(8,128)(2,1)S(1)} %bitcast.35), channel_id=1, replica_groups={{0,32,64,96,128,160,192,224},{16,48,80,112,144,176,208,240},{1,33,65,97..., dimensions={0} | all-to-all | bytes 1179648 | tf_op jit(solution)/shard_map/all_to_all | solution.py:258
  116.3 20.1 %all_to_all.21 = bf16[16,48,240]{2,1,0:T(8,128)(2,1)S(1)} all-to-all(bf16[16,48,240]{2,1,0:T(8,128)(2,1)S(1)} %copy.13), channel_id=1, replica_groups=mesh['dp'=16,'seq'=16] {'seq'}, dimensions={0} | all-to-all | bytes 737280 | tf_op jit(solution)/shard_map/all_to_all | solution.py:258
  136.5 15.1 %all_to_all.22.pieces_ref = bf16[16,48,240]{2,1,0:T(8,128)(2,1)S(1)} all-to-all(bf16[16,48,240]{2,1,0:T(8,128)(2,1)S(1)} %broadcast_in_dim.10), channel_id=1, replica_groups=mesh['dp'=16,'seq'=16] {'dp'}, dimensions={0} | all-to-all | bytes 737280 | tf_op jit(solution)/shard_map/all_to_all | solution.py:258
  (49 shorter events, 17.7 us)
Async XLA Ops:
  4.6 80.7 %all-to-all-start = ((bf16[16,2,2,32,768]{4,3,2,1,0:T(8,128)(2,1)}), bf16[16,2,2,32,768]{4,3,2,1,0:T(8,128)(2,1)S(1)}, u32[]{:S(2)}, u32[]{:S(2)}) async-start(bf16[16,2,2,32,768]{4,3,2,1,0:T(8,128)(2,1)} %send.1), calls=%async_computation | async-start | bytes 6291456 | tf_op jit(solution)/shard_map/all_to_all | solution.py:258
  32.0 3.5 %copy-start.4 = (bf16[768,1536]{1,0:T(8,128)(2,1)S(1)}, bf16[768,1536]{1,0:T(8,128)(2,1)}, u32[]{:S(2)}) copy-start(bf16[768,1536]{1,0:T(8,128)(2,1)} %get-tuple-element.10) | copy-start | bytes 7077892
  34.6 3.8 %collective-permute-start = (bf16[2,1,384,768]{3,2,1,0:T(8,128)(2,1)}, bf16[2,1,384,768]{3,2,1,0:T(8,128)(2,1)}, u32[]{:S(2)}, u32[]{:S(2)}) collective-permute-start(bf16[2,1,384,768]{3,2,1,0:T(8,128)(2,1)} %constant_dynamic-slice_fusion.1), channel_id=1, source_target_pairs={{0,16},{16,0},{32,48},{48,32},{64,80},{80,64},{96,112},{112,96},{1... | collective-permute-start | bytes 3538952 | tf_op jit(solution)/shard_map/ppermute | solution.py:226
  36.6 6.0 %collective-permute-start.4 = (bf16[1,1,384,1536]{3,2,1,0:T(8,128)(2,1)}, bf16[1,1,384,1536]{3,2,1,0:T(8,128)(2,1)}, u32[]{:S(2)}, u32[]{:S(2)}) collective-permute-start(bf16[1,1,384,1536]{3,2,1,0:T(8,128)(2,1)} %constant_dynamic-slice_fusion), channel_id=1, source_target_pairs={{0,16},{16,0},{32,48},{48,32},{64,80},{80,64},{96,112},{112,96},{1... | collective-permute-start | bytes 3538952 | tf_op jit(solution)/shard_map/ppermute | solution.py:226
  38.3 4.2 %copy-start.5 = (bf16[768,1536]{1,0:T(8,128)(2,1)S(1)}, bf16[768,1536]{1,0:T(8,128)(2,1)}, u32[]{:S(2)}) copy-start(bf16[768,1536]{1,0:T(8,128)(2,1)} %get-tuple-element.10) | copy-start | bytes 7077892
  40.4 2.2 %copy-start.3 = (f32[2,1,384,768]{3,2,1,0:T(8,128)}, f32[2,1,384,768]{3,2,1,0:T(8,128)S(1)}, u32[]{:S(2)}) copy-start(f32[2,1,384,768]{3,2,1,0:T(8,128)S(1)} %convert_add_fusion.1) | copy-start | bytes 7077892
  41.4 14.9 %collective-permute-start.1 = (bf16[2,1,2,2,48,768]{5,4,3,2,1,0:T(8,128)(2,1)}, bf16[2,1,2,2,48,768]{5,4,3,2,1,0:T(8,128)(2,1)}, u32[]{:S(2)}, u32[]{:S(2)}) collective-permute-start(bf16[2,1,2,2,48,768]{5,4,3,2,1,0:T(8,128)(2,1)} %dynamic-slice_convert_fusion.1), channel_id=1, source_target_pairs={{0,32},{16,48},{32,0},{48,16},{64,96},{80,112},{96,64},{112,80},{1... | collective-permute-start | bytes 1769480 | tf_op jit(solution)/shard_map/ppermute | solution.py:226
  44.2 1.5 copy-start.1
  46.6 15.7 %collective-permute-start.5 = (bf16[1,2,1,2,48,1536]{5,4,3,2,1,0:T(8,128)(2,1)}, bf16[1,2,1,2,48,1536]{5,4,3,2,1,0:T(8,128)(2,1)}, u32[]{:S(2)}, u32[]{:S(2)}) collective-permute-start(bf16[1,2,1,2,48,1536]{5,4,3,2,1,0:T(8,128)(2,1)} %dynamic-slice_convert_fusion), channel_id=1, source_target_pairs={{0,96},{16,112},{32,64},{48,80},{64,32},{80,48},{96,0},{112,16},{1... | collective-permute-start | bytes 1769480 | tf_op jit(solution)/shard_map/ppermute | solution.py:226
  49.6 12.8 %copy-start.2 = (f32[1,1,384,1536]{3,2,1,0:T(8,128)S(1)}, f32[1,1,384,1536]{3,2,1,0:T(8,128)}, u32[]{:S(2)}) copy-start(f32[1,1,384,1536]{3,2,1,0:T(8,128)} %copy-done.1) | copy-start | bytes 7077892
  57.8 10.7 %collective-permute-start.2 = (bf16[2,1,1,2,48,768]{5,4,3,2,1,0:T(8,128)(2,1)S(1)}, bf16[2,1,1,2,48,768]{5,4,3,2,1,0:T(8,128)(2,1)S(1)}, u32[]{:S(2)}, u32[]{:S(2)}) collective-permute-start(bf16[2,1,1,2,48,768]{5,4,3,2,1,0:T(8,128)(2,1)S(1)} %dynamic-slice_convert_fusion.3), channel_id=1, source_target_pairs={{0,96},{16,112},{32,64},{48,80},{64,32},{80,48},{96,0},{112,16},{1... | collective-permute-start | bytes 884744 | tf_op jit(solution)/shard_map/ppermute | solution.py:226
  63.6 7.8 %collective-permute-start.6 = (bf16[1,1,1,2,48,1536]{5,4,3,2,1,0:T(8,128)(2,1)S(1)}, bf16[1,1,1,2,48,1536]{5,4,3,2,1,0:T(8,128)(2,1)S(1)}, u32[]{:S(2)}, u32[]{:S(2)}) collective-permute-start(bf16[1,1,1,2,48,1536]{5,4,3,2,1,0:T(8,128)(2,1)S(1)} %dynamic-slice_convert_fusion.2), channel_id=1, source_target_pairs={{0,32},{16,48},{32,0},{48,16},{64,96},{80,112},{96,64},{112,80},{1... | collective-permute-start | bytes 884744 | tf_op jit(solution)/shard_map/ppermute | solution.py:226
  68.7 5.9 %collective-permute-start.3 = (bf16[2,1,1,1,48,768]{5,4,3,2,1,0:T(8,128)(2,1)S(1)}, bf16[2,1,1,1,48,768]{5,4,3,2,1,0:T(8,128)(2,1)S(1)}, u32[]{:S(2)}, u32[]{:S(2)}) collective-permute-start(bf16[2,1,1,1,48,768]{5,4,3,2,1,0:T(8,128)(2,1)S(1)} %dynamic-slice_convert_fusion.5), channel_id=1, source_target_pairs={{0,128},{16,144},{32,160},{48,176},{64,192},{80,208},{96,224},{112... | collective-permute-start | bytes 442376 | tf_op jit(solution)/shard_map/ppermute | solution.py:226
  71.4 0.8 copy-start.6
  72.9 6.5 %collective-permute-start.7 = (bf16[1,1,1,1,48,1536]{5,4,3,2,1,0:T(8,128)(2,1)}, bf16[1,1,1,1,48,1536]{5,4,3,2,1,0:T(8,128)(2,1)}, u32[]{:S(2)}, u32[]{:S(2)}) collective-permute-start(bf16[1,1,1,1,48,1536]{5,4,3,2,1,0:T(8,128)(2,1)} %dynamic-slice_convert_fusion.4), channel_id=1, source_target_pairs={{0,128},{16,144},{32,160},{48,176},{64,192},{80,208},{96,224},{112... | collective-permute-start | bytes 442376 | tf_op jit(solution)/shard_map/ppermute | solution.py:226
  85.4 1.3 copy-start
  92.3 4.3 %collective-permute-start.8 = (bf16[384,768]{1,0:T(8,128)(2,1)S(1)}, bf16[384,768]{1,0:T(8,128)(2,1)S(1)}, u32[]{:S(2)}, u32[]{:S(2)}) collective-permute-start(bf16[384,768]{1,0:T(8,128)(2,1)S(1)} %get-tuple-element.13), channel_id=1, source_target_pairs={{0,16},{16,0},{32,48},{48,32},{64,80},{80,64},{96,112},{112,96},{1... | collective-permute-start | bytes 1769480 | tf_op jit(solution)/shard_map/ppermute | solution.py:226
  96.7 19.3 %copy-start.7 = (bf16[16,48,192]{2,0,1:T(8,128)(2,1)S(1)}, bf16[16,48,192]{2,0,1:T(8,128)(2,1)}, u32[]{:S(2)}) copy-start(bf16[16,48,192]{2,0,1:T(8,128)(2,1)} %pad_maximum_fusion) | copy-start | bytes 884740

commit v6 on v5

--- a/solution.py
+++ b/solution.py
@@ -99,44 +99,12 @@
     )(inputs, cotangent, up_weight, down_weight)
 
 
-def value_kernel(
-    core_ref, mix_ref, weighted_ref, stacked_ref, weight_ref, keep_ref, give_ref,
-    both_ref, held_ref, copied,
-):
-    groups, positions, size = stacked_ref.shape
-    step = pl.program_id(0)
-    half = held_ref.shape[2]
-
-    def copy(k):
-        part = jnp.where(k == 0, 1 - core_ref[0], core_ref[0])
-        lanes = pl.ds(pl.multiple_of(part * half, half), half)
-        return pltpu.make_async_copy(weight_ref.at[:, lanes], held_ref.at[k], copied.at[k])
-
-    @pl.when(step == 0)
-    def _():
-        copy(0).start()
-        copy(1).start()
-        blocks = positions // size
-        take = lax.broadcasted_iota(jnp.int32, (size, positions), 1) // blocks
-        spread = (take == lax.broadcasted_iota(jnp.int32, (size, positions), 0)).astype(BF16)
-        row = lax.broadcasted_iota(jnp.int32, (positions, positions), 0)
-        col = lax.broadcasted_iota(jnp.int32, (positions, positions), 1)
-        same = row % blocks == col % blocks
-        for k in range(groups):
-            wide = product(stacked_ref[k], spread, 1, 0)
-            second = jnp.where(same, wide, 0.0).astype(BF16)
-            first_mix = mix_ref[:, 0, k].reshape(positions, -1)
-            both = product(second, first_mix, 1, 0)
-            both_ref[pl.ds(k * positions, positions)] = both.astype(BF16)
-        copy(0).wait()
-
-    @pl.when(step == 1)
-    def _():
-        copy(1).wait()
-
+def value_half(both_ref, weighted_ref, weight_ref, out_ref):
     slopes = []
+    groups = weighted_ref.shape[2]
+    positions = both_ref.shape[0] // groups
     for k in range(groups):
-        mixed = product(both_ref[pl.ds(k * positions, positions)], held_ref[step], 1, 0)
+        mixed = product(both_ref[pl.ds(k * positions, positions)], weight_ref[...], 1, 0)
         sigmoid_part = 0.5 + 0.5 * jnp.tanh(0.5 * mixed)
         weighted = weighted_ref[:, 0, k].reshape(mixed.shape).astype(F32)
         slope = weighted * (sigmoid_part * (1.0 + mixed * (1.0 - sigmoid_part)))
@@ -144,51 +112,77 @@
     grad = product(jnp.concatenate(slopes, axis=0), both_ref[...], 0, 0).astype(BF16)
     size = grad.shape[0] // CHIPS
     pieces = [PIECE[2 * chip] % CHIPS for chip in range(CHIPS)]
-    grad = jnp.concatenate([grad[p * size : (p + 1) * size] for p in pieces], axis=0)
-
-    @pl.when(step == 0)
-    def _():
-        give_ref[...] = grad
-
-    @pl.when(step == 1)
-    def _():
-        keep_ref[...] = grad
-
-
-def value_grad(core, came, second_blocks, value_weight):
+    out_ref[...] = jnp.concatenate([grad[p * size : (p + 1) * size] for p in pieces], axis=0)
+
+
+def give_kernel(part_ref, mix_ref, weighted_ref, stacked_ref, weight_ref, both_ref, out_ref):
+    groups, positions, size = stacked_ref.shape
+    blocks = positions // size
+    take = lax.broadcasted_iota(jnp.int32, (size, positions), 1) // blocks
+    spread = (take == lax.broadcasted_iota(jnp.int32, (size, positions), 0)).astype(BF16)
+    row = lax.broadcasted_iota(jnp.int32, (positions, positions), 0)
+    col = lax.broadcasted_iota(jnp.int32, (positions, positions), 1)
+    same = row % blocks == col % blocks
+    for k in range(groups):
+        wide = product(stacked_ref[k], spread, 1, 0)
+        second = jnp.where(same, wide, 0.0).astype(BF16)
+        first_mix = mix_ref[:, 0, k].reshape(positions, -1)
+        both_ref[pl.ds(k * positions, positions)] = product(second, first_mix, 1, 0).astype(BF16)
+    value_half(both_ref, weighted_ref, weight_ref, out_ref)
+
+
+def keep_kernel(part_ref, both_ref, weighted_ref, weight_ref, out_ref):
+    value_half(both_ref, weighted_ref, weight_ref, out_ref)
+
+
+def value_specs(came):
     places, _, groups, tile, width = came.shape
+    half = width // 2
     positions = places * groups * tile
-    half = width // 2
-    size = second_blocks.shape[1]
+    return (
+        pl.BlockSpec((places, 1, groups, tile, width), lambda k, p: (0, 0, 0, 0, 0)),
+        pl.BlockSpec((places, 1, groups, tile, half), lambda k, p: (0, 1, 0, 0, p[0])),
+        pl.BlockSpec((positions, width), lambda k, p: (0, 0)),
+        pl.BlockSpec((width, half), lambda k, p: (0, p[0])),
+        pl.BlockSpec((half, width), lambda k, p: (0, 0)),
+        jax.ShapeDtypeStruct((positions, width), BF16),
+        jax.ShapeDtypeStruct((half, width), BF16),
+    )
+
+
+def value_given(part, came, second_blocks, value_weight):
+    mix, weighted, both, weight, out, both_shape, out_shape = value_specs(came)
+    groups, size = came.shape[2], second_blocks.shape[1]
     stacked = second_blocks.reshape(groups, -1, size, size).transpose(0, 2, 1, 3)
-    stacked = stacked.reshape(groups, positions // groups, size)
-
-    def part(e, c):
-        return jnp.where(e == 0, 1 - c[0], c[0])
-
-    whole = pl.BlockSpec((half, width), lambda e, c: (0, 0))
-    return pl.pallas_call(
-        value_kernel,
+    stacked = stacked.reshape(groups, -1, size)
+    return pl.pallas_call(
+        give_kernel,
         grid_spec=pltpu.PrefetchScalarGridSpec(
             num_scalar_prefetch=1,
-            grid=(2,),
-            in_specs=[
-                pl.BlockSpec((places, 1, groups, tile, width), lambda e, c: (0, 0, 0, 0, 0)),
-                pl.BlockSpec((places, 1, groups, tile, half), lambda e, c: (0, 1, 0, 0, part(e, c))),
-                pl.BlockSpec(stacked.shape, lambda e, c: (0, 0, 0)),
-                pl.BlockSpec(memory_space=pltpu.HBM),
-            ],
-            out_specs=[whole, whole],
-            scratch_shapes=[
-                pltpu.VMEM((positions, width), BF16),
-                pltpu.VMEM((2, width, half), BF16),
-                pltpu.SemaphoreType.DMA((2,)),
-            ],
+            grid=(1,),
+            in_specs=[mix, weighted, pl.BlockSpec(stacked.shape, lambda k, p: (0, 0, 0)), weight],
+            out_specs=[both, out],
         ),
-        out_shape=[jax.ShapeDtypeStruct((half, width), BF16)] * 2,
+        out_shape=[both_shape, out_shape],
         compiler_params=pltpu.CompilerParams(vmem_limit_bytes=SMALL_LIMIT),
-        name="value",
-    )(core, came, came, stacked, value_weight)
+        name="give",
+    )(part, came, came, stacked, value_weight)
+
+
+def value_kept(part, both, came, value_weight):
+    _, weighted, rows, weight, out, _, out_shape = value_specs(came)
+    return pl.pallas_call(
+        keep_kernel,
+        grid_spec=pltpu.PrefetchScalarGridSpec(
+            num_scalar_prefetch=1,
+            grid=(1,),
+            in_specs=[rows, weighted, weight],
+            out_specs=out,
+        ),
+        out_shape=out_shape,
+        compiler_params=pltpu.CompilerParams(vmem_limit_bytes=SMALL_LIMIT),
+        name="keep",
+    )(part, both, came, value_weight)
 
 
 def join_kernel(pieces_ref, value_ref, up_ref, down_ref, rows_ref):
@@ -222,18 +216,18 @@
     )(pieces)
 
 
-def swap(block, flip):
-    return lax.ppermute(block, "dp", [(i, i ^ flip) for i in range(16)])
-
-
-def add_swapped(keep, give, flip):
-    return keep.astype(F32) + swap(give.astype(BF16), flip).astype(F32)
-
-
-def halve(total, axis, bit, flip):
+def swap(block, flip, over):
+    return lax.ppermute(block, over, [(i, i ^ flip) for i in range(16)])
+
+
+def add_swapped(keep, give, flip, over="dp"):
+    return keep.astype(F32) + swap(give.astype(BF16), flip, over).astype(F32)
+
+
+def halve(total, axis, bit, flip, over="dp"):
     keep = lax.dynamic_slice_in_dim(total, bit, 1, axis)
     give = lax.dynamic_slice_in_dim(total, 1 - bit, 1, axis)
-    return add_swapped(keep, give, flip)
+    return add_swapped(keep, give, flip, over)
 
 
 def scatter_chips(left, right):
@@ -273,6 +267,7 @@
     width = inputs.shape[3]
     half = width // 2
     places = lax.axis_size("seq")
+    share = width // places
     core = lax.axis_index("dp") & 1
     core_arg = jnp.full((1,), core, jnp.int32)
     total_tokens = (
@@ -291,12 +286,15 @@
     down_t = halve(down_t.reshape(1, 2, half, 2 * width), 1, core, 1).reshape(1, half, 2 * width)
     up_t, down_t = scatter_chips(up_t, down_t)
 
+
+    came, up_t, down_t = lax.optimization_barrier((came, up_t, down_t))
+    both, value_give = value_given(1 - core_arg, came, second_blocks, value_weight)
+    value_keep = value_kept(core_arg, both, came, value_weight)
+    value_t = add_swapped(value_keep, value_give, 1).astype(BF16)
+
+    value_t, up_t, down_t = lax.optimization_barrier((value_t, up_t, down_t))
+    value_t = exchange(value_t.reshape(CHIPS, -1, width), "dp", same_core())
     mlp_part = pack((up_t[0], up_t[1], down_t[0]))
-
-    came, mlp_part = lax.optimization_barrier((came, mlp_part))
-    value_keep, value_give = value_grad(core_arg, came, second_blocks, value_weight)
-    value_t = add_swapped(value_keep, value_give, 1)
-    value_t = exchange(value_t.astype(BF16).reshape(CHIPS, -1, width), "dp", same_core())
     value_t = jnp.sum(value_t.astype(F32), axis=0).astype(BF16)
 
     part = exchange(jnp.concatenate([pack((value_t,)), mlp_part], axis=2), "seq")

time: 153 us -> 149 us (0.974)
  blocking collectives: 54.1 us -> 34 us
  waiting for transfers between devices: 22.5 us -> 39.1 us
  starting transfers between devices: 23 us -> 28.7 us
  local copies, waits for them, and re-layouts: 14 us -> 10.5 us
  other arithmetic: 10.3 us -> 8.73 us
    all_to_all x3 -> x2, blocking collectives: 54.1 us -> 34 us  [exchange(): lax.all_to_all(block, axis, split_axis=0, concat_axis=0, tiled=True, axis...]
    all_to_all x1 -> x2, waiting for transfers between devices: 1.84 us -> 17.9 us  [exchange(): lax.all_to_all(block, axis, split_axis=0, concat_axis=0, tiled=True, axis...]
    all_to_all x1 -> x2, starting transfers between devices: 10.1 us -> 16.6 us  [exchange(): lax.all_to_all(block, axis, split_axis=0, concat_axis=0, tiled=True, axis...]
    dynamic_slice x2 -> x1, local copies, waits for them, and re-layouts: 3.64 us -> 1.08 us  [halve(): give = lax.dynamic_slice_in_dim(total, 1 - bit, 1, axis)]
    concatenate x1 -> x0, other arithmetic: 2.19 us -> none  [pack(): return jnp.concatenate([by_place(part, places) for part in parts], axis=2)]
    unnamed x16 -> x17, local copies, waits for them, and re-layouts: 3.56 us -> 5.28 us
    convert_element_type x7 -> x6, local copies, waits for them, and re-layouts: 3.56 us -> 2.07 us  [add_swapped(): return keep.astype(F32) + swap(give.astype(BF16), flip, over).astype(F32)]
    pallas_call x1 -> x2, Pallas kernels: 5.66 us -> 4.88 us  [the longest x1 2.95 us: value_given(): pl.pallas_call(give_kernel, grid_spec=pltpu.PrefetchScalarGridSpec(num_sc...]
  transfers between devices with their start and end apart: 10 -> 11, of which waited for: 8 -> 8; matrix products, arithmetic and copies ran while one was open for 13% -> 10% of each run, Pallas kernels for 11% -> 13%
where the time goes in v6:
time: 149 us
  waiting for transfers between devices  39.1 us (26%)
  blocking collectives  34 us (23%)
  starting transfers between devices  28.7 us (19%)
  Pallas kernels  27 us (18%)
  local copies, waits for them, and re-layouts  10.5 us (7%)
  other arithmetic  8.73 us (6%)
    all_to_all x2, blocking collectives, exchange(): lax.all_to_all(block, axis, split_axis=0, concat_axis=0, tiled=True, axis...  34 us
    ppermute x9, waiting for transfers between devices, swap(): return lax.ppermute(block, over, [(i, i ^ flip) for i in range(16)])  21.2 us
    all_to_all x2, waiting for transfers between devices, exchange(): lax.all_to_all(block, axis, split_axis=0, concat_axis=0, tiled=True, axis...  17.9 us
    pallas_call x1, Pallas kernels, mlp_grads(): pl.pallas_call(mlp_kernel, grid=(units // step,), in_specs=[whole, whole,...  17.2 us
    all_to_all x2, starting transfers between devices, exchange(): lax.all_to_all(block, axis, split_axis=0, concat_axis=0, tiled=True, axis...  16.6 us
    ppermute x9, starting transfers between devices, swap(): return lax.ppermute(block, over, [(i, i ^ flip) for i in range(16)])  12 us
    add x6, other arithmetic, add_swapped(): return keep.astype(F32) + swap(give.astype(BF16), flip, over).astype(F32)  6.5 us
    unnamed x17, local copies, waits for them, and re-layouts  5.28 us
  transfers between devices with their start and end apart: 11, of which 8 were waited for; matrix products, arithmetic and copies ran while one was open for 10% of the time, Pallas kernels for 13%

profile of v6, /device:TPU:1, one launch (start us, length us, event | category | flops | bytes accessed | tf_op | source)
XLA Modules:
  0.0 148.9 jit_solution(14152117805312212855)
XLA Ops:
  0.6 4.0 %send.1 = bf16[16,2,2,32,768]{4,3,2,1,0:T(8,128)(2,1)} custom-call(bf16[1,4,256,768]{3,2,1,0:T(8,128)(2,1)} %inputs_ref.1, bf16[1,4,256,768]{3,2,1,0:T(8,128)(2,1)} %cot_ref.1, bf16[4,256,256]{2,1,0:T(8,128)(2,1)} %first_ref.1), custom_call_target="tpu_custom_call" | custom-call | tf_op jit(solution)/shard_map/send/pallas_call | solution.py:50
  4.6 10.1 %all-to-all-start = ((bf16[16,2,2,32,768]{4,3,2,1,0:T(8,128)(2,1)}), bf16[16,2,2,32,768]{4,3,2,1,0:T(8,128)(2,1)S(1)}, u32[]{:S(2)}, u32[]{:S(2)}) async-start(bf16[16,2,2,32,768]{4,3,2,1,0:T(8,128)(2,1)} %send.1), calls=%async_computation | async-start | bytes 6291456 | tf_op jit(solution)/shard_map/all_to_all | solution.py:252
  14.8 17.2 %mlp.1 = (bf16[1536,768]{1,0:T(8,128)(2,1)}, bf16[768,1536]{1,0:T(8,128)(2,1)}) custom-call(bf16[1024,768]{1,0:T(8,128)(2,1)} %bitcast.31, bf16[1024,768]{1,0:T(8,128)(2,1)} %bitcast.32, bf16[768,1536]{1,0:T(8,128)(2,1)} %up_ref.1, bf16[1536,768]{1,0:T(8,128)(2,1)} %down_ref.1), custom_call_target="tpu_custom_call" | custom-call | tf_op jit(solution)/shard_map/mlp/pallas_call | solution.py:87
  32.0 2.5 %dynamic-slice_bitcast_fusion = bf16[2,1,384,768]{3,2,0,1:T(8,128)(2,1)} fusion(bf16[2,2,384,768]{3,2,1,0:T(8,128)(2,1)} %bitcast.35, s32[]{:T(128)S(6)} %select_n.33), kind=kLoop, calls=%fused_computation.7 | loop fusion | bytes 2359300
  36.6 1.7 %collective-permute-done = bf16[2,1,384,768]{3,2,0,1:T(8,128)(2,1)} collective-permute-done((bf16[2,1,384,768]{3,2,0,1:T(8,128)(2,1)}, bf16[2,1,384,768]{3,2,0,1:T(8,128)(2,1)}, u32[]{:S(2)}, u32[]{:S(2)}) %collective-permute-start) | collective-permute-done | bytes 1179680 | tf_op jit(solution)/shard_map/ppermute | solution.py:220
  38.3 2.0 %convert_add_fusion.1 = f32[2,1,384,768]{3,2,0,1:T(8,128)S(1)} fusion(bf16[2,1,384,768]{3,2,0,1:T(8,128)(2,1)} %collective-permute-done, bf16[2,2,384,768]{3,2,1,0:T(8,128)(2,1)} %bitcast.36, s32[]{:T(128)S(6)} %select_n.32), kind=kLoop, calls=%fused_computation.1 | loop fusion | flops 1769472 | bytes 4718596 | tf_op jit(solution)/shard_map/add | solution.py:224
  42.6 1.6 %convert_add_fusion = f32[1,1,384,1536]{3,2,1,0:T(8,128)S(1)} fusion(bf16[1,1,384,1536]{3,2,1,0:T(8,128)(2,1)} %collective-permute-done.4, bf16[1,2,384,1536]{3,2,1,0:T(8,128)(2,1)S(1)} %bitcast.34, s32[]{:T(128)S(6)} %select_n.32), kind=kLoop, calls=%fused_computation | loop fusion | flops 1769472 | bytes 4718596 | tf_op jit(solution)/shard_map/add | solution.py:224
  46.6 1.9 %collective-permute-start.5 = (bf16[1,2,1,2,48,1536]{5,4,3,2,1,0:T(8,128)(2,1)}, bf16[1,2,1,2,48,1536]{5,4,3,2,1,0:T(8,128)(2,1)}, u32[]{:S(2)}, u32[]{:S(2)}) collective-permute-start(bf16[1,2,1,2,48,1536]{5,4,3,2,1,0:T(8,128)(2,1)} %dynamic-slice_convert_fusion), channel_id=1, source_target_pairs={{0,96},{16,112},{32,64},{48,80},{64,32},{80,48},{96,0},{112,16},{1... | collective-permute-start | bytes 1769480 | tf_op jit(solution)/shard_map/ppermute | solution.py:220
  49.6 6.6 %collective-permute-done.1 = bf16[2,1,2,2,48,768]{5,4,3,2,1,0:T(8,128)(2,1)} collective-permute-done((bf16[2,1,2,2,48,768]{5,4,3,2,1,0:T(8,128)(2,1)}, bf16[2,1,2,2,48,768]{5,4,3,2,1,0:T(8,128)(2,1)}, u32[]{:S(2)}, u32[]{:S(2)}) %collective-permute-start.1) | collective-permute-done | bytes 589856 | tf_op jit(solution)/shard_map/ppermute | solution.py:220
  56.2 1.6 %convert_add_fusion.3 = f32[2,1,2,2,48,768]{5,4,3,2,1,0:T(8,128)S(1)} fusion(bf16[2,1,2,2,48,768]{5,4,3,2,1,0:T(8,128)(2,1)} %collective-permute-done.1, f32[2,2,2,2,48,768]{5,4,3,2,1,0:T(8,128)} %bitcast.30, s32[]{:T(128)S(6)} %select_n.34), kind=kLoop, calls=%fused_computation.5 | loop fusion | flops 589824 | bytes 2949124 | tf_op jit(solution)/shard_map/add | solution.py:224
  57.8 2.6 %collective-permute-start.2 = (bf16[2,1,1,2,48,768]{5,4,3,2,1,0:T(8,128)(2,1)S(1)}, bf16[2,1,1,2,48,768]{5,4,3,2,1,0:T(8,128)(2,1)S(1)}, u32[]{:S(2)}, u32[]{:S(2)}) collective-permute-start(bf16[2,1,1,2,48,768]{5,4,3,2,1,0:T(8,128)(2,1)S(1)} %dynamic-slice_convert_fusion.3), channel_id=1, source_target_pairs={{0,96},{16,112},{32,64},{48,80},{64,32},{80,48},{96,0},{112,16},{1... | collective-permute-start | bytes 884744 | tf_op jit(solution)/shard_map/ppermute | solution.py:220
  60.4 1.9 %collective-permute-done.5 = bf16[1,2,1,2,48,1536]{5,4,3,2,1,0:T(8,128)(2,1)} collective-permute-done((bf16[1,2,1,2,48,1536]{5,4,3,2,1,0:T(8,128)(2,1)}, bf16[1,2,1,2,48,1536]{5,4,3,2,1,0:T(8,128)(2,1)}, u32[]{:S(2)}, u32[]{:S(2)}) %collective-permute-start.5) | collective-permute-done | bytes 589856 | tf_op jit(solution)/shard_map/ppermute | solution.py:220
  63.7 4.9 %collective-permute-done.2 = bf16[2,1,1,2,48,768]{5,4,3,2,1,0:T(8,128)(2,1)S(1)} collective-permute-done((bf16[2,1,1,2,48,768]{5,4,3,2,1,0:T(8,128)(2,1)S(1)}, bf16[2,1,1,2,48,768]{5,4,3,2,1,0:T(8,128)(2,1)S(1)}, u32[]{:S(2)}, u32[]{:S(2)}) %collective-permute-start.2) | collective-permute-done | bytes 294944 | tf_op jit(solution)/shard_map/ppermute | solution.py:220
  68.6 2.7 %collective-permute-start.3 = (bf16[2,1,1,1,48,768]{5,4,3,2,1,0:T(8,128)(2,1)S(1)}, bf16[2,1,1,1,48,768]{5,4,3,2,1,0:T(8,128)(2,1)S(1)}, u32[]{:S(2)}, u32[]{:S(2)}) collective-permute-start(bf16[2,1,1,1,48,768]{5,4,3,2,1,0:T(8,128)(2,1)S(1)} %dynamic-slice_convert_fusion.5), channel_id=1, source_target_pairs={{0,128},{16,144},{32,160},{48,176},{64,192},{80,208},{96,224},{112... | collective-permute-start | bytes 442376 | tf_op jit(solution)/shard_map/ppermute | solution.py:220
  72.5 2.0 %collective-permute-done.3 = bf16[2,1,1,1,48,768]{5,4,3,2,1,0:T(8,128)(2,1)S(1)} collective-permute-done((bf16[2,1,1,1,48,768]{5,4,3,2,1,0:T(8,128)(2,1)S(1)}, bf16[2,1,1,1,48,768]{5,4,3,2,1,0:T(8,128)(2,1)S(1)}, u32[]{:S(2)}, u32[]{:S(2)}) %collective-permute-start.3) | collective-permute-done | bytes 147488 | tf_op jit(solution)/shard_map/ppermute | solution.py:220
  74.5 4.1 %collective-permute-done.7 = bf16[1,1,1,1,48,1536]{5,4,3,2,1,0:T(8,128)(2,1)S(1)} collective-permute-done((bf16[1,1,1,1,48,1536]{5,4,3,2,1,0:T(8,128)(2,1)S(1)}, bf16[1,1,1,1,48,1536]{5,4,3,2,1,0:T(8,128)(2,1)S(1)}, u32[]{:S(2)}, u32[]{:S(2)}) %collective-permute-start.7) | collective-permute-done | bytes 147488 | tf_op jit(solution)/shard_map/ppermute | solution.py:220
  79.3 6.1 %all-to-all-done.mix_ref.weighted_ref = bf16[16,2,2,32,768]{4,3,2,1,0:T(8,128)(2,1)S(1)} async-done(((bf16[16,2,2,32,768]{4,3,2,1,0:T(8,128)(2,1)}), bf16[16,2,2,32,768]{4,3,2,1,0:T(8,128)(2,1)S(1)}, u32[]{:S(2)}, u32[]{:S(2)}) %all-to-all-start) | async-done | bytes 3145760 | tf_op jit(solution)/shard_map/all_to_all | solution.py:252
  86.6 3.0 %give.1 = (bf16[1024,768]{1,0:T(8,128)(2,1)S(1)}, bf16[384,768]{1,0:T(8,128)(2,1)S(1)}) custom-call(s32[1]{0:T(128)S(6)} %sub.19.part_ref, bf16[16,2,2,32,768]{4,3,2,1,0:T(8,128)(2,1)S(1)} %all-to-all-done.mix_ref.weighted_ref, bf16[16,2,2,32,768]{4,3,2,1,0:T(8,128)(2,1)S(1)} %all-to-all-done.mix_ref.weighted_ref, bf16[2,512,64]{2,1,0:T(8,128)(2,1)S(1)} %bitcast.26, ...), custom_call_target="tpu_custom_call" | custom-call | tf_op jit(solution)/shard_map/give/pallas_call | solution.py:158
  89.6 1.6 %collective-permute-start.8 = (bf16[384,768]{1,0:T(8,128)(2,1)S(1)}, bf16[384,768]{1,0:T(8,128)(2,1)S(1)}, u32[]{:S(2)}, u32[]{:S(2)}) collective-permute-start(bf16[384,768]{1,0:T(8,128)(2,1)S(1)} %get-tuple-element.17), channel_id=1, source_target_pairs={{0,16},{16,0},{32,48},{48,32},{64,80},{80,64},{96,112},{112,96},{1... | collective-permute-start | bytes 1769480 | tf_op jit(solution)/shard_map/ppermute | solution.py:220
  91.2 1.9 %keep.1 = bf16[384,768]{1,0:T(8,128)(2,1)S(1)} custom-call(s32[1]{0:T(128)} %bitcast.part_ref, bf16[1024,768]{1,0:T(8,128)(2,1)S(1)} %get-tuple-element.16.both_ref, bf16[16,2,2,32,768]{4,3,2,1,0:T(8,128)(2,1)S(1)} %all-to-all-done.mix_ref.weighted_ref, bf16[768,768]{1,0:T(8,128)(2,1)S(1)} %copy-done.1), custom_call_target="tpu_custom_call" | custom-call | tf_op jit(solution)/shard_map/keep/pallas_call | solution.py:174
  94.1 6.5 %all-to-all-start.1 = ((bf16[8,48,768]{2,1,0:T(8,128)(2,1)}), bf16[8,48,768]{2,1,0:T(8,128)(2,1)S(1)}, u32[]{:S(2)}, u32[]{:S(2)}) async-start(bf16[8,48,768]{2,1,0:T(8,128)(2,1)} %bitcast.12), calls=%async_computation.1 | async-start | bytes 1179648 | tf_op jit(solution)/shard_map/all_to_all | solution.py:252
  101.2 11.8 %all-to-all-done.1 = bf16[8,48,768]{2,1,0:T(8,128)(2,1)S(1)} async-done(((bf16[8,48,768]{2,1,0:T(8,128)(2,1)}), bf16[8,48,768]{2,1,0:T(8,128)(2,1)S(1)}, u32[]{:S(2)}, u32[]{:S(2)}) %all-to-all-start.1) | async-done | bytes 589856 | tf_op jit(solution)/shard_map/all_to_all | solution.py:252
  113.9 18.9 %all_to_all.20 = bf16[16,48,240]{2,1,0:T(8,128)(2,1)S(1)} all-to-all(bf16[16,48,240]{2,1,0:T(8,128)(2,1)S(1)} %copy.17), channel_id=1, replica_groups=mesh['dp'=16,'seq'=16] {'seq'}, dimensions={0} | all-to-all | bytes 737280 | tf_op jit(solution)/shard_map/all_to_all | solution.py:252
  133.0 15.1 %all_to_all.21.pieces_ref = bf16[16,48,240]{2,1,0:T(8,128)(2,1)S(1)} all-to-all(bf16[16,48,240]{2,1,0:T(8,128)(2,1)S(1)} %broadcast_in_dim.10), channel_id=1, replica_groups=mesh['dp'=16,'seq'=16] {'dp'}, dimensions={0} | all-to-all | bytes 737280 | tf_op jit(solution)/shard_map/all_to_all | solution.py:252
  (50 shorter events, 15.7 us)
Async XLA Ops:
  4.6 80.7 %all-to-all-start = ((bf16[16,2,2,32,768]{4,3,2,1,0:T(8,128)(2,1)}), bf16[16,2,2,32,768]{4,3,2,1,0:T(8,128)(2,1)S(1)}, u32[]{:S(2)}, u32[]{:S(2)}) async-start(bf16[16,2,2,32,768]{4,3,2,1,0:T(8,128)(2,1)} %send.1), calls=%async_computation | async-start | bytes 6291456 | tf_op jit(solution)/shard_map/all_to_all | solution.py:252
  32.0 3.5 %copy-start.5 = (bf16[768,1536]{1,0:T(8,128)(2,1)S(1)}, bf16[768,1536]{1,0:T(8,128)(2,1)}, u32[]{:S(2)}) copy-start(bf16[768,1536]{1,0:T(8,128)(2,1)} %get-tuple-element.14) | copy-start | bytes 7077892
  34.5 3.8 %collective-permute-start = (bf16[2,1,384,768]{3,2,0,1:T(8,128)(2,1)}, bf16[2,1,384,768]{3,2,0,1:T(8,128)(2,1)}, u32[]{:S(2)}, u32[]{:S(2)}) collective-permute-start(bf16[2,1,384,768]{3,2,0,1:T(8,128)(2,1)} %dynamic-slice_bitcast_fusion), channel_id=1, source_target_pairs={{0,16},{16,0},{32,48},{48,32},{64,80},{80,64},{96,112},{112,96},{1... | collective-permute-start | bytes 3538952 | tf_op jit(solution)/shard_map/ppermute | solution.py:220
  36.6 6.0 %collective-permute-start.4 = (bf16[1,1,384,1536]{3,2,1,0:T(8,128)(2,1)}, bf16[1,1,384,1536]{3,2,1,0:T(8,128)(2,1)}, u32[]{:S(2)}, u32[]{:S(2)}) collective-permute-start(bf16[1,1,384,1536]{3,2,1,0:T(8,128)(2,1)} %constant_dynamic-slice_fusion), channel_id=1, source_target_pairs={{0,16},{16,0},{32,48},{48,32},{64,80},{80,64},{96,112},{112,96},{1... | collective-permute-start | bytes 3538952 | tf_op jit(solution)/shard_map/ppermute | solution.py:220
  38.3 4.3 %copy-start.6 = (bf16[768,1536]{1,0:T(8,128)(2,1)S(1)}, bf16[768,1536]{1,0:T(8,128)(2,1)}, u32[]{:S(2)}) copy-start(bf16[768,1536]{1,0:T(8,128)(2,1)} %get-tuple-element.14) | copy-start | bytes 7077892
  40.3 2.2 %copy-start.4 = (f32[2,1,384,768]{3,2,0,1:T(8,128)}, f32[2,1,384,768]{3,2,0,1:T(8,128)S(1)}, u32[]{:S(2)}) copy-start(f32[2,1,384,768]{3,2,0,1:T(8,128)S(1)} %convert_add_fusion.1) | copy-start | bytes 7077892
  41.4 14.9 %collective-permute-start.1 = (bf16[2,1,2,2,48,768]{5,4,3,2,1,0:T(8,128)(2,1)}, bf16[2,1,2,2,48,768]{5,4,3,2,1,0:T(8,128)(2,1)}, u32[]{:S(2)}, u32[]{:S(2)}) collective-permute-start(bf16[2,1,2,2,48,768]{5,4,3,2,1,0:T(8,128)(2,1)} %dynamic-slice_convert_fusion.1), channel_id=1, source_target_pairs={{0,32},{16,48},{32,0},{48,16},{64,96},{80,112},{96,64},{112,80},{1... | collective-permute-start | bytes 1769480 | tf_op jit(solution)/shard_map/ppermute | solution.py:220
  44.2 1.5 copy-start.2
  46.6 15.7 %collective-permute-start.5 = (bf16[1,2,1,2,48,1536]{5,4,3,2,1,0:T(8,128)(2,1)}, bf16[1,2,1,2,48,1536]{5,4,3,2,1,0:T(8,128)(2,1)}, u32[]{:S(2)}, u32[]{:S(2)}) collective-permute-start(bf16[1,2,1,2,48,1536]{5,4,3,2,1,0:T(8,128)(2,1)} %dynamic-slice_convert_fusion), channel_id=1, source_target_pairs={{0,96},{16,112},{32,64},{48,80},{64,32},{80,48},{96,0},{112,16},{1... | collective-permute-start | bytes 1769480 | tf_op jit(solution)/shard_map/ppermute | solution.py:220
  49.6 12.8 %copy-start.3 = (f32[1,1,384,1536]{3,2,1,0:T(8,128)S(1)}, f32[1,1,384,1536]{3,2,1,0:T(8,128)}, u32[]{:S(2)}) copy-start(f32[1,1,384,1536]{3,2,1,0:T(8,128)} %copy-done.2) | copy-start | bytes 7077892
  57.8 10.7 %collective-permute-start.2 = (bf16[2,1,1,2,48,768]{5,4,3,2,1,0:T(8,128)(2,1)S(1)}, bf16[2,1,1,2,48,768]{5,4,3,2,1,0:T(8,128)(2,1)S(1)}, u32[]{:S(2)}, u32[]{:S(2)}) collective-permute-start(bf16[2,1,1,2,48,768]{5,4,3,2,1,0:T(8,128)(2,1)S(1)} %dynamic-slice_convert_fusion.3), channel_id=1, source_target_pairs={{0,96},{16,112},{32,64},{48,80},{64,32},{80,48},{96,0},{112,16},{1... | collective-permute-start | bytes 884744 | tf_op jit(solution)/shard_map/ppermute | solution.py:220
  63.6 7.8 %collective-permute-start.6 = (bf16[1,1,1,2,48,1536]{5,4,3,2,1,0:T(8,128)(2,1)S(1)}, bf16[1,1,1,2,48,1536]{5,4,3,2,1,0:T(8,128)(2,1)S(1)}, u32[]{:S(2)}, u32[]{:S(2)}) collective-permute-start(bf16[1,1,1,2,48,1536]{5,4,3,2,1,0:T(8,128)(2,1)S(1)} %dynamic-slice_convert_fusion.2), channel_id=1, source_target_pairs={{0,32},{16,48},{32,0},{48,16},{64,96},{80,112},{96,64},{112,80},{1... | collective-permute-start | bytes 884744 | tf_op jit(solution)/shard_map/ppermute | solution.py:220
  68.6 5.9 %collective-permute-start.3 = (bf16[2,1,1,1,48,768]{5,4,3,2,1,0:T(8,128)(2,1)S(1)}, bf16[2,1,1,1,48,768]{5,4,3,2,1,0:T(8,128)(2,1)S(1)}, u32[]{:S(2)}, u32[]{:S(2)}) collective-permute-start(bf16[2,1,1,1,48,768]{5,4,3,2,1,0:T(8,128)(2,1)S(1)} %dynamic-slice_convert_fusion.5), channel_id=1, source_target_pairs={{0,128},{16,144},{32,160},{48,176},{64,192},{80,208},{96,224},{112... | collective-permute-start | bytes 442376 | tf_op jit(solution)/shard_map/ppermute | solution.py:220
  71.4 7.2 %collective-permute-start.7 = (bf16[1,1,1,1,48,1536]{5,4,3,2,1,0:T(8,128)(2,1)S(1)}, bf16[1,1,1,1,48,1536]{5,4,3,2,1,0:T(8,128)(2,1)S(1)}, u32[]{:S(2)}, u32[]{:S(2)}) collective-permute-start(bf16[1,1,1,1,48,1536]{5,4,3,2,1,0:T(8,128)(2,1)S(1)} %dynamic-slice_convert_fusion.4), channel_id=1, source_target_pairs={{0,128},{16,144},{32,160},{48,176},{64,192},{80,208},{96,224},{112... | collective-permute-start | bytes 442376 | tf_op jit(solution)/shard_map/ppermute | solution.py:220
  85.4 1.3 copy-start
  86.6 4.6 %copy-start.1 = (bf16[768,768]{1,0:T(8,128)(2,1)S(1)}, bf16[768,768]{1,0:T(8,128)(2,1)}, u32[]{:S(2)}) copy-start(bf16[768,768]{1,0:T(8,128)(2,1)} %weight_ref.3) | copy-start | bytes 3538948
  89.6 3.5 %collective-permute-start.8 = (bf16[384,768]{1,0:T(8,128)(2,1)S(1)}, bf16[384,768]{1,0:T(8,128)(2,1)S(1)}, u32[]{:S(2)}, u32[]{:S(2)}) collective-permute-start(bf16[384,768]{1,0:T(8,128)(2,1)S(1)} %get-tuple-element.17), channel_id=1, source_target_pairs={{0,16},{16,0},{32,48},{48,32},{64,80},{80,64},{96,112},{112,96},{1... | collective-permute-start | bytes 1769480 | tf_op jit(solution)/shard_map/ppermute | solution.py:220
  94.1 7.0 %copy-start.7 = (bf16[1,48,1536]{2,1,0:T(8,128)(2,1)S(1)}, bf16[1,48,1536]{2,1,0:T(8,128)(2,1)}, u32[]{:S(2)}) copy-start(bf16[1,48,1536]{2,1,0:T(8,128)(2,1)} %fusion.1) | copy-start | bytes 442372
  94.1 19.0 %all-to-all-start.1 = ((bf16[8,48,768]{2,1,0:T(8,128)(2,1)}), bf16[8,48,768]{2,1,0:T(8,128)(2,1)S(1)}, u32[]{:S(2)}, u32[]{:S(2)}) async-start(bf16[8,48,768]{2,1,0:T(8,128)(2,1)} %bitcast.12), calls=%async_computation.1 | async-start | bytes 1179648 | tf_op jit(solution)/shard_map/all_to_all | solution.py:252

commit v7 on v6

--- a/solution.py
+++ b/solution.py
@@ -105,7 +105,7 @@
     positions = both_ref.shape[0] // groups
     for k in range(groups):
         mixed = product(both_ref[pl.ds(k * positions, positions)], weight_ref[...], 1, 0)
-        sigmoid_part = 0.5 + 0.5 * jnp.tanh(0.5 * mixed)
+        sigmoid_part = jax.nn.sigmoid(mixed)
         weighted = weighted_ref[:, 0, k].reshape(mixed.shape).astype(F32)
         slope = weighted * (sigmoid_part * (1.0 + mixed * (1.0 - sigmoid_part)))
         slopes.append(slope.astype(BF16))
@@ -115,7 +115,7 @@
     out_ref[...] = jnp.concatenate([grad[p * size : (p + 1) * size] for p in pieces], axis=0)
 
 
-def give_kernel(part_ref, mix_ref, weighted_ref, stacked_ref, weight_ref, both_ref, out_ref):
+def mix_kernel(mix_ref, stacked_ref, both_ref):
     groups, positions, size = stacked_ref.shape
     blocks = positions // size
     take = lax.broadcasted_iota(jnp.int32, (size, positions), 1) // blocks
@@ -128,60 +128,49 @@
         second = jnp.where(same, wide, 0.0).astype(BF16)
         first_mix = mix_ref[:, 0, k].reshape(positions, -1)
         both_ref[pl.ds(k * positions, positions)] = product(second, first_mix, 1, 0).astype(BF16)
+
+
+def half_kernel(part_ref, both_ref, weighted_ref, weight_ref, out_ref):
     value_half(both_ref, weighted_ref, weight_ref, out_ref)
 
 
-def keep_kernel(part_ref, both_ref, weighted_ref, weight_ref, out_ref):
-    value_half(both_ref, weighted_ref, weight_ref, out_ref)
-
-
-def value_specs(came):
+def second_mix(came, second_blocks):
+    places, _, groups, tile, width = came.shape
+    size = second_blocks.shape[1]
+    stacked = second_blocks.reshape(groups, -1, size, size).transpose(0, 2, 1, 3)
+    stacked = stacked.reshape(groups, -1, size)
+    return pl.pallas_call(
+        mix_kernel,
+        grid=(1,),
+        in_specs=[
+            pl.BlockSpec((places, 1, groups, tile, width), lambda k: (0, 0, 0, 0, 0)),
+            pl.BlockSpec(stacked.shape, lambda k: (0, 0, 0)),
+        ],
+        out_specs=pl.BlockSpec((places * groups * tile, width), lambda k: (0, 0)),
+        out_shape=jax.ShapeDtypeStruct((places * groups * tile, width), BF16),
+        compiler_params=pltpu.CompilerParams(vmem_limit_bytes=SMALL_LIMIT),
+        name="mix",
+    )(came, stacked)
+
+
+def value_part(part, both, came, value_weight):
     places, _, groups, tile, width = came.shape
     half = width // 2
-    positions = places * groups * tile
-    return (
-        pl.BlockSpec((places, 1, groups, tile, width), lambda k, p: (0, 0, 0, 0, 0)),
-        pl.BlockSpec((places, 1, groups, tile, half), lambda k, p: (0, 1, 0, 0, p[0])),
-        pl.BlockSpec((positions, width), lambda k, p: (0, 0)),
-        pl.BlockSpec((width, half), lambda k, p: (0, p[0])),
-        pl.BlockSpec((half, width), lambda k, p: (0, 0)),
-        jax.ShapeDtypeStruct((positions, width), BF16),
-        jax.ShapeDtypeStruct((half, width), BF16),
-    )
-
-
-def value_given(part, came, second_blocks, value_weight):
-    mix, weighted, both, weight, out, both_shape, out_shape = value_specs(came)
-    groups, size = came.shape[2], second_blocks.shape[1]
-    stacked = second_blocks.reshape(groups, -1, size, size).transpose(0, 2, 1, 3)
-    stacked = stacked.reshape(groups, -1, size)
-    return pl.pallas_call(
-        give_kernel,
+    return pl.pallas_call(
+        half_kernel,
         grid_spec=pltpu.PrefetchScalarGridSpec(
             num_scalar_prefetch=1,
             grid=(1,),
-            in_specs=[mix, weighted, pl.BlockSpec(stacked.shape, lambda k, p: (0, 0, 0)), weight],
-            out_specs=[both, out],
+            in_specs=[
+                pl.BlockSpec(both.shape, lambda k, p: (0, 0)),
+                pl.BlockSpec((places, 1, groups, tile, half), lambda k, p: (0, 1, 0, 0, p[0])),
+                pl.BlockSpec((width, half), lambda k, p: (0, p[0])),
+            ],
+            out_specs=pl.BlockSpec((half, width), lambda k, p: (0, 0)),
         ),
-        out_shape=[both_shape, out_shape],
+        out_shape=jax.ShapeDtypeStruct((half, width), BF16),
         compiler_params=pltpu.CompilerParams(vmem_limit_bytes=SMALL_LIMIT),
-        name="give",
-    )(part, came, came, stacked, value_weight)
-
-
-def value_kept(part, both, came, value_weight):
-    _, weighted, rows, weight, out, _, out_shape = value_specs(came)
-    return pl.pallas_call(
-        keep_kernel,
-        grid_spec=pltpu.PrefetchScalarGridSpec(
-            num_scalar_prefetch=1,
-            grid=(1,),
-            in_specs=[rows, weighted, weight],
-            out_specs=out,
-        ),
-        out_shape=out_shape,
-        compiler_params=pltpu.CompilerParams(vmem_limit_bytes=SMALL_LIMIT),
-        name="keep",
+        name="half",
     )(part, both, came, value_weight)
 
 
@@ -278,9 +267,10 @@
     def pack(parts):
         return jnp.concatenate([by_place(part, places) for part in parts], axis=2)
 
-    came = exchange(build_sent(inputs, cotangent, first_blocks, places), "seq")
-
-    flat = inputs.reshape(-1, width)
+    sent = build_sent(inputs, cotangent, first_blocks, places)
+    sent, flat = lax.optimization_barrier((sent, inputs.reshape(-1, width)))
+    came = exchange(sent, "seq")
+
     up_t, down_t = mlp_grads(flat, cotangent.reshape(-1, width), up_weight, down_weight)
     up_t = halve(up_t.reshape(2, 2, half, width), 1, core, 1).reshape(2, half, width)
     down_t = halve(down_t.reshape(1, 2, half, 2 * width), 1, core, 1).reshape(1, half, 2 * width)
@@ -288,8 +278,9 @@
 
 
     came, up_t, down_t = lax.optimization_barrier((came, up_t, down_t))
-    both, value_give = value_given(1 - core_arg, came, second_blocks, value_weight)
-    value_keep = value_kept(core_arg, both, came, value_weight)
+    both = second_mix(came, second_blocks)
+    value_give = value_part(1 - core_arg, both, came, value_weight)
+    value_keep = value_part(core_arg, both, came, value_weight)
     value_t = add_swapped(value_keep, value_give, 1).astype(BF16)
 
     value_t, up_t, down_t = lax.optimization_barrier((value_t, up_t, down_t))

time: 149 us -> 148 us (level)
    unnamed x17 -> x15, local copies, waits for them, and re-layouts: 5.28 us -> 4.04 us
    pallas_call x2 -> x3, Pallas kernels: 4.88 us -> 5.16 us  [the longest x2 3.81 us: value_part(): pl.pallas_call(half_kernel, grid_spec=pltpu.PrefetchScalarGridSpec(num_sc...]
where the time goes in v7:
time: 148 us
  waiting for transfers between devices  39.1 us (26%)
  blocking collectives  34 us (23%)
  starting transfers between devices  28.7 us (19%)
  Pallas kernels  27.3 us (18%)
  local copies, waits for them, and re-layouts  9.27 us (6%)
  other arithmetic  8.72 us (6%)
    all_to_all x2, blocking collectives, exchange(): lax.all_to_all(block, axis, split_axis=0, concat_axis=0, tiled=True, axis...  34 us
    ppermute x9, waiting for transfers between devices, swap(): return lax.ppermute(block, over, [(i, i ^ flip) for i in range(16)])  21.2 us
    all_to_all x2, waiting for transfers between devices, exchange(): lax.all_to_all(block, axis, split_axis=0, concat_axis=0, tiled=True, axis...  17.9 us
    pallas_call x1, Pallas kernels, mlp_grads(): pl.pallas_call(mlp_kernel, grid=(units // step,), in_specs=[whole, whole,...  17.2 us
    all_to_all x2, starting transfers between devices, exchange(): lax.all_to_all(block, axis, split_axis=0, concat_axis=0, tiled=True, axis...  16.6 us
    ppermute x9, starting transfers between devices, swap(): return lax.ppermute(block, over, [(i, i ^ flip) for i in range(16)])  12 us
    add x6, other arithmetic, add_swapped(): return keep.astype(F32) + swap(give.astype(BF16), flip, over).astype(F32)  6.5 us
    unnamed x15, local copies, waits for them, and re-layouts  4.04 us
  transfers between devices with their start and end apart: 11, of which 8 were waited for; matrix products, arithmetic and copies ran while one was open for 10% of the time, Pallas kernels for 13%

profile of v7, /device:TPU:1, one launch (start us, length us, event | category | flops | bytes accessed | tf_op | source)
XLA Modules:
  0.0 147.9 jit_solution(1219494786660192071)
XLA Ops:
  0.6 4.0 %send.1 = bf16[16,2,2,32,768]{4,3,2,1,0:T(8,128)(2,1)} custom-call(bf16[1,4,256,768]{3,2,1,0:T(8,128)(2,1)} %inputs_ref.1, bf16[1,4,256,768]{3,2,1,0:T(8,128)(2,1)} %cot_ref.1, bf16[4,256,256]{2,1,0:T(8,128)(2,1)} %first_ref.1), custom_call_target="tpu_custom_call" | custom-call | tf_op jit(solution)/shard_map/send/pallas_call | solution.py:50
  4.6 10.1 %all-to-all-start = ((bf16[16,2,2,32,768]{4,3,2,1,0:T(8,128)(2,1)}), bf16[16,2,2,32,768]{4,3,2,1,0:T(8,128)(2,1)S(1)}, u32[]{:S(2)}, u32[]{:S(2)}) async-start(bf16[16,2,2,32,768]{4,3,2,1,0:T(8,128)(2,1)} %send.1), calls=%async_computation | async-start | bytes 6291456 | tf_op jit(solution)/shard_map/all_to_all | solution.py:241
  14.8 17.2 %mlp.1 = (bf16[1536,768]{1,0:T(8,128)(2,1)}, bf16[768,1536]{1,0:T(8,128)(2,1)}) custom-call(bf16[1024,768]{1,0:T(8,128)(2,1)} %bitcast.31, bf16[1024,768]{1,0:T(8,128)(2,1)} %bitcast.32, bf16[768,1536]{1,0:T(8,128)(2,1)} %up_ref.1, bf16[1536,768]{1,0:T(8,128)(2,1)} %down_ref.1), custom_call_target="tpu_custom_call" | custom-call | tf_op jit(solution)/shard_map/mlp/pallas_call | solution.py:87
  32.0 2.6 %dynamic-slice_bitcast_fusion = bf16[2,1,384,768]{3,2,0,1:T(8,128)(2,1)} fusion(bf16[2,2,384,768]{3,2,1,0:T(8,128)(2,1)} %bitcast.35, s32[]{:T(128)S(6)} %select_n.33), kind=kLoop, calls=%fused_computation.7 | loop fusion | bytes 2359300
  36.6 1.7 %collective-permute-done = bf16[2,1,384,768]{3,2,0,1:T(8,128)(2,1)} collective-permute-done((bf16[2,1,384,768]{3,2,0,1:T(8,128)(2,1)}, bf16[2,1,384,768]{3,2,0,1:T(8,128)(2,1)}, u32[]{:S(2)}, u32[]{:S(2)}) %collective-permute-start) | collective-permute-done | bytes 1179680 | tf_op jit(solution)/shard_map/ppermute | solution.py:209
  38.3 2.0 %convert_add_fusion.1 = f32[2,1,384,768]{3,2,0,1:T(8,128)S(1)} fusion(bf16[2,1,384,768]{3,2,0,1:T(8,128)(2,1)} %collective-permute-done, bf16[2,2,384,768]{3,2,1,0:T(8,128)(2,1)} %bitcast.36, s32[]{:T(128)S(6)} %select_n.32), kind=kLoop, calls=%fused_computation.1 | loop fusion | flops 1769472 | bytes 4718596 | tf_op jit(solution)/shard_map/add | solution.py:213
  42.6 1.6 %convert_add_fusion = f32[1,1,384,1536]{3,2,1,0:T(8,128)S(1)} fusion(bf16[1,1,384,1536]{3,2,1,0:T(8,128)(2,1)} %collective-permute-done.4, bf16[1,2,384,1536]{3,2,1,0:T(8,128)(2,1)S(1)} %bitcast.34, s32[]{:T(128)S(6)} %select_n.32), kind=kLoop, calls=%fused_computation | loop fusion | flops 1769472 | bytes 4718596 | tf_op jit(solution)/shard_map/add | solution.py:213
  46.6 1.9 %collective-permute-start.5 = (bf16[1,2,1,2,48,1536]{5,4,3,2,1,0:T(8,128)(2,1)}, bf16[1,2,1,2,48,1536]{5,4,3,2,1,0:T(8,128)(2,1)}, u32[]{:S(2)}, u32[]{:S(2)}) collective-permute-start(bf16[1,2,1,2,48,1536]{5,4,3,2,1,0:T(8,128)(2,1)} %dynamic-slice_convert_fusion), channel_id=1, source_target_pairs={{0,96},{16,112},{32,64},{48,80},{64,32},{80,48},{96,0},{112,16},{1... | collective-permute-start | bytes 1769480 | tf_op jit(solution)/shard_map/ppermute | solution.py:209
  49.6 6.6 %collective-permute-done.1 = bf16[2,1,2,2,48,768]{5,4,3,2,1,0:T(8,128)(2,1)} collective-permute-done((bf16[2,1,2,2,48,768]{5,4,3,2,1,0:T(8,128)(2,1)}, bf16[2,1,2,2,48,768]{5,4,3,2,1,0:T(8,128)(2,1)}, u32[]{:S(2)}, u32[]{:S(2)}) %collective-permute-start.1) | collective-permute-done | bytes 589856 | tf_op jit(solution)/shard_map/ppermute | solution.py:209
  56.2 1.6 %convert_add_fusion.3 = f32[2,1,2,2,48,768]{5,4,3,2,1,0:T(8,128)S(1)} fusion(bf16[2,1,2,2,48,768]{5,4,3,2,1,0:T(8,128)(2,1)} %collective-permute-done.1, f32[2,2,2,2,48,768]{5,4,3,2,1,0:T(8,128)} %bitcast.30, s32[]{:T(128)S(6)} %select_n.34), kind=kLoop, calls=%fused_computation.5 | loop fusion | flops 589824 | bytes 2949124 | tf_op jit(solution)/shard_map/add | solution.py:213
  57.8 2.6 %collective-permute-start.2 = (bf16[2,1,1,2,48,768]{5,4,3,2,1,0:T(8,128)(2,1)S(1)}, bf16[2,1,1,2,48,768]{5,4,3,2,1,0:T(8,128)(2,1)S(1)}, u32[]{:S(2)}, u32[]{:S(2)}) collective-permute-start(bf16[2,1,1,2,48,768]{5,4,3,2,1,0:T(8,128)(2,1)S(1)} %dynamic-slice_convert_fusion.3), channel_id=1, source_target_pairs={{0,96},{16,112},{32,64},{48,80},{64,32},{80,48},{96,0},{112,16},{1... | collective-permute-start | bytes 884744 | tf_op jit(solution)/shard_map/ppermute | solution.py:209
  60.4 2.0 %collective-permute-done.5 = bf16[1,2,1,2,48,1536]{5,4,3,2,1,0:T(8,128)(2,1)} collective-permute-done((bf16[1,2,1,2,48,1536]{5,4,3,2,1,0:T(8,128)(2,1)}, bf16[1,2,1,2,48,1536]{5,4,3,2,1,0:T(8,128)(2,1)}, u32[]{:S(2)}, u32[]{:S(2)}) %collective-permute-start.5) | collective-permute-done | bytes 589856 | tf_op jit(solution)/shard_map/ppermute | solution.py:209
  63.7 4.9 %collective-permute-done.2 = bf16[2,1,1,2,48,768]{5,4,3,2,1,0:T(8,128)(2,1)S(1)} collective-permute-done((bf16[2,1,1,2,48,768]{5,4,3,2,1,0:T(8,128)(2,1)S(1)}, bf16[2,1,1,2,48,768]{5,4,3,2,1,0:T(8,128)(2,1)S(1)}, u32[]{:S(2)}, u32[]{:S(2)}) %collective-permute-start.2) | collective-permute-done | bytes 294944 | tf_op jit(solution)/shard_map/ppermute | solution.py:209
  68.7 2.7 %collective-permute-start.3 = (bf16[2,1,1,1,48,768]{5,4,3,2,1,0:T(8,128)(2,1)S(1)}, bf16[2,1,1,1,48,768]{5,4,3,2,1,0:T(8,128)(2,1)S(1)}, u32[]{:S(2)}, u32[]{:S(2)}) collective-permute-start(bf16[2,1,1,1,48,768]{5,4,3,2,1,0:T(8,128)(2,1)S(1)} %dynamic-slice_convert_fusion.5), channel_id=1, source_target_pairs={{0,128},{16,144},{32,160},{48,176},{64,192},{80,208},{96,224},{112... | collective-permute-start | bytes 442376 | tf_op jit(solution)/shard_map/ppermute | solution.py:209
  72.6 2.0 %collective-permute-done.3 = bf16[2,1,1,1,48,768]{5,4,3,2,1,0:T(8,128)(2,1)S(1)} collective-permute-done((bf16[2,1,1,1,48,768]{5,4,3,2,1,0:T(8,128)(2,1)S(1)}, bf16[2,1,1,1,48,768]{5,4,3,2,1,0:T(8,128)(2,1)S(1)}, u32[]{:S(2)}, u32[]{:S(2)}) %collective-permute-start.3) | collective-permute-done | bytes 147488 | tf_op jit(solution)/shard_map/ppermute | solution.py:209
  74.6 4.1 %collective-permute-done.7 = bf16[1,1,1,1,48,1536]{5,4,3,2,1,0:T(8,128)(2,1)S(1)} collective-permute-done((bf16[1,1,1,1,48,1536]{5,4,3,2,1,0:T(8,128)(2,1)S(1)}, bf16[1,1,1,1,48,1536]{5,4,3,2,1,0:T(8,128)(2,1)S(1)}, u32[]{:S(2)}, u32[]{:S(2)}) %collective-permute-start.7) | collective-permute-done | bytes 147488 | tf_op jit(solution)/shard_map/ppermute | solution.py:209
  79.3 6.0 %all-to-all-done.mix_ref.weighted_ref = bf16[16,2,2,32,768]{4,3,2,1,0:T(8,128)(2,1)S(1)} async-done(((bf16[16,2,2,32,768]{4,3,2,1,0:T(8,128)(2,1)}), bf16[16,2,2,32,768]{4,3,2,1,0:T(8,128)(2,1)S(1)}, u32[]{:S(2)}, u32[]{:S(2)}) %all-to-all-start) | async-done | bytes 3145760 | tf_op jit(solution)/shard_map/all_to_all | solution.py:241
  86.8 1.9 %half.3 = bf16[384,768]{1,0:T(8,128)(2,1)S(1)} custom-call(s32[1]{0:T(128)S(6)} %sub.23.part_ref, bf16[1024,768]{1,0:T(8,128)(2,1)S(1)} %mix.1.both_ref, bf16[16,2,2,32,768]{4,3,2,1,0:T(8,128)(2,1)S(1)} %all-to-all-done.mix_ref.weighted_ref, bf16[768,768]{1,0:T(8,128)(2,1)S(1)} %copy-done), custom_call_target="tpu_custom_call" | custom-call | tf_op jit(solution)/shard_map/half/pallas_call | solution.py:159
  88.7 1.6 %collective-permute-start.8 = (bf16[384,768]{1,0:T(8,128)(2,1)S(1)}, bf16[384,768]{1,0:T(8,128)(2,1)S(1)}, u32[]{:S(2)}, u32[]{:S(2)}) collective-permute-start(bf16[384,768]{1,0:T(8,128)(2,1)S(1)} %half.3), channel_id=1, source_target_pairs={{0,16},{16,0},{32,48},{48,32},{64,80},{80,64},{96,112},{112,96},{1... | collective-permute-start | bytes 1769480 | tf_op jit(solution)/shard_map/ppermute | solution.py:209
  90.2 1.9 %half.2 = bf16[384,768]{1,0:T(8,128)(2,1)S(1)} custom-call(s32[1]{0:T(128)} %bitcast.part_ref, bf16[1024,768]{1,0:T(8,128)(2,1)S(1)} %mix.1.both_ref, bf16[16,2,2,32,768]{4,3,2,1,0:T(8,128)(2,1)S(1)} %all-to-all-done.mix_ref.weighted_ref, bf16[768,768]{1,0:T(8,128)(2,1)S(1)} %copy-done), custom_call_target="tpu_custom_call" | custom-call | tf_op jit(solution)/shard_map/half/pallas_call | solution.py:159
  93.1 6.5 %all-to-all-start.1 = ((bf16[8,48,768]{2,1,0:T(8,128)(2,1)}), bf16[8,48,768]{2,1,0:T(8,128)(2,1)S(1)}, u32[]{:S(2)}, u32[]{:S(2)}) async-start(bf16[8,48,768]{2,1,0:T(8,128)(2,1)} %bitcast.12), calls=%async_computation.1 | async-start | bytes 1179648 | tf_op jit(solution)/shard_map/all_to_all | solution.py:241
  100.3 11.8 %all-to-all-done.1 = bf16[8,48,768]{2,1,0:T(8,128)(2,1)S(1)} async-done(((bf16[8,48,768]{2,1,0:T(8,128)(2,1)}), bf16[8,48,768]{2,1,0:T(8,128)(2,1)S(1)}, u32[]{:S(2)}, u32[]{:S(2)}) %all-to-all-start.1) | async-done | bytes 589856 | tf_op jit(solution)/shard_map/all_to_all | solution.py:241
  112.9 18.9 %all_to_all.20 = bf16[16,48,240]{2,1,0:T(8,128)(2,1)S(1)} all-to-all(bf16[16,48,240]{2,1,0:T(8,128)(2,1)S(1)} %copy.17), channel_id=1, replica_groups=mesh['dp'=16,'seq'=16] {'seq'}, dimensions={0} | all-to-all | bytes 737280 | tf_op jit(solution)/shard_map/all_to_all | solution.py:241
  132.0 15.1 %all_to_all.21.pieces_ref = bf16[16,48,240]{2,1,0:T(8,128)(2,1)S(1)} all-to-all(bf16[16,48,240]{2,1,0:T(8,128)(2,1)S(1)} %broadcast_in_dim.10), channel_id=1, replica_groups=mesh['dp'=16,'seq'=16] {'dp'}, dimensions={0} | all-to-all | bytes 737280 | tf_op jit(solution)/shard_map/all_to_all | solution.py:241
  (49 shorter events, 15.8 us)
Async XLA Ops:
  4.6 80.7 %all-to-all-start = ((bf16[16,2,2,32,768]{4,3,2,1,0:T(8,128)(2,1)}), bf16[16,2,2,32,768]{4,3,2,1,0:T(8,128)(2,1)S(1)}, u32[]{:S(2)}, u32[]{:S(2)}) async-start(bf16[16,2,2,32,768]{4,3,2,1,0:T(8,128)(2,1)} %send.1), calls=%async_computation | async-start | bytes 6291456 | tf_op jit(solution)/shard_map/all_to_all | solution.py:241
  32.0 3.5 %copy-start.4 = (bf16[768,1536]{1,0:T(8,128)(2,1)S(1)}, bf16[768,1536]{1,0:T(8,128)(2,1)}, u32[]{:S(2)}) copy-start(bf16[768,1536]{1,0:T(8,128)(2,1)} %get-tuple-element.16) | copy-start | bytes 7077892
  34.6 3.8 %collective-permute-start = (bf16[2,1,384,768]{3,2,0,1:T(8,128)(2,1)}, bf16[2,1,384,768]{3,2,0,1:T(8,128)(2,1)}, u32[]{:S(2)}, u32[]{:S(2)}) collective-permute-start(bf16[2,1,384,768]{3,2,0,1:T(8,128)(2,1)} %dynamic-slice_bitcast_fusion), channel_id=1, source_target_pairs={{0,16},{16,0},{32,48},{48,32},{64,80},{80,64},{96,112},{112,96},{1... | collective-permute-start | bytes 3538952 | tf_op jit(solution)/shard_map/ppermute | solution.py:209
  36.6 6.0 %collective-permute-start.4 = (bf16[1,1,384,1536]{3,2,1,0:T(8,128)(2,1)}, bf16[1,1,384,1536]{3,2,1,0:T(8,128)(2,1)}, u32[]{:S(2)}, u32[]{:S(2)}) collective-permute-start(bf16[1,1,384,1536]{3,2,1,0:T(8,128)(2,1)} %constant_dynamic-slice_fusion), channel_id=1, source_target_pairs={{0,16},{16,0},{32,48},{48,32},{64,80},{80,64},{96,112},{112,96},{1... | collective-permute-start | bytes 3538952 | tf_op jit(solution)/shard_map/ppermute | solution.py:209
  38.3 4.2 %copy-start.5 = (bf16[768,1536]{1,0:T(8,128)(2,1)S(1)}, bf16[768,1536]{1,0:T(8,128)(2,1)}, u32[]{:S(2)}) copy-start(bf16[768,1536]{1,0:T(8,128)(2,1)} %get-tuple-element.16) | copy-start | bytes 7077892
  40.4 2.2 %copy-start.3 = (f32[2,1,384,768]{3,2,0,1:T(8,128)}, f32[2,1,384,768]{3,2,0,1:T(8,128)S(1)}, u32[]{:S(2)}) copy-start(f32[2,1,384,768]{3,2,0,1:T(8,128)S(1)} %convert_add_fusion.1) | copy-start | bytes 7077892
  41.4 14.9 %collective-permute-start.1 = (bf16[2,1,2,2,48,768]{5,4,3,2,1,0:T(8,128)(2,1)}, bf16[2,1,2,2,48,768]{5,4,3,2,1,0:T(8,128)(2,1)}, u32[]{:S(2)}, u32[]{:S(2)}) collective-permute-start(bf16[2,1,2,2,48,768]{5,4,3,2,1,0:T(8,128)(2,1)} %dynamic-slice_convert_fusion.1), channel_id=1, source_target_pairs={{0,32},{16,48},{32,0},{48,16},{64,96},{80,112},{96,64},{112,80},{1... | collective-permute-start | bytes 1769480 | tf_op jit(solution)/shard_map/ppermute | solution.py:209
  44.2 1.5 copy-start.1
  46.6 15.7 %collective-permute-start.5 = (bf16[1,2,1,2,48,1536]{5,4,3,2,1,0:T(8,128)(2,1)}, bf16[1,2,1,2,48,1536]{5,4,3,2,1,0:T(8,128)(2,1)}, u32[]{:S(2)}, u32[]{:S(2)}) collective-permute-start(bf16[1,2,1,2,48,1536]{5,4,3,2,1,0:T(8,128)(2,1)} %dynamic-slice_convert_fusion), channel_id=1, source_target_pairs={{0,96},{16,112},{32,64},{48,80},{64,32},{80,48},{96,0},{112,16},{1... | collective-permute-start | bytes 1769480 | tf_op jit(solution)/shard_map/ppermute | solution.py:209
  49.6 12.8 %copy-start.2 = (f32[1,1,384,1536]{3,2,1,0:T(8,128)S(1)}, f32[1,1,384,1536]{3,2,1,0:T(8,128)}, u32[]{:S(2)}) copy-start(f32[1,1,384,1536]{3,2,1,0:T(8,128)} %copy-done.1) | copy-start | bytes 7077892
  57.8 10.7 %collective-permute-start.2 = (bf16[2,1,1,2,48,768]{5,4,3,2,1,0:T(8,128)(2,1)S(1)}, bf16[2,1,1,2,48,768]{5,4,3,2,1,0:T(8,128)(2,1)S(1)}, u32[]{:S(2)}, u32[]{:S(2)}) collective-permute-start(bf16[2,1,1,2,48,768]{5,4,3,2,1,0:T(8,128)(2,1)S(1)} %dynamic-slice_convert_fusion.3), channel_id=1, source_target_pairs={{0,96},{16,112},{32,64},{48,80},{64,32},{80,48},{96,0},{112,16},{1... | collective-permute-start | bytes 884744 | tf_op jit(solution)/shard_map/ppermute | solution.py:209
  63.6 7.8 %collective-permute-start.6 = (bf16[1,1,1,2,48,1536]{5,4,3,2,1,0:T(8,128)(2,1)S(1)}, bf16[1,1,1,2,48,1536]{5,4,3,2,1,0:T(8,128)(2,1)S(1)}, u32[]{:S(2)}, u32[]{:S(2)}) collective-permute-start(bf16[1,1,1,2,48,1536]{5,4,3,2,1,0:T(8,128)(2,1)S(1)} %dynamic-slice_convert_fusion.2), channel_id=1, source_target_pairs={{0,32},{16,48},{32,0},{48,16},{64,96},{80,112},{96,64},{112,80},{1... | collective-permute-start | bytes 884744 | tf_op jit(solution)/shard_map/ppermute | solution.py:209
  68.7 5.9 %collective-permute-start.3 = (bf16[2,1,1,1,48,768]{5,4,3,2,1,0:T(8,128)(2,1)S(1)}, bf16[2,1,1,1,48,768]{5,4,3,2,1,0:T(8,128)(2,1)S(1)}, u32[]{:S(2)}, u32[]{:S(2)}) collective-permute-start(bf16[2,1,1,1,48,768]{5,4,3,2,1,0:T(8,128)(2,1)S(1)} %dynamic-slice_convert_fusion.5), channel_id=1, source_target_pairs={{0,128},{16,144},{32,160},{48,176},{64,192},{80,208},{96,224},{112... | collective-permute-start | bytes 442376 | tf_op jit(solution)/shard_map/ppermute | solution.py:209
  71.5 7.2 %collective-permute-start.7 = (bf16[1,1,1,1,48,1536]{5,4,3,2,1,0:T(8,128)(2,1)S(1)}, bf16[1,1,1,1,48,1536]{5,4,3,2,1,0:T(8,128)(2,1)S(1)}, u32[]{:S(2)}, u32[]{:S(2)}) collective-permute-start(bf16[1,1,1,1,48,1536]{5,4,3,2,1,0:T(8,128)(2,1)S(1)} %dynamic-slice_convert_fusion.4), channel_id=1, source_target_pairs={{0,128},{16,144},{32,160},{48,176},{64,192},{80,208},{96,224},{112... | collective-permute-start | bytes 442376 | tf_op jit(solution)/shard_map/ppermute | solution.py:209
  85.4 1.4 copy-start
  88.7 3.5 %collective-permute-start.8 = (bf16[384,768]{1,0:T(8,128)(2,1)S(1)}, bf16[384,768]{1,0:T(8,128)(2,1)S(1)}, u32[]{:S(2)}, u32[]{:S(2)}) collective-permute-start(bf16[384,768]{1,0:T(8,128)(2,1)S(1)} %half.3), channel_id=1, source_target_pairs={{0,16},{16,0},{32,48},{48,32},{64,80},{80,64},{96,112},{112,96},{1... | collective-permute-start | bytes 1769480 | tf_op jit(solution)/shard_map/ppermute | solution.py:209
  93.1 7.0 %copy-start.6 = (bf16[1,48,1536]{2,1,0:T(8,128)(2,1)S(1)}, bf16[1,48,1536]{2,1,0:T(8,128)(2,1)}, u32[]{:S(2)}) copy-start(bf16[1,48,1536]{2,1,0:T(8,128)(2,1)} %fusion.1) | copy-start | bytes 442372
  93.1 19.0 %all-to-all-start.1 = ((bf16[8,48,768]{2,1,0:T(8,128)(2,1)}), bf16[8,48,768]{2,1,0:T(8,128)(2,1)S(1)}, u32[]{:S(2)}, u32[]{:S(2)}) async-start(bf16[8,48,768]{2,1,0:T(8,128)(2,1)} %bitcast.12), calls=%async_computation.1 | async-start | bytes 1179648 | tf_op jit(solution)/shard_map/all_to_all | solution.py:241

commit v8 on v7

--- a/solution.py
+++ b/solution.py
@@ -174,10 +174,15 @@
     )(part, both, came, value_weight)
 
 
-def join_kernel(pieces_ref, value_ref, up_ref, down_ref, rows_ref):
-    places, size, lanes = pieces_ref.shape
-    for i in range(places):
-        rows_ref[PIECE[i] * size : (PIECE[i] + 1) * size, :lanes] = pieces_ref[i]
+def join_kernel(core_ref, own_ref, other_ref, value_ref, up_ref, down_ref, rows_ref):
+    chips, size, lanes = own_ref.shape
+    first = core_ref[0] == 0
+    for chip in range(chips):
+        own, other = own_ref[chip], other_ref[chip]
+        low = PIECE[2 * chip] * size
+        high = PIECE[2 * chip + 1] * size
+        rows_ref[low : low + size, :lanes] = jnp.where(first, own, other)
+        rows_ref[high : high + size, :lanes] = jnp.where(first, other, own)
     turned = rows_ref[...].T
     width = value_ref.shape[1]
     share = value_ref.shape[0]
@@ -187,13 +192,15 @@
     down_ref[...] = turned[3 * share : 5 * share]
 
 
-def join(pieces):
-    places, size, lanes = pieces.shape
-    width = places * size
+def join(core, own, other):
+    chips, size, lanes = own.shape
+    width = 2 * chips * size
     share = lanes // 5
     padded = -(-lanes // 128) * 128
+    whole = pl.BlockSpec(memory_space=pltpu.VMEM)
     return pl.pallas_call(
         join_kernel,
+        in_specs=[pl.BlockSpec(memory_space=pltpu.SMEM), whole, whole],
         out_shape=[
             jax.ShapeDtypeStruct((share, width), BF16),
             jax.ShapeDtypeStruct((share, 2 * width), BF16),
@@ -202,7 +209,7 @@
         scratch_shapes=[pltpu.VMEM((width, padded), BF16)],
         compiler_params=pltpu.CompilerParams(vmem_limit_bytes=SMALL_LIMIT),
         name="join",
-    )(pieces)
+    )(core, own, other)
 
 
 def swap(block, flip, over):
@@ -290,7 +297,8 @@
 
     part = exchange(jnp.concatenate([pack((value_t,)), mlp_part], axis=2), "seq")
     part = (jnp.sum(part.astype(F32), axis=0) * factor).astype(BF16)
-    return tuple(join(exchange(jnp.broadcast_to(part[None], (16,) + part.shape), "dp")))
+    own = exchange(jnp.broadcast_to(part[None], (CHIPS,) + part.shape), "dp", same_core())
+    return tuple(join(core_arg, own, swap(own, 1, "dp")))
 
 
 def solution(mesh):

time: 148 us -> 148 us (level)
  blocking collectives: 34 us -> 28.9 us
  starting transfers between devices: 28.7 us -> 32.4 us
    all_to_all x2, blocking collectives: 34 us -> 28.9 us  [exchange(): lax.all_to_all(block, axis, split_axis=0, concat_axis=0, tiled=True, axis...]
    ppermute x9 -> x10, starting transfers between devices: 12 us -> 15.8 us  [swap(): return lax.ppermute(block, over, [(i, i ^ flip) for i in range(16)])]
    ppermute x9 -> x10, waiting for transfers between devices: 21.2 us -> 22.3 us  [swap(): return lax.ppermute(block, over, [(i, i ^ flip) for i in range(16)])]
  transfers between devices with their start and end apart: 11 -> 12, of which waited for: 8 -> 9; matrix products, arithmetic and copies ran while one was open for 10% -> 10% of each run, Pallas kernels for 13% -> 13%
where the time goes in v8:
time: 148 us
  waiting for transfers between devices  40.2 us (27%)
  starting transfers between devices  32.4 us (22%)
  blocking collectives  28.9 us (20%)
  Pallas kernels  27.3 us (18%)
  local copies, waits for them, and re-layouts  9.25 us (6%)
  other arithmetic  8.73 us (6%)
    all_to_all x2, blocking collectives, exchange(): lax.all_to_all(block, axis, split_axis=0, concat_axis=0, tiled=True, axis...  28.9 us
    ppermute x10, waiting for transfers between devices, swap(): return lax.ppermute(block, over, [(i, i ^ flip) for i in range(16)])  22.3 us
    all_to_all x2, waiting for transfers between devices, exchange(): lax.all_to_all(block, axis, split_axis=0, concat_axis=0, tiled=True, axis...  17.9 us
    pallas_call x1, Pallas kernels, mlp_grads(): pl.pallas_call(mlp_kernel, grid=(units // step,), in_specs=[whole, whole,...  17.2 us
    all_to_all x2, starting transfers between devices, exchange(): lax.all_to_all(block, axis, split_axis=0, concat_axis=0, tiled=True, axis...  16.6 us
    ppermute x10, starting transfers between devices, swap(): return lax.ppermute(block, over, [(i, i ^ flip) for i in range(16)])  15.8 us
    add x6, other arithmetic, add_swapped(): return keep.astype(F32) + swap(give.astype(BF16), flip, over).astype(F32)  6.5 us
    pallas_call x1, Pallas kernels, build_sent(): pl.pallas_call(send_kernel, grid=(rows // step,), in_specs=[whole, whole,...  4.07 us
  transfers between devices with their start and end apart: 12, of which 9 were waited for; matrix products, arithmetic and copies ran while one was open for 10% of the time, Pallas kernels for 13%

profile of v8, /device:TPU:1, one launch (start us, length us, event | category | flops | bytes accessed | tf_op | source)
XLA Modules:
  0.0 147.7 jit_solution(13604699285720308111)
XLA Ops:
  0.6 4.1 %send.1 = bf16[16,2,2,32,768]{4,3,2,1,0:T(8,128)(2,1)} custom-call(bf16[1,4,256,768]{3,2,1,0:T(8,128)(2,1)} %inputs_ref.1, bf16[1,4,256,768]{3,2,1,0:T(8,128)(2,1)} %cot_ref.1, bf16[4,256,256]{2,1,0:T(8,128)(2,1)} %first_ref.1), custom_call_target="tpu_custom_call" | custom-call | tf_op jit(solution)/shard_map/send/pallas_call | solution.py:50
  4.7 10.1 %all-to-all-start = ((bf16[16,2,2,32,768]{4,3,2,1,0:T(8,128)(2,1)}), bf16[16,2,2,32,768]{4,3,2,1,0:T(8,128)(2,1)S(1)}, u32[]{:S(2)}, u32[]{:S(2)}) async-start(bf16[16,2,2,32,768]{4,3,2,1,0:T(8,128)(2,1)} %send.1), calls=%async_computation | async-start | bytes 6291456 | tf_op jit(solution)/shard_map/all_to_all | solution.py:248
  14.8 17.2 %mlp.1 = (bf16[1536,768]{1,0:T(8,128)(2,1)}, bf16[768,1536]{1,0:T(8,128)(2,1)}) custom-call(bf16[1024,768]{1,0:T(8,128)(2,1)} %bitcast.31, bf16[1024,768]{1,0:T(8,128)(2,1)} %bitcast.32, bf16[768,1536]{1,0:T(8,128)(2,1)} %up_ref.1, bf16[1536,768]{1,0:T(8,128)(2,1)} %down_ref.1), custom_call_target="tpu_custom_call" | custom-call | tf_op jit(solution)/shard_map/mlp/pallas_call | solution.py:87
  32.0 2.5 %dynamic-slice_bitcast_fusion = bf16[2,1,384,768]{3,2,0,1:T(8,128)(2,1)} fusion(bf16[2,2,384,768]{3,2,1,0:T(8,128)(2,1)} %bitcast.35, s32[]{:T(128)S(6)} %select_n.33), kind=kLoop, calls=%fused_computation.7 | loop fusion | bytes 2359300
  36.6 1.7 %collective-permute-done = bf16[2,1,384,768]{3,2,0,1:T(8,128)(2,1)} collective-permute-done((bf16[2,1,384,768]{3,2,0,1:T(8,128)(2,1)}, bf16[2,1,384,768]{3,2,0,1:T(8,128)(2,1)}, u32[]{:S(2)}, u32[]{:S(2)}) %collective-permute-start) | collective-permute-done | bytes 1179680 | tf_op jit(solution)/shard_map/ppermute | solution.py:216
  38.4 2.0 %convert_add_fusion.1 = f32[2,1,384,768]{3,2,0,1:T(8,128)S(1)} fusion(bf16[2,1,384,768]{3,2,0,1:T(8,128)(2,1)} %collective-permute-done, bf16[2,2,384,768]{3,2,1,0:T(8,128)(2,1)} %bitcast.36, s32[]{:T(128)S(6)} %select_n.32), kind=kLoop, calls=%fused_computation.1 | loop fusion | flops 1769472 | bytes 4718596 | tf_op jit(solution)/shard_map/add | solution.py:220
  42.6 1.6 %convert_add_fusion = f32[1,1,384,1536]{3,2,1,0:T(8,128)S(1)} fusion(bf16[1,1,384,1536]{3,2,1,0:T(8,128)(2,1)} %collective-permute-done.4, bf16[1,2,384,1536]{3,2,1,0:T(8,128)(2,1)S(1)} %bitcast.34, s32[]{:T(128)S(6)} %select_n.32), kind=kLoop, calls=%fused_computation | loop fusion | flops 1769472 | bytes 4718596 | tf_op jit(solution)/shard_map/add | solution.py:220
  46.6 1.9 %collective-permute-start.5 = (bf16[1,2,1,2,48,1536]{5,4,3,2,1,0:T(8,128)(2,1)}, bf16[1,2,1,2,48,1536]{5,4,3,2,1,0:T(8,128)(2,1)}, u32[]{:S(2)}, u32[]{:S(2)}) collective-permute-start(bf16[1,2,1,2,48,1536]{5,4,3,2,1,0:T(8,128)(2,1)} %dynamic-slice_convert_fusion), channel_id=1, source_target_pairs={{0,96},{16,112},{32,64},{48,80},{64,32},{80,48},{96,0},{112,16},{1... | collective-permute-start | bytes 1769480 | tf_op jit(solution)/shard_map/ppermute | solution.py:216
  49.6 6.6 %collective-permute-done.1 = bf16[2,1,2,2,48,768]{5,4,3,2,1,0:T(8,128)(2,1)} collective-permute-done((bf16[2,1,2,2,48,768]{5,4,3,2,1,0:T(8,128)(2,1)}, bf16[2,1,2,2,48,768]{5,4,3,2,1,0:T(8,128)(2,1)}, u32[]{:S(2)}, u32[]{:S(2)}) %collective-permute-start.1) | collective-permute-done | bytes 589856 | tf_op jit(solution)/shard_map/ppermute | solution.py:216
  56.2 1.6 %convert_add_fusion.3 = f32[2,1,2,2,48,768]{5,4,3,2,1,0:T(8,128)S(1)} fusion(bf16[2,1,2,2,48,768]{5,4,3,2,1,0:T(8,128)(2,1)} %collective-permute-done.1, f32[2,2,2,2,48,768]{5,4,3,2,1,0:T(8,128)} %bitcast.30, s32[]{:T(128)S(6)} %select_n.34), kind=kLoop, calls=%fused_computation.5 | loop fusion | flops 589824 | bytes 2949124 | tf_op jit(solution)/shard_map/add | solution.py:220
  57.9 2.6 %collective-permute-start.2 = (bf16[2,1,1,2,48,768]{5,4,3,2,1,0:T(8,128)(2,1)S(1)}, bf16[2,1,1,2,48,768]{5,4,3,2,1,0:T(8,128)(2,1)S(1)}, u32[]{:S(2)}, u32[]{:S(2)}) collective-permute-start(bf16[2,1,1,2,48,768]{5,4,3,2,1,0:T(8,128)(2,1)S(1)} %dynamic-slice_convert_fusion.3), channel_id=1, source_target_pairs={{0,96},{16,112},{32,64},{48,80},{64,32},{80,48},{96,0},{112,16},{1... | collective-permute-start | bytes 884744 | tf_op jit(solution)/shard_map/ppermute | solution.py:216
  60.4 1.9 %collective-permute-done.5 = bf16[1,2,1,2,48,1536]{5,4,3,2,1,0:T(8,128)(2,1)} collective-permute-done((bf16[1,2,1,2,48,1536]{5,4,3,2,1,0:T(8,128)(2,1)}, bf16[1,2,1,2,48,1536]{5,4,3,2,1,0:T(8,128)(2,1)}, u32[]{:S(2)}, u32[]{:S(2)}) %collective-permute-start.5) | collective-permute-done | bytes 589856 | tf_op jit(solution)/shard_map/ppermute | solution.py:216
  63.7 4.9 %collective-permute-done.2 = bf16[2,1,1,2,48,768]{5,4,3,2,1,0:T(8,128)(2,1)S(1)} collective-permute-done((bf16[2,1,1,2,48,768]{5,4,3,2,1,0:T(8,128)(2,1)S(1)}, bf16[2,1,1,2,48,768]{5,4,3,2,1,0:T(8,128)(2,1)S(1)}, u32[]{:S(2)}, u32[]{:S(2)}) %collective-permute-start.2) | collective-permute-done | bytes 294944 | tf_op jit(solution)/shard_map/ppermute | solution.py:216
  68.7 2.7 %collective-permute-start.3 = (bf16[2,1,1,1,48,768]{5,4,3,2,1,0:T(8,128)(2,1)S(1)}, bf16[2,1,1,1,48,768]{5,4,3,2,1,0:T(8,128)(2,1)S(1)}, u32[]{:S(2)}, u32[]{:S(2)}) collective-permute-start(bf16[2,1,1,1,48,768]{5,4,3,2,1,0:T(8,128)(2,1)S(1)} %dynamic-slice_convert_fusion.5), channel_id=1, source_target_pairs={{0,128},{16,144},{32,160},{48,176},{64,192},{80,208},{96,224},{112... | collective-permute-start | bytes 442376 | tf_op jit(solution)/shard_map/ppermute | solution.py:216
  72.6 2.0 %collective-permute-done.3 = bf16[2,1,1,1,48,768]{5,4,3,2,1,0:T(8,128)(2,1)S(1)} collective-permute-done((bf16[2,1,1,1,48,768]{5,4,3,2,1,0:T(8,128)(2,1)S(1)}, bf16[2,1,1,1,48,768]{5,4,3,2,1,0:T(8,128)(2,1)S(1)}, u32[]{:S(2)}, u32[]{:S(2)}) %collective-permute-start.3) | collective-permute-done | bytes 147488 | tf_op jit(solution)/shard_map/ppermute | solution.py:216
  74.6 4.1 %collective-permute-done.7 = bf16[1,1,1,1,48,1536]{5,4,3,2,1,0:T(8,128)(2,1)S(1)} collective-permute-done((bf16[1,1,1,1,48,1536]{5,4,3,2,1,0:T(8,128)(2,1)S(1)}, bf16[1,1,1,1,48,1536]{5,4,3,2,1,0:T(8,128)(2,1)S(1)}, u32[]{:S(2)}, u32[]{:S(2)}) %collective-permute-start.7) | collective-permute-done | bytes 147488 | tf_op jit(solution)/shard_map/ppermute | solution.py:216
  79.4 6.1 %all-to-all-done.mix_ref.weighted_ref = bf16[16,2,2,32,768]{4,3,2,1,0:T(8,128)(2,1)S(1)} async-done(((bf16[16,2,2,32,768]{4,3,2,1,0:T(8,128)(2,1)}), bf16[16,2,2,32,768]{4,3,2,1,0:T(8,128)(2,1)S(1)}, u32[]{:S(2)}, u32[]{:S(2)}) %all-to-all-start) | async-done | bytes 3145760 | tf_op jit(solution)/shard_map/all_to_all | solution.py:248
  86.8 1.9 %half.3 = bf16[384,768]{1,0:T(8,128)(2,1)S(1)} custom-call(s32[1]{0:T(128)S(6)} %sub.23.part_ref, bf16[1024,768]{1,0:T(8,128)(2,1)S(1)} %mix.1.both_ref, bf16[16,2,2,32,768]{4,3,2,1,0:T(8,128)(2,1)S(1)} %all-to-all-done.mix_ref.weighted_ref, bf16[768,768]{1,0:T(8,128)(2,1)S(1)} %copy-done), custom_call_target="tpu_custom_call" | custom-call | tf_op jit(solution)/shard_map/half/pallas_call | solution.py:159
  90.3 1.9 %half.2 = bf16[384,768]{1,0:T(8,128)(2,1)S(1)} custom-call(s32[1]{0:T(128)} %bitcast.part_ref.core_ref, bf16[1024,768]{1,0:T(8,128)(2,1)S(1)} %mix.1.both_ref, bf16[16,2,2,32,768]{4,3,2,1,0:T(8,128)(2,1)S(1)} %all-to-all-done.mix_ref.weighted_ref, bf16[768,768]{1,0:T(8,128)(2,1)S(1)} %copy-done), custom_call_target="tpu_custom_call" | custom-call | tf_op jit(solution)/shard_map/half/pallas_call | solution.py:159
  93.2 6.5 %all-to-all-start.1 = ((bf16[8,48,768]{2,1,0:T(8,128)(2,1)}), bf16[8,48,768]{2,1,0:T(8,128)(2,1)S(1)}, u32[]{:S(2)}, u32[]{:S(2)}) async-start(bf16[8,48,768]{2,1,0:T(8,128)(2,1)} %bitcast.12), calls=%async_computation.1 | async-start | bytes 1179648 | tf_op jit(solution)/shard_map/all_to_all | solution.py:248
  100.3 11.8 %all-to-all-done.1 = bf16[8,48,768]{2,1,0:T(8,128)(2,1)S(1)} async-done(((bf16[8,48,768]{2,1,0:T(8,128)(2,1)}), bf16[8,48,768]{2,1,0:T(8,128)(2,1)S(1)}, u32[]{:S(2)}, u32[]{:S(2)}) %all-to-all-start.1) | async-done | bytes 589856 | tf_op jit(solution)/shard_map/all_to_all | solution.py:248
  113.0 18.9 %all_to_all.20 = bf16[16,48,240]{2,1,0:T(8,128)(2,1)S(1)} all-to-all(bf16[16,48,240]{2,1,0:T(8,128)(2,1)S(1)} %copy.17), channel_id=1, replica_groups=mesh['dp'=16,'seq'=16] {'seq'}, dimensions={0} | all-to-all | bytes 737280 | tf_op jit(solution)/shard_map/all_to_all | solution.py:248
  132.0 10.0 %all_to_all.21.own_ref = bf16[8,48,240]{2,1,0:T(8,128)(2,1)S(1)} all-to-all(bf16[8,48,240]{2,1,0:T(8,128)(2,1)S(1)} %broadcast_in_dim.10), channel_id=1, replica_groups={{0,32,64,96,128,160,192,224},{16,48,80,112,144,176,208,240},{1,33,65,97..., dimensions={0} | all-to-all | bytes 368640 | tf_op jit(solution)/shard_map/all_to_all | solution.py:248
  142.0 3.7 %collective-permute-start.9 = (bf16[8,48,240]{2,1,0:T(8,128)(2,1)S(1)}, bf16[8,48,240]{2,1,0:T(8,128)(2,1)S(1)}, u32[]{:S(2)}, u32[]{:S(2)}) collective-permute-start(bf16[8,48,240]{2,1,0:T(8,128)(2,1)S(1)} %all_to_all.21.own_ref), channel_id=1, source_target_pairs={{0,16},{16,0},{32,48},{48,32},{64,80},{80,64},{96,112},{112,96},{1... | collective-permute-start | bytes 552968 | tf_op jit(solution)/shard_map/ppermute | solution.py:216
  (51 shorter events, 18.4 us)
Async XLA Ops:
  4.7 80.7 %all-to-all-start = ((bf16[16,2,2,32,768]{4,3,2,1,0:T(8,128)(2,1)}), bf16[16,2,2,32,768]{4,3,2,1,0:T(8,128)(2,1)S(1)}, u32[]{:S(2)}, u32[]{:S(2)}) async-start(bf16[16,2,2,32,768]{4,3,2,1,0:T(8,128)(2,1)} %send.1), calls=%async_computation | async-start | bytes 6291456 | tf_op jit(solution)/shard_map/all_to_all | solution.py:248
  32.0 3.5 %copy-start.4 = (bf16[768,1536]{1,0:T(8,128)(2,1)S(1)}, bf16[768,1536]{1,0:T(8,128)(2,1)}, u32[]{:S(2)}) copy-start(bf16[768,1536]{1,0:T(8,128)(2,1)} %get-tuple-element.16) | copy-start | bytes 7077892
  34.6 3.8 %collective-permute-start = (bf16[2,1,384,768]{3,2,0,1:T(8,128)(2,1)}, bf16[2,1,384,768]{3,2,0,1:T(8,128)(2,1)}, u32[]{:S(2)}, u32[]{:S(2)}) collective-permute-start(bf16[2,1,384,768]{3,2,0,1:T(8,128)(2,1)} %dynamic-slice_bitcast_fusion), channel_id=1, source_target_pairs={{0,16},{16,0},{32,48},{48,32},{64,80},{80,64},{96,112},{112,96},{1... | collective-permute-start | bytes 3538952 | tf_op jit(solution)/shard_map/ppermute | solution.py:216
  36.6 6.0 %collective-permute-start.4 = (bf16[1,1,384,1536]{3,2,1,0:T(8,128)(2,1)}, bf16[1,1,384,1536]{3,2,1,0:T(8,128)(2,1)}, u32[]{:S(2)}, u32[]{:S(2)}) collective-permute-start(bf16[1,1,384,1536]{3,2,1,0:T(8,128)(2,1)} %constant_dynamic-slice_fusion), channel_id=1, source_target_pairs={{0,16},{16,0},{32,48},{48,32},{64,80},{80,64},{96,112},{112,96},{1... | collective-permute-start | bytes 3538952 | tf_op jit(solution)/shard_map/ppermute | solution.py:216
  38.4 4.2 %copy-start.5 = (bf16[768,1536]{1,0:T(8,128)(2,1)S(1)}, bf16[768,1536]{1,0:T(8,128)(2,1)}, u32[]{:S(2)}) copy-start(bf16[768,1536]{1,0:T(8,128)(2,1)} %get-tuple-element.16) | copy-start | bytes 7077892
  40.4 2.2 %copy-start.3 = (f32[2,1,384,768]{3,2,0,1:T(8,128)}, f32[2,1,384,768]{3,2,0,1:T(8,128)S(1)}, u32[]{:S(2)}) copy-start(f32[2,1,384,768]{3,2,0,1:T(8,128)S(1)} %convert_add_fusion.1) | copy-start | bytes 7077892
  41.4 14.9 %collective-permute-start.1 = (bf16[2,1,2,2,48,768]{5,4,3,2,1,0:T(8,128)(2,1)}, bf16[2,1,2,2,48,768]{5,4,3,2,1,0:T(8,128)(2,1)}, u32[]{:S(2)}, u32[]{:S(2)}) collective-permute-start(bf16[2,1,2,2,48,768]{5,4,3,2,1,0:T(8,128)(2,1)} %dynamic-slice_convert_fusion.1), channel_id=1, source_target_pairs={{0,32},{16,48},{32,0},{48,16},{64,96},{80,112},{96,64},{112,80},{1... | collective-permute-start | bytes 1769480 | tf_op jit(solution)/shard_map/ppermute | solution.py:216
  44.2 1.5 copy-start.1
  46.6 15.7 %collective-permute-start.5 = (bf16[1,2,1,2,48,1536]{5,4,3,2,1,0:T(8,128)(2,1)}, bf16[1,2,1,2,48,1536]{5,4,3,2,1,0:T(8,128)(2,1)}, u32[]{:S(2)}, u32[]{:S(2)}) collective-permute-start(bf16[1,2,1,2,48,1536]{5,4,3,2,1,0:T(8,128)(2,1)} %dynamic-slice_convert_fusion), channel_id=1, source_target_pairs={{0,96},{16,112},{32,64},{48,80},{64,32},{80,48},{96,0},{112,16},{1... | collective-permute-start | bytes 1769480 | tf_op jit(solution)/shard_map/ppermute | solution.py:216
  49.6 12.8 %copy-start.2 = (f32[1,1,384,1536]{3,2,1,0:T(8,128)S(1)}, f32[1,1,384,1536]{3,2,1,0:T(8,128)}, u32[]{:S(2)}) copy-start(f32[1,1,384,1536]{3,2,1,0:T(8,128)} %copy-done.1) | copy-start | bytes 7077892
  57.9 10.7 %collective-permute-start.2 = (bf16[2,1,1,2,48,768]{5,4,3,2,1,0:T(8,128)(2,1)S(1)}, bf16[2,1,1,2,48,768]{5,4,3,2,1,0:T(8,128)(2,1)S(1)}, u32[]{:S(2)}, u32[]{:S(2)}) collective-permute-start(bf16[2,1,1,2,48,768]{5,4,3,2,1,0:T(8,128)(2,1)S(1)} %dynamic-slice_convert_fusion.3), channel_id=1, source_target_pairs={{0,96},{16,112},{32,64},{48,80},{64,32},{80,48},{96,0},{112,16},{1... | collective-permute-start | bytes 884744 | tf_op jit(solution)/shard_map/ppermute | solution.py:216
  63.6 7.8 %collective-permute-start.6 = (bf16[1,1,1,2,48,1536]{5,4,3,2,1,0:T(8,128)(2,1)S(1)}, bf16[1,1,1,2,48,1536]{5,4,3,2,1,0:T(8,128)(2,1)S(1)}, u32[]{:S(2)}, u32[]{:S(2)}) collective-permute-start(bf16[1,1,1,2,48,1536]{5,4,3,2,1,0:T(8,128)(2,1)S(1)} %dynamic-slice_convert_fusion.2), channel_id=1, source_target_pairs={{0,32},{16,48},{32,0},{48,16},{64,96},{80,112},{96,64},{112,80},{1... | collective-permute-start | bytes 884744 | tf_op jit(solution)/shard_map/ppermute | solution.py:216
  68.7 5.9 %collective-permute-start.3 = (bf16[2,1,1,1,48,768]{5,4,3,2,1,0:T(8,128)(2,1)S(1)}, bf16[2,1,1,1,48,768]{5,4,3,2,1,0:T(8,128)(2,1)S(1)}, u32[]{:S(2)}, u32[]{:S(2)}) collective-permute-start(bf16[2,1,1,1,48,768]{5,4,3,2,1,0:T(8,128)(2,1)S(1)} %dynamic-slice_convert_fusion.5), channel_id=1, source_target_pairs={{0,128},{16,144},{32,160},{48,176},{64,192},{80,208},{96,224},{112... | collective-permute-start | bytes 442376 | tf_op jit(solution)/shard_map/ppermute | solution.py:216
  71.5 7.2 %collective-permute-start.7 = (bf16[1,1,1,1,48,1536]{5,4,3,2,1,0:T(8,128)(2,1)S(1)}, bf16[1,1,1,1,48,1536]{5,4,3,2,1,0:T(8,128)(2,1)S(1)}, u32[]{:S(2)}, u32[]{:S(2)}) collective-permute-start(bf16[1,1,1,1,48,1536]{5,4,3,2,1,0:T(8,128)(2,1)S(1)} %dynamic-slice_convert_fusion.4), channel_id=1, source_target_pairs={{0,128},{16,144},{32,160},{48,176},{64,192},{80,208},{96,224},{112... | collective-permute-start | bytes 442376 | tf_op jit(solution)/shard_map/ppermute | solution.py:216
  85.4 1.4 copy-start
  88.7 3.5 %collective-permute-start.8 = (bf16[384,768]{1,0:T(8,128)(2,1)S(1)}, bf16[384,768]{1,0:T(8,128)(2,1)S(1)}, u32[]{:S(2)}, u32[]{:S(2)}) collective-permute-start(bf16[384,768]{1,0:T(8,128)(2,1)S(1)} %half.3), channel_id=1, source_target_pairs={{0,16},{16,0},{32,48},{48,32},{64,80},{80,64},{96,112},{112,96},{1... | collective-permute-start | bytes 1769480 | tf_op jit(solution)/shard_map/ppermute | solution.py:216
  93.2 7.0 %copy-start.6 = (bf16[1,48,1536]{2,1,0:T(8,128)(2,1)S(1)}, bf16[1,48,1536]{2,1,0:T(8,128)(2,1)}, u32[]{:S(2)}) copy-start(bf16[1,48,1536]{2,1,0:T(8,128)(2,1)} %fusion.1) | copy-start | bytes 442372
  93.2 19.0 %all-to-all-start.1 = ((bf16[8,48,768]{2,1,0:T(8,128)(2,1)}), bf16[8,48,768]{2,1,0:T(8,128)(2,1)S(1)}, u32[]{:S(2)}, u32[]{:S(2)}) async-start(bf16[8,48,768]{2,1,0:T(8,128)(2,1)} %bitcast.12), calls=%async_computation.1 | async-start | bytes 1179648 | tf_op jit(solution)/shard_map/all_to_all | solution.py:248
  142.0 4.8 %collective-permute-start.9 = (bf16[8,48,240]{2,1,0:T(8,128)(2,1)S(1)}, bf16[8,48,240]{2,1,0:T(8,128)(2,1)S(1)}, u32[]{:S(2)}, u32[]{:S(2)}) collective-permute-start(bf16[8,48,240]{2,1,0:T(8,128)(2,1)S(1)} %all_to_all.21.own_ref), channel_id=1, source_target_pairs={{0,16},{16,0},{32,48},{48,32},{64,80},{80,64},{96,112},{112,96},{1... | collective-permute-start | bytes 552968 | tf_op jit(solution)/shard_map/ppermute | solution.py:216

commit v9 on v8

--- a/solution.py
+++ b/solution.py
@@ -100,16 +100,18 @@
 
 
 def value_half(both_ref, weighted_ref, weight_ref, out_ref):
-    slopes = []
     groups = weighted_ref.shape[2]
     positions = both_ref.shape[0] // groups
+    grad = None
     for k in range(groups):
-        mixed = product(both_ref[pl.ds(k * positions, positions)], weight_ref[...], 1, 0)
+        both = both_ref[pl.ds(k * positions, positions)]
+        mixed = product(both, weight_ref[...], 1, 0)
         sigmoid_part = jax.nn.sigmoid(mixed)
         weighted = weighted_ref[:, 0, k].reshape(mixed.shape).astype(F32)
         slope = weighted * (sigmoid_part * (1.0 + mixed * (1.0 - sigmoid_part)))
-        slopes.append(slope.astype(BF16))
-    grad = product(jnp.concatenate(slopes, axis=0), both_ref[...], 0, 0).astype(BF16)
+        term = product(slope.astype(BF16), both, 0, 0)
+        grad = term if grad is None else grad + term
+    grad = grad.astype(BF16)
     size = grad.shape[0] // CHIPS
     pieces = [PIECE[2 * chip] % CHIPS for chip in range(CHIPS)]
     out_ref[...] = jnp.concatenate([grad[p * size : (p + 1) * size] for p in pieces], axis=0)

time: 148 us -> 149 us (level)
  no operation moved by 1% of the time
where the time goes in v9:
time: 149 us; the launch traced here: 148 us
  waiting for transfers between devices  40.2 us (27%)
  starting transfers between devices  32.5 us (22%)
  blocking collectives  28.9 us (19%)
  Pallas kernels  27.7 us (19%)
  local copies, waits for them, and re-layouts  9.25 us (6%)
  other arithmetic  8.73 us (6%)
    all_to_all x2, blocking collectives, exchange(): lax.all_to_all(block, axis, split_axis=0, concat_axis=0, tiled=True, axis...  28.9 us
    ppermute x10, waiting for transfers between devices, swap(): return lax.ppermute(block, over, [(i, i ^ flip) for i in range(16)])  22.3 us
    all_to_all x2, waiting for transfers between devices, exchange(): lax.all_to_all(block, axis, split_axis=0, concat_axis=0, tiled=True, axis...  17.9 us
    pallas_call x1, Pallas kernels, mlp_grads(): pl.pallas_call(mlp_kernel, grid=(units // step,), in_specs=[whole, whole,...  17.2 us
    all_to_all x2, starting transfers between devices, exchange(): lax.all_to_all(block, axis, split_axis=0, concat_axis=0, tiled=True, axis...  16.6 us
    ppermute x10, starting transfers between devices, swap(): return lax.ppermute(block, over, [(i, i ^ flip) for i in range(16)])  15.8 us
    add x6, other arithmetic, add_swapped(): return keep.astype(F32) + swap(give.astype(BF16), flip, over).astype(F32)  6.5 us
    pallas_call x2, Pallas kernels, value_part(): pl.pallas_call(half_kernel, grid_spec=pltpu.PrefetchScalarGridSpec(num_sc...  4.2 us
  transfers between devices with their start and end apart: 12, of which 9 were waited for; matrix products, arithmetic and copies ran while one was open for 10% of the time, Pallas kernels for 13%

profile of v9, /device:TPU:1, one launch (start us, length us, event | category | flops | bytes accessed | tf_op | source)
XLA Modules:
  0.0 148.1 jit_solution(10780765575902391846)
XLA Ops:
  0.6 4.1 %send.1 = bf16[16,2,2,32,768]{4,3,2,1,0:T(8,128)(2,1)} custom-call(bf16[1,4,256,768]{3,2,1,0:T(8,128)(2,1)} %inputs_ref.1, bf16[1,4,256,768]{3,2,1,0:T(8,128)(2,1)} %cot_ref.1, bf16[4,256,256]{2,1,0:T(8,128)(2,1)} %first_ref.1), custom_call_target="tpu_custom_call" | custom-call | tf_op jit(solution)/shard_map/send/pallas_call | solution.py:50
  4.7 10.1 %all-to-all-start = ((bf16[16,2,2,32,768]{4,3,2,1,0:T(8,128)(2,1)}), bf16[16,2,2,32,768]{4,3,2,1,0:T(8,128)(2,1)S(1)}, u32[]{:S(2)}, u32[]{:S(2)}) async-start(bf16[16,2,2,32,768]{4,3,2,1,0:T(8,128)(2,1)} %send.1), calls=%async_computation | async-start | bytes 6291456 | tf_op jit(solution)/shard_map/all_to_all | solution.py:250
  14.8 17.2 %mlp.1 = (bf16[1536,768]{1,0:T(8,128)(2,1)}, bf16[768,1536]{1,0:T(8,128)(2,1)}) custom-call(bf16[1024,768]{1,0:T(8,128)(2,1)} %bitcast.31, bf16[1024,768]{1,0:T(8,128)(2,1)} %bitcast.32, bf16[768,1536]{1,0:T(8,128)(2,1)} %up_ref.1, bf16[1536,768]{1,0:T(8,128)(2,1)} %down_ref.1), custom_call_target="tpu_custom_call" | custom-call | tf_op jit(solution)/shard_map/mlp/pallas_call | solution.py:87
  32.0 2.5 %dynamic-slice_bitcast_fusion = bf16[2,1,384,768]{3,2,0,1:T(8,128)(2,1)} fusion(bf16[2,2,384,768]{3,2,1,0:T(8,128)(2,1)} %bitcast.35, s32[]{:T(128)S(6)} %select_n.33), kind=kLoop, calls=%fused_computation.7 | loop fusion | bytes 2359300
  36.6 1.7 %collective-permute-done = bf16[2,1,384,768]{3,2,0,1:T(8,128)(2,1)} collective-permute-done((bf16[2,1,384,768]{3,2,0,1:T(8,128)(2,1)}, bf16[2,1,384,768]{3,2,0,1:T(8,128)(2,1)}, u32[]{:S(2)}, u32[]{:S(2)}) %collective-permute-start) | collective-permute-done | bytes 1179680 | tf_op jit(solution)/shard_map/ppermute | solution.py:218
  38.4 2.0 %convert_add_fusion.1 = f32[2,1,384,768]{3,2,0,1:T(8,128)S(1)} fusion(bf16[2,1,384,768]{3,2,0,1:T(8,128)(2,1)} %collective-permute-done, bf16[2,2,384,768]{3,2,1,0:T(8,128)(2,1)} %bitcast.36, s32[]{:T(128)S(6)} %select_n.32), kind=kLoop, calls=%fused_computation.1 | loop fusion | flops 1769472 | bytes 4718596 | tf_op jit(solution)/shard_map/add | solution.py:222
  42.6 1.6 %convert_add_fusion = f32[1,1,384,1536]{3,2,1,0:T(8,128)S(1)} fusion(bf16[1,1,384,1536]{3,2,1,0:T(8,128)(2,1)} %collective-permute-done.4, bf16[1,2,384,1536]{3,2,1,0:T(8,128)(2,1)S(1)} %bitcast.34, s32[]{:T(128)S(6)} %select_n.32), kind=kLoop, calls=%fused_computation | loop fusion | flops 1769472 | bytes 4718596 | tf_op jit(solution)/shard_map/add | solution.py:222
  46.6 1.9 %collective-permute-start.5 = (bf16[1,2,1,2,48,1536]{5,4,3,2,1,0:T(8,128)(2,1)}, bf16[1,2,1,2,48,1536]{5,4,3,2,1,0:T(8,128)(2,1)}, u32[]{:S(2)}, u32[]{:S(2)}) collective-permute-start(bf16[1,2,1,2,48,1536]{5,4,3,2,1,0:T(8,128)(2,1)} %dynamic-slice_convert_fusion), channel_id=1, source_target_pairs={{0,96},{16,112},{32,64},{48,80},{64,32},{80,48},{96,0},{112,16},{1... | collective-permute-start | bytes 1769480 | tf_op jit(solution)/shard_map/ppermute | solution.py:218
  49.6 6.6 %collective-permute-done.1 = bf16[2,1,2,2,48,768]{5,4,3,2,1,0:T(8,128)(2,1)} collective-permute-done((bf16[2,1,2,2,48,768]{5,4,3,2,1,0:T(8,128)(2,1)}, bf16[2,1,2,2,48,768]{5,4,3,2,1,0:T(8,128)(2,1)}, u32[]{:S(2)}, u32[]{:S(2)}) %collective-permute-start.1) | collective-permute-done | bytes 589856 | tf_op jit(solution)/shard_map/ppermute | solution.py:218
  56.2 1.6 %convert_add_fusion.3 = f32[2,1,2,2,48,768]{5,4,3,2,1,0:T(8,128)S(1)} fusion(bf16[2,1,2,2,48,768]{5,4,3,2,1,0:T(8,128)(2,1)} %collective-permute-done.1, f32[2,2,2,2,48,768]{5,4,3,2,1,0:T(8,128)} %bitcast.30, s32[]{:T(128)S(6)} %select_n.34), kind=kLoop, calls=%fused_computation.5 | loop fusion | flops 589824 | bytes 2949124 | tf_op jit(solution)/shard_map/add | solution.py:222
  57.9 2.6 %collective-permute-start.2 = (bf16[2,1,1,2,48,768]{5,4,3,2,1,0:T(8,128)(2,1)S(1)}, bf16[2,1,1,2,48,768]{5,4,3,2,1,0:T(8,128)(2,1)S(1)}, u32[]{:S(2)}, u32[]{:S(2)}) collective-permute-start(bf16[2,1,1,2,48,768]{5,4,3,2,1,0:T(8,128)(2,1)S(1)} %dynamic-slice_convert_fusion.3), channel_id=1, source_target_pairs={{0,96},{16,112},{32,64},{48,80},{64,32},{80,48},{96,0},{112,16},{1... | collective-permute-start | bytes 884744 | tf_op jit(solution)/shard_map/ppermute | solution.py:218
  60.4 1.9 %collective-permute-done.5 = bf16[1,2,1,2,48,1536]{5,4,3,2,1,0:T(8,128)(2,1)} collective-permute-done((bf16[1,2,1,2,48,1536]{5,4,3,2,1,0:T(8,128)(2,1)}, bf16[1,2,1,2,48,1536]{5,4,3,2,1,0:T(8,128)(2,1)}, u32[]{:S(2)}, u32[]{:S(2)}) %collective-permute-start.5) | collective-permute-done | bytes 589856 | tf_op jit(solution)/shard_map/ppermute | solution.py:218
  63.7 4.9 %collective-permute-done.2 = bf16[2,1,1,2,48,768]{5,4,3,2,1,0:T(8,128)(2,1)S(1)} collective-permute-done((bf16[2,1,1,2,48,768]{5,4,3,2,1,0:T(8,128)(2,1)S(1)}, bf16[2,1,1,2,48,768]{5,4,3,2,1,0:T(8,128)(2,1)S(1)}, u32[]{:S(2)}, u32[]{:S(2)}) %collective-permute-start.2) | collective-permute-done | bytes 294944 | tf_op jit(solution)/shard_map/ppermute | solution.py:218
  68.7 2.7 %collective-permute-start.3 = (bf16[2,1,1,1,48,768]{5,4,3,2,1,0:T(8,128)(2,1)S(1)}, bf16[2,1,1,1,48,768]{5,4,3,2,1,0:T(8,128)(2,1)S(1)}, u32[]{:S(2)}, u32[]{:S(2)}) collective-permute-start(bf16[2,1,1,1,48,768]{5,4,3,2,1,0:T(8,128)(2,1)S(1)} %dynamic-slice_convert_fusion.5), channel_id=1, source_target_pairs={{0,128},{16,144},{32,160},{48,176},{64,192},{80,208},{96,224},{112... | collective-permute-start | bytes 442376 | tf_op jit(solution)/shard_map/ppermute | solution.py:218
  72.6 2.0 %collective-permute-done.3 = bf16[2,1,1,1,48,768]{5,4,3,2,1,0:T(8,128)(2,1)S(1)} collective-permute-done((bf16[2,1,1,1,48,768]{5,4,3,2,1,0:T(8,128)(2,1)S(1)}, bf16[2,1,1,1,48,768]{5,4,3,2,1,0:T(8,128)(2,1)S(1)}, u32[]{:S(2)}, u32[]{:S(2)}) %collective-permute-start.3) | collective-permute-done | bytes 147488 | tf_op jit(solution)/shard_map/ppermute | solution.py:218
  74.6 4.1 %collective-permute-done.7 = bf16[1,1,1,1,48,1536]{5,4,3,2,1,0:T(8,128)(2,1)S(1)} collective-permute-done((bf16[1,1,1,1,48,1536]{5,4,3,2,1,0:T(8,128)(2,1)S(1)}, bf16[1,1,1,1,48,1536]{5,4,3,2,1,0:T(8,128)(2,1)S(1)}, u32[]{:S(2)}, u32[]{:S(2)}) %collective-permute-start.7) | collective-permute-done | bytes 147488 | tf_op jit(solution)/shard_map/ppermute | solution.py:218
  79.4 6.1 %all-to-all-done.mix_ref.weighted_ref = bf16[16,2,2,32,768]{4,3,2,1,0:T(8,128)(2,1)S(1)} async-done(((bf16[16,2,2,32,768]{4,3,2,1,0:T(8,128)(2,1)}), bf16[16,2,2,32,768]{4,3,2,1,0:T(8,128)(2,1)S(1)}, u32[]{:S(2)}, u32[]{:S(2)}) %all-to-all-start) | async-done | bytes 3145760 | tf_op jit(solution)/shard_map/all_to_all | solution.py:250
  86.8 2.1 %half.3 = bf16[384,768]{1,0:T(8,128)(2,1)S(1)} custom-call(s32[1]{0:T(128)S(6)} %sub.23.part_ref, bf16[1024,768]{1,0:T(8,128)(2,1)S(1)} %mix.1.both_ref, bf16[16,2,2,32,768]{4,3,2,1,0:T(8,128)(2,1)S(1)} %all-to-all-done.mix_ref.weighted_ref, bf16[768,768]{1,0:T(8,128)(2,1)S(1)} %copy-done), custom_call_target="tpu_custom_call" | custom-call | tf_op jit(solution)/shard_map/half/pallas_call | solution.py:161
  90.5 2.1 %half.2 = bf16[384,768]{1,0:T(8,128)(2,1)S(1)} custom-call(s32[1]{0:T(128)} %bitcast.part_ref.core_ref, bf16[1024,768]{1,0:T(8,128)(2,1)S(1)} %mix.1.both_ref, bf16[16,2,2,32,768]{4,3,2,1,0:T(8,128)(2,1)S(1)} %all-to-all-done.mix_ref.weighted_ref, bf16[768,768]{1,0:T(8,128)(2,1)S(1)} %copy-done), custom_call_target="tpu_custom_call" | custom-call | tf_op jit(solution)/shard_map/half/pallas_call | solution.py:161
  93.6 6.5 %all-to-all-start.1 = ((bf16[8,48,768]{2,1,0:T(8,128)(2,1)}), bf16[8,48,768]{2,1,0:T(8,128)(2,1)S(1)}, u32[]{:S(2)}, u32[]{:S(2)}) async-start(bf16[8,48,768]{2,1,0:T(8,128)(2,1)} %bitcast.12), calls=%async_computation.1 | async-start | bytes 1179648 | tf_op jit(solution)/shard_map/all_to_all | solution.py:250
  100.7 11.9 %all-to-all-done.1 = bf16[8,48,768]{2,1,0:T(8,128)(2,1)S(1)} async-done(((bf16[8,48,768]{2,1,0:T(8,128)(2,1)}), bf16[8,48,768]{2,1,0:T(8,128)(2,1)S(1)}, u32[]{:S(2)}, u32[]{:S(2)}) %all-to-all-start.1) | async-done | bytes 589856 | tf_op jit(solution)/shard_map/all_to_all | solution.py:250
  113.4 18.9 %all_to_all.20 = bf16[16,48,240]{2,1,0:T(8,128)(2,1)S(1)} all-to-all(bf16[16,48,240]{2,1,0:T(8,128)(2,1)S(1)} %copy.17), channel_id=1, replica_groups=mesh['dp'=16,'seq'=16] {'seq'}, dimensions={0} | all-to-all | bytes 737280 | tf_op jit(solution)/shard_map/all_to_all | solution.py:250
  132.4 10.0 %all_to_all.21.own_ref = bf16[8,48,240]{2,1,0:T(8,128)(2,1)S(1)} all-to-all(bf16[8,48,240]{2,1,0:T(8,128)(2,1)S(1)} %broadcast_in_dim.10), channel_id=1, replica_groups={{0,32,64,96,128,160,192,224},{16,48,80,112,144,176,208,240},{1,33,65,97..., dimensions={0} | all-to-all | bytes 368640 | tf_op jit(solution)/shard_map/all_to_all | solution.py:250
  142.4 3.8 %collective-permute-start.9 = (bf16[8,48,240]{2,1,0:T(8,128)(2,1)S(1)}, bf16[8,48,240]{2,1,0:T(8,128)(2,1)S(1)}, u32[]{:S(2)}, u32[]{:S(2)}) collective-permute-start(bf16[8,48,240]{2,1,0:T(8,128)(2,1)S(1)} %all_to_all.21.own_ref), channel_id=1, source_target_pairs={{0,16},{16,0},{32,48},{48,32},{64,80},{80,64},{96,112},{112,96},{1... | collective-permute-start | bytes 552968 | tf_op jit(solution)/shard_map/ppermute | solution.py:218
  (51 shorter events, 18.4 us)
Async XLA Ops:
  4.7 80.7 %all-to-all-start = ((bf16[16,2,2,32,768]{4,3,2,1,0:T(8,128)(2,1)}), bf16[16,2,2,32,768]{4,3,2,1,0:T(8,128)(2,1)S(1)}, u32[]{:S(2)}, u32[]{:S(2)}) async-start(bf16[16,2,2,32,768]{4,3,2,1,0:T(8,128)(2,1)} %send.1), calls=%async_computation | async-start | bytes 6291456 | tf_op jit(solution)/shard_map/all_to_all | solution.py:250
  32.0 3.5 %copy-start.4 = (bf16[768,1536]{1,0:T(8,128)(2,1)S(1)}, bf16[768,1536]{1,0:T(8,128)(2,1)}, u32[]{:S(2)}) copy-start(bf16[768,1536]{1,0:T(8,128)(2,1)} %get-tuple-element.16) | copy-start | bytes 7077892
  34.6 3.8 %collective-permute-start = (bf16[2,1,384,768]{3,2,0,1:T(8,128)(2,1)}, bf16[2,1,384,768]{3,2,0,1:T(8,128)(2,1)}, u32[]{:S(2)}, u32[]{:S(2)}) collective-permute-start(bf16[2,1,384,768]{3,2,0,1:T(8,128)(2,1)} %dynamic-slice_bitcast_fusion), channel_id=1, source_target_pairs={{0,16},{16,0},{32,48},{48,32},{64,80},{80,64},{96,112},{112,96},{1... | collective-permute-start | bytes 3538952 | tf_op jit(solution)/shard_map/ppermute | solution.py:218
  36.6 6.0 %collective-permute-start.4 = (bf16[1,1,384,1536]{3,2,1,0:T(8,128)(2,1)}, bf16[1,1,384,1536]{3,2,1,0:T(8,128)(2,1)}, u32[]{:S(2)}, u32[]{:S(2)}) collective-permute-start(bf16[1,1,384,1536]{3,2,1,0:T(8,128)(2,1)} %constant_dynamic-slice_fusion), channel_id=1, source_target_pairs={{0,16},{16,0},{32,48},{48,32},{64,80},{80,64},{96,112},{112,96},{1... | collective-permute-start | bytes 3538952 | tf_op jit(solution)/shard_map/ppermute | solution.py:218
  38.4 4.2 %copy-start.5 = (bf16[768,1536]{1,0:T(8,128)(2,1)S(1)}, bf16[768,1536]{1,0:T(8,128)(2,1)}, u32[]{:S(2)}) copy-start(bf16[768,1536]{1,0:T(8,128)(2,1)} %get-tuple-element.16) | copy-start | bytes 7077892
  40.4 2.2 %copy-start.3 = (f32[2,1,384,768]{3,2,0,1:T(8,128)}, f32[2,1,384,768]{3,2,0,1:T(8,128)S(1)}, u32[]{:S(2)}) copy-start(f32[2,1,384,768]{3,2,0,1:T(8,128)S(1)} %convert_add_fusion.1) | copy-start | bytes 7077892
  41.4 14.9 %collective-permute-start.1 = (bf16[2,1,2,2,48,768]{5,4,3,2,1,0:T(8,128)(2,1)}, bf16[2,1,2,2,48,768]{5,4,3,2,1,0:T(8,128)(2,1)}, u32[]{:S(2)}, u32[]{:S(2)}) collective-permute-start(bf16[2,1,2,2,48,768]{5,4,3,2,1,0:T(8,128)(2,1)} %dynamic-slice_convert_fusion.1), channel_id=1, source_target_pairs={{0,32},{16,48},{32,0},{48,16},{64,96},{80,112},{96,64},{112,80},{1... | collective-permute-start | bytes 1769480 | tf_op jit(solution)/shard_map/ppermute | solution.py:218
  44.2 1.5 copy-start.1
  46.6 15.7 %collective-permute-start.5 = (bf16[1,2,1,2,48,1536]{5,4,3,2,1,0:T(8,128)(2,1)}, bf16[1,2,1,2,48,1536]{5,4,3,2,1,0:T(8,128)(2,1)}, u32[]{:S(2)}, u32[]{:S(2)}) collective-permute-start(bf16[1,2,1,2,48,1536]{5,4,3,2,1,0:T(8,128)(2,1)} %dynamic-slice_convert_fusion), channel_id=1, source_target_pairs={{0,96},{16,112},{32,64},{48,80},{64,32},{80,48},{96,0},{112,16},{1... | collective-permute-start | bytes 1769480 | tf_op jit(solution)/shard_map/ppermute | solution.py:218
  49.6 12.8 %copy-start.2 = (f32[1,1,384,1536]{3,2,1,0:T(8,128)S(1)}, f32[1,1,384,1536]{3,2,1,0:T(8,128)}, u32[]{:S(2)}) copy-start(f32[1,1,384,1536]{3,2,1,0:T(8,128)} %copy-done.1) | copy-start | bytes 7077892
  57.9 10.7 %collective-permute-start.2 = (bf16[2,1,1,2,48,768]{5,4,3,2,1,0:T(8,128)(2,1)S(1)}, bf16[2,1,1,2,48,768]{5,4,3,2,1,0:T(8,128)(2,1)S(1)}, u32[]{:S(2)}, u32[]{:S(2)}) collective-permute-start(bf16[2,1,1,2,48,768]{5,4,3,2,1,0:T(8,128)(2,1)S(1)} %dynamic-slice_convert_fusion.3), channel_id=1, source_target_pairs={{0,96},{16,112},{32,64},{48,80},{64,32},{80,48},{96,0},{112,16},{1... | collective-permute-start | bytes 884744 | tf_op jit(solution)/shard_map/ppermute | solution.py:218
  63.6 7.8 %collective-permute-start.6 = (bf16[1,1,1,2,48,1536]{5,4,3,2,1,0:T(8,128)(2,1)S(1)}, bf16[1,1,1,2,48,1536]{5,4,3,2,1,0:T(8,128)(2,1)S(1)}, u32[]{:S(2)}, u32[]{:S(2)}) collective-permute-start(bf16[1,1,1,2,48,1536]{5,4,3,2,1,0:T(8,128)(2,1)S(1)} %dynamic-slice_convert_fusion.2), channel_id=1, source_target_pairs={{0,32},{16,48},{32,0},{48,16},{64,96},{80,112},{96,64},{112,80},{1... | collective-permute-start | bytes 884744 | tf_op jit(solution)/shard_map/ppermute | solution.py:218
  68.7 5.9 %collective-permute-start.3 = (bf16[2,1,1,1,48,768]{5,4,3,2,1,0:T(8,128)(2,1)S(1)}, bf16[2,1,1,1,48,768]{5,4,3,2,1,0:T(8,128)(2,1)S(1)}, u32[]{:S(2)}, u32[]{:S(2)}) collective-permute-start(bf16[2,1,1,1,48,768]{5,4,3,2,1,0:T(8,128)(2,1)S(1)} %dynamic-slice_convert_fusion.5), channel_id=1, source_target_pairs={{0,128},{16,144},{32,160},{48,176},{64,192},{80,208},{96,224},{112... | collective-permute-start | bytes 442376 | tf_op jit(solution)/shard_map/ppermute | solution.py:218
  71.5 7.2 %collective-permute-start.7 = (bf16[1,1,1,1,48,1536]{5,4,3,2,1,0:T(8,128)(2,1)S(1)}, bf16[1,1,1,1,48,1536]{5,4,3,2,1,0:T(8,128)(2,1)S(1)}, u32[]{:S(2)}, u32[]{:S(2)}) collective-permute-start(bf16[1,1,1,1,48,1536]{5,4,3,2,1,0:T(8,128)(2,1)S(1)} %dynamic-slice_convert_fusion.4), channel_id=1, source_target_pairs={{0,128},{16,144},{32,160},{48,176},{64,192},{80,208},{96,224},{112... | collective-permute-start | bytes 442376 | tf_op jit(solution)/shard_map/ppermute | solution.py:218
  85.4 1.4 copy-start
  88.9 3.7 %collective-permute-start.8 = (bf16[384,768]{1,0:T(8,128)(2,1)S(1)}, bf16[384,768]{1,0:T(8,128)(2,1)S(1)}, u32[]{:S(2)}, u32[]{:S(2)}) collective-permute-start(bf16[384,768]{1,0:T(8,128)(2,1)S(1)} %half.3), channel_id=1, source_target_pairs={{0,16},{16,0},{32,48},{48,32},{64,80},{80,64},{96,112},{112,96},{1... | collective-permute-start | bytes 1769480 | tf_op jit(solution)/shard_map/ppermute | solution.py:218
  93.6 7.0 %copy-start.6 = (bf16[1,48,1536]{2,1,0:T(8,128)(2,1)S(1)}, bf16[1,48,1536]{2,1,0:T(8,128)(2,1)}, u32[]{:S(2)}) copy-start(bf16[1,48,1536]{2,1,0:T(8,128)(2,1)} %fusion.1) | copy-start | bytes 442372
  93.6 19.0 %all-to-all-start.1 = ((bf16[8,48,768]{2,1,0:T(8,128)(2,1)}), bf16[8,48,768]{2,1,0:T(8,128)(2,1)S(1)}, u32[]{:S(2)}, u32[]{:S(2)}) async-start(bf16[8,48,768]{2,1,0:T(8,128)(2,1)} %bitcast.12), calls=%async_computation.1 | async-start | bytes 1179648 | tf_op jit(solution)/shard_map/all_to_all | solution.py:250
  142.4 4.9 %collective-permute-start.9 = (bf16[8,48,240]{2,1,0:T(8,128)(2,1)S(1)}, bf16[8,48,240]{2,1,0:T(8,128)(2,1)S(1)}, u32[]{:S(2)}, u32[]{:S(2)}) collective-permute-start(bf16[8,48,240]{2,1,0:T(8,128)(2,1)S(1)} %all_to_all.21.own_ref), channel_id=1, source_target_pairs={{0,16},{16,0},{32,48},{48,32},{64,80},{80,64},{96,112},{112,96},{1... | collective-permute-start | bytes 552968 | tf_op jit(solution)/shard_map/ppermute | solution.py:218
